TPU v7x, 32 devices: a whole 2x2x4 slice. The times are simulated.
32 devices in a mesh: panel: 2 (over core), lat: 4 (over z), lon: 4 (over y, x).
Axes of the slice: x: 2, y: 2, z: 4, core: 2. Of those that a mesh axis runs over, the one named last changes fastest.
Arguments:
- tracers: float32 [2, 4, 8, 32, 512], P('panel', None, None, 'lat', 'lon'), may hold values from 0.2 to 4
- courant_lon: float32 [2, 8, 32, 512], P('panel', None, 'lat', 'lon'), may hold values from -0.45 to 0.45
- courant_lat: float32 [2, 8, 32, 512], P('panel', None, 'lat', 'lon'), may hold values from -0.45 to 0.45
- cell_mass: float32 [2, 8, 32, 512], P('panel', None, 'lat', 'lon'), as said below
- donor_cell: int32 [2, 4, 4, 4, 64], P('panel', 'lat', 'lon'), may hold values from 0 to 636, as said below
- donor_frac: float32 [2, 2, 4, 4, 4, 64], P(None, 'panel', 'lat', 'lon'), may hold values from 0 to 1
- target_cell: int32 [2, 4, 4, 4, 64], P('panel', 'lat', 'lon'), may hold values from 0 to 1023, as said below
- live_count: int32 [2, 4, 4, 4], P('panel', 'lat', 'lon'), may hold values from 0 to 64, as said below
Outputs:
- updated: float32 [2, 4, 8, 32, 512], P('panel', None, None, 'lat', 'lon')
Inputs may be any that keep to these rules, and one draw needn't show every extreme that they name: `donor_cell`: entry [p, a, b, d, k] is r * 128 + c with 0 <= r <= 4 and 0 <= c <= 124, so the whole stencil lies in the block of (p, a, b). `target_cell`: entry [p, d, b, s, k] is a flattened cell of the block of (p, d, b); the 256 entries of one device are all distinct. `live_count`: slots k >= the count carry nothing. `cell_mass`: the cell masses are positive.
All inputs are finite; a program needn't handle non-finite values.
Results may differ from a plain program's by a relative error of at most 0.0003.
Values sent between devices are 32-bit elements; how exact they have to be, the bound alone decides.
No kernel may reach another device: no remote copies, remote signals or barrier semaphores. Data moves between devices by JAX's collectives and lax.ppermute only.
A program may use at most 64 MiB of HBM per device.

v0:
```python
import jax
import jax.numpy as jnp
from jax import lax
from jax.sharding import PartitionSpec as P


def with_halo(cells, sides, width):
    for axis, dim in sides:
        count = lax.axis_size(axis)
        ends = count - 1
        head = lax.slice_in_dim(cells, 0, width, axis=dim)
        tail = lax.slice_in_dim(cells, cells.shape[dim] - width, cells.shape[dim], axis=dim)
        cells = jnp.concatenate(
            [
                lax.ppermute(tail, axis, [(i, (i + 1) % count) for i in range(ends)]),
                cells,
                lax.ppermute(head, axis, [((i + 1) % count, i) for i in range(ends)]),
            ],
            axis=dim,
        )
    return cells


def cut(source, begin_at, end_at, dim_index):
    return lax.slice_in_dim(source, begin_at, end_at, axis=dim_index)


def face_flux(padded_field, courant, length, from_end):
    dim_index = padded_field.ndim - from_end
    edge_values = 7.0 / 12.0 * (
        cut(padded_field, 1, length + 4, dim_index) + cut(padded_field, 2, length + 5, dim_index)
    ) - 1.0 / 12.0 * (
        cut(padded_field, 0, length + 3, dim_index) + cut(padded_field, 3, length + 6, dim_index)
    )
    edge_left = cut(edge_values, 0, length + 1, dim_index)
    edge_middle = cut(edge_values, 1, length + 2, dim_index)
    edge_right = cut(edge_values, 2, length + 3, dim_index)
    cell_left = cut(padded_field, 2, length + 3, dim_index)
    cell_right = cut(padded_field, 3, length + 4, dim_index)
    number = cut(courant, 3, length + 4, dim_index)
    slope_left = edge_middle - edge_left
    curve_left = 6.0 * (cell_left - 0.5 * (edge_left + edge_middle))
    flux_positive = number * (
        edge_middle - 0.5 * number * (slope_left - (1.0 - 2.0 / 3.0 * number) * curve_left)
    )
    reverse_speed = -number
    slope_right = edge_right - edge_middle
    curve_right = 6.0 * (cell_right - 0.5 * (edge_middle + edge_right))
    flux_negative = number * (
        edge_middle
        + 0.5 * reverse_speed * (slope_right + (1.0 - 2.0 / 3.0 * reverse_speed) * curve_right)
    )
    return jnp.where(number > 0.0, flux_positive, flux_negative)


def advect(padded_field, zonal_padded, meridional_padded):
    row_total = padded_field.shape[-2] - 6
    column_total = padded_field.shape[-1] - 6
    zonal_flux = face_flux(
        padded_field[..., 3 : 3 + row_total, :],
        zonal_padded[..., 3 : 3 + row_total, :],
        column_total,
        1,
    )
    meridional_flux = face_flux(
        padded_field[..., 3 : 3 + column_total],
        meridional_padded[..., 3 : 3 + column_total],
        row_total,
        2,
    )
    center = padded_field[..., 3 : 3 + row_total, 3 : 3 + column_total]
    return (
        center
        - (zonal_flux[..., 1:] - zonal_flux[..., :-1])
        - (meridional_flux[..., 1:, :] - meridional_flux[..., :-1, :])
    )


def cubic_weights(fraction):
    return jnp.stack(
        [
            -fraction * (fraction - 1.0) * (fraction - 2.0) / 6.0,
            (fraction + 1.0) * (fraction - 1.0) * (fraction - 2.0) / 2.0,
            -(fraction + 1.0) * fraction * (fraction - 2.0) / 2.0,
            (fraction + 1.0) * fraction * (fraction - 1.0) / 6.0,
        ],
        axis=-1,
    )


def interpolate(flat_field, base_cell, fraction_row, fraction_column, column_total):
    row_weights = cubic_weights(fraction_row)
    column_weights = cubic_weights(fraction_column)
    point_count = base_cell.shape[0]
    stencil_rows = jnp.arange(4, dtype=jnp.int32)[:, None] * column_total
    stencil_columns = jnp.arange(4, dtype=jnp.int32)[None, :]
    offsets = (stencil_rows + stencil_columns).reshape(16)
    spots = (offsets[:, None] + base_cell[None, :]).reshape(-1)
    factors = (row_weights[:, :, None] * column_weights[:, None, :]).reshape(point_count, 16).T
    picked = jnp.take(flat_field, spots, axis=1).reshape(flat_field.shape[0], 16, point_count)
    return jnp.sum(factors[None] * picked, axis=1)


def body(
    tracers, courant_lon, courant_lat, cell_mass, donor_cell, donor_frac, target_cell, live_count
):
    tracer_field = tracers[0]
    tracer_count, level_count, row_total, column_total = tracer_field.shape
    mass_weights = cell_mass[0]
    mass_old = lax.psum(
        jnp.sum(mass_weights[None] * tracer_field, axis=(1, 2, 3)), ("panel", "lat", "lon")
    )
    stacked = jnp.concatenate([tracer_field, courant_lon, courant_lat], axis=0)
    padded = with_halo(stacked, (("lat", 2), ("lon", 3)), 3)
    padded_field = padded[:tracer_count]
    zonal_padded = padded[tracer_count : tracer_count + 1]
    meridional_padded = padded[tracer_count + 1 :]
    advected = advect(padded_field, zonal_padded, meridional_padded)
    stack_rows = tracer_count * level_count
    cell_total = row_total * column_total
    flat_field = advected.reshape(stack_rows, cell_total)
    row_blocks = donor_cell.shape[3]
    capacity = donor_cell.shape[4]
    payload = interpolate(
        flat_field,
        donor_cell.reshape(-1),
        donor_frac[0].reshape(-1),
        donor_frac[1].reshape(-1),
        column_total,
    )
    blank_rows = jnp.zeros_like(payload)
    is_first = lax.axis_index("panel") == 0
    outgoing = jnp.where(
        is_first,
        jnp.concatenate([blank_rows, payload], axis=1),
        jnp.concatenate([payload, blank_rows], axis=1),
    )
    incoming = lax.all_to_all(outgoing, ("panel", "lat"), split_axis=1, concat_axis=1, tiled=True)
    source_start = jnp.where(is_first, row_blocks * capacity, 0).astype(jnp.int32)
    arrived = lax.dynamic_slice_in_dim(incoming, source_start, row_blocks * capacity, 1)
    live_slots = jnp.arange(capacity, dtype=jnp.int32)[None, :] < live_count.reshape(row_blocks, 1)
    target_spots = jnp.where(
        live_slots, target_cell.reshape(row_blocks, capacity), cell_total
    ).reshape(-1)
    merged = flat_field.at[:, target_spots].set(arrived, mode="drop")
    intersected = merged.reshape(tracer_count, level_count, row_total, column_total)
    local_after = jnp.sum(mass_weights[None] * intersected, axis=(1, 2, 3))
    mass_new = lax.psum(local_after, ("panel", "lat", "lon"))
    return (intersected * (mass_old / mass_new)[:, None, None, None])[None]


def solution(mesh):
    in_specs = (
        P("panel", None, None, "lat", "lon"),
        P("panel", None, "lat", "lon"),
        P("panel", None, "lat", "lon"),
        P("panel", None, "lat", "lon"),
        P("panel", "lat", "lon", None, None),
        P(None, "panel", "lat", "lon", None, None),
        P("panel", "lat", "lon", None, None),
        P("panel", "lat", "lon", None),
    )
    out_specs = P("panel", None, None, "lat", "lon")
    return jax.shard_map(body, mesh=mesh, in_specs=in_specs, out_specs=out_specs, check_vma=False)
```

profile of v0, /device:TPU:0, one launch (start us, length us, event | category | flops | bytes accessed | tf_op | source)
XLA Modules:
  0.0 101.6 jit_solution(7541795355663308758)
XLA Ops:
  0.0 0.0 copy-start
  0.0 0.0 copy-start.1
  0.0 0.0 copy-start.2
  0.0 1.0 pad_maximum_fusion.18
  1.0 1.3 %collective-permute-start.1 = (f32[6,8,3,128]{3,2,1,0:T(4,128)S(1)}, f32[6,8,3,128]{3,2,1,0:T(4,128)S(1)}, u32[]{:S(2)}, u32[]{:S(2)}) collective-permute-start(f32[6,8,3,128]{3,2,1,0:T(4,128)S(1)} %get-tuple-element.16), channel_id=1, source_target_pairs={{4,0},{8,4},{12,8},{5,1},{9,5},{13,9},{6,2},{10,6},{14,10},{7,3},{... | collective-permute-start | bytes 221192 | tf_op jit(solution)/shard_map/ppermute | solution.py:17
  2.3 5.6 %collective-permute-start = (f32[6,8,3,128]{3,2,1,0:T(4,128)S(1)}, f32[6,8,3,128]{3,2,1,0:T(4,128)S(1)}, u32[]{:S(2)}, u32[]{:S(2)}) collective-permute-start(f32[6,8,3,128]{3,2,1,0:T(4,128)S(1)} %get-tuple-element.15), channel_id=1, source_target_pairs={{0,4},{4,8},{8,12},{1,5},{5,9},{9,13},{2,6},{6,10},{10,14},{3,7},{... | collective-permute-start | bytes 221192 | tf_op jit(solution)/shard_map/ppermute | solution.py:15
  7.9 0.1 iota_add_fusion
  8.0 0.1 add.249
  8.1 0.8 add.251
  8.8 0.1 add_bitcast_fusion
  8.9 0.1 fusion.36
  9.1 0.7 fusion.39
  9.8 0.1 reshape_squeeze.6
  9.9 0.1 reshape_squeeze.7
  10.0 0.7 iota_compare_fusion
  10.7 0.1 lt.66
  10.8 0.8 reshape.365
  11.6 0.0 collective-permute-done.1
  11.6 0.0 collective-permute-done
  11.6 1.0 %pad_maximum_fusion = f32[6,8,14,128]{3,2,1,0:T(8,128)S(1)} fusion(f32[6,8,3,128]{3,2,1,0:T(4,128)S(1)} %collective-permute-done.1, f32[1,8,8,128]{3,2,1,0:T(8,128)} %param.10, f32[1,8,8,128]{3,2,1,0:T(8,128)} %param.9, f32[4,8,8,128]{3,2,1,0:T(8,128)} %bitcast.60, f32[6,8,3,128]{3,2,1,0:T(4,128)S(1)} %collective-permute-done), kind=kLoop, calls=%fused_computation.4 | loop fusion | flops 344064 | bytes 688128 | tf_op jit(solution)/shard_map/concatenate | solution.py:13
  12.6 0.2 fusion.37
  12.8 1.3 %collective-permute-start.2 = (f32[6,8,14,3]{3,2,1,0:T(8,128)S(1)}, f32[6,8,14,3]{3,2,1,0:T(8,128)S(1)}, u32[]{:S(2)}, u32[]{:S(2)}) collective-permute-start(f32[6,8,14,3]{3,2,1,0:T(8,128)S(1)} %get-tuple-element.12), channel_id=1, source_target_pairs={{1,0},{2,1},{3,2},{5,4},{6,5},{7,6},{9,8},{10,9},{11,10},{13,12},{... | collective-permute-start | bytes 24200 | tf_op jit(solution)/shard_map/ppermute | solution.py:17
  14.1 4.6 %collective-permute-start.3 = (f32[6,8,14,3]{3,2,1,0:T(8,128)S(1)}, f32[6,8,14,3]{3,2,1,0:T(8,128)S(1)}, u32[]{:S(2)}, u32[]{:S(2)}) collective-permute-start(f32[6,8,14,3]{3,2,1,0:T(8,128)S(1)} %get-tuple-element.11), channel_id=1, source_target_pairs={{0,1},{1,2},{2,3},{4,5},{5,6},{6,7},{8,9},{9,10},{10,11},{12,13},{... | collective-permute-start | bytes 24200 | tf_op jit(solution)/shard_map/ppermute | solution.py:15
  18.7 0.0 copy-done
  18.7 0.0 copy-done.1
  18.7 0.0 copy-done.2
  18.8 0.1 maximum_maximum_fusion
  18.8 0.1 fusion.12
  18.9 0.2 fusion.5
  19.2 7.6 %collective-permute-done.2 = f32[6,8,14,3]{3,2,1,0:T(8,128)S(1)} collective-permute-done((f32[6,8,14,3]{3,2,1,0:T(8,128)S(1)}, f32[6,8,14,3]{3,2,1,0:T(8,128)S(1)}, u32[]{:S(2)}, u32[]{:S(2)}) %collective-permute-start.2) | collective-permute-done | bytes 8096 | tf_op jit(solution)/shard_map/ppermute | solution.py:17
  26.7 0.0 copy-start.3
  26.8 0.0 collective-permute-done.3
  26.8 0.6 fusion.28
  27.4 0.4 fusion.20
  27.8 0.0 copy-done.3
  27.8 0.1 multiply_reduce_fusion.2
  28.0 0.1 copy_bitcast_fusion
  28.0 0.2 copy.31
  28.2 10.8 %gather_fusion = f32[4096,32]{1,0:T(8,128)S(1)} fusion(f32[32,1024]{0,1:T(8,128)S(1)} %copy.31, s32[4096]{0:T(1024)S(1)} %broadcast_clamp_fusion), kind=kCustom, calls=%fused_computation | custom fusion | bytes 1064960 | tf_op jit(solution)/shard_map/jit(_take)/gather | solution.py:100
  39.0 1.4 %multiply_reduce_fusion = f32[32,256]{0,1:T(8,128)S(1)} fusion(f32[32,16,256]{0,2,1:T(8,128)S(1)} %bitcast.66, f32[16,256]{1,0:T(8,128)S(1)} %bitcast.73, pred[16,256]{1,0:T(8,128)(4,1)S(1)} %fusion.36), kind=kLoop, calls=%fused_computation.2 | loop fusion | flops 385024 | bytes 577536 | tf_op jit(solution)/shard_map/reduce_sum | solution.py:101
  40.5 0.1 copy.29
  40.6 0.8 reshape.383
  41.4 4.7 %all-to-all-start = ((f32[8,1,2048]{2,1,0:T(1,128)}), f32[8,1,2048]{2,1,0:T(1,128)S(1)}, u32[]{:S(2)}, u32[]{:S(2)}) async-start(f32[8,1,2048]{2,1,0:T(1,128)} %reshape.383), calls=%async_computation | async-start | bytes 131072 | tf_op jit(solution)/shard_map/all_to_all | solution.py:138
  46.0 0.2 copy.34
  46.2 5.8 %all-to-all-done = f32[8,1,2048]{2,1,0:T(1,128)S(1)} async-done(((f32[8,1,2048]{2,1,0:T(1,128)}), f32[8,1,2048]{2,1,0:T(1,128)S(1)}, u32[]{:S(2)}, u32[]{:S(2)}) %all-to-all-start) | async-done | bytes 65568 | tf_op jit(solution)/shard_map/all_to_all | solution.py:138
  52.0 0.5 broadcast.373
  52.5 0.8 reduce.2
  53.3 0.1 reshape.384
  53.4 0.1 copy.30
  53.5 0.1 all_to_all.10
  53.6 0.1 copy.32
  53.7 1.4 %scatter_fusion = f32[32,1024]{0,1:T(8,128)S(1)} fusion(f32[32,1024]{0,1:T(8,128)S(1)} %copy.31, s32[256]{0:T(256)S(1)} %bitcast.77, f32[256,32]{1,0:T(8,128)S(1)} %copy.32), kind=kCustom, calls=%fused_computation.1 | custom fusion | bytes 99328 | tf_op jit(solution)/shard_map/scatter | solution.py:145
  55.1 0.2 copy.33
  55.3 0.2 multiply_reduce_fusion.1
  55.4 0.1 reduce_sum.37
  55.5 0.1 reduce_sum.38
  55.6 45.3 %all-reduce.2 = (f32[4]{0:T(128)S(1)}, f32[4]{0:T(128)S(1)}) all-reduce(f32[4]{0:T(128)S(1)} %get-tuple-element.17, f32[4]{0:T(128)S(1)} %reduce_sum.38), channel_id=1, replica_groups=mesh['panel'=2,'lat'=4,'lon'=4] {'panel','lat','lon'}, use_global_device_ids=true, to_apply=%region_3.4 | all-reduce | flops 8 | bytes 64 | tf_op jit(solution)/shard_map/psum | solution.py:110
  100.9 0.7 bitcast_multiply_fusion
  (18 shorter events, 0.3 us)
Async XLA Ops:
  0.0 18.7 %copy-start = (f32[1,4,8,8,128]{4,3,2,1,0:T(8,128)S(1)}, f32[1,4,8,8,128]{4,3,2,1,0:T(8,128)}, u32[]{:S(2)}) copy-start(f32[1,4,8,8,128]{4,3,2,1,0:T(8,128)} %param.8) | copy-start | bytes 393220
  0.0 18.7 %copy-start.1 = (f32[1,8,8,128]{3,2,1,0:T(8,128)S(1)}, f32[1,8,8,128]{3,2,1,0:T(8,128)}, u32[]{:S(2)}) copy-start(f32[1,8,8,128]{3,2,1,0:T(8,128)} %param.10) | copy-start | bytes 98308
  0.0 18.7 %copy-start.2 = (f32[1,8,8,128]{3,2,1,0:T(8,128)S(1)}, f32[1,8,8,128]{3,2,1,0:T(8,128)}, u32[]{:S(2)}) copy-start(f32[1,8,8,128]{3,2,1,0:T(8,128)} %param.9) | copy-start | bytes 98308
  1.0 10.5 %collective-permute-start.1 = (f32[6,8,3,128]{3,2,1,0:T(4,128)S(1)}, f32[6,8,3,128]{3,2,1,0:T(4,128)S(1)}, u32[]{:S(2)}, u32[]{:S(2)}) collective-permute-start(f32[6,8,3,128]{3,2,1,0:T(4,128)S(1)} %get-tuple-element.16), channel_id=1, source_target_pairs={{4,0},{8,4},{12,8},{5,1},{9,5},{13,9},{6,2},{10,6},{14,10},{7,3},{... | collective-permute-start | bytes 221192 | tf_op jit(solution)/shard_map/ppermute | solution.py:17
  2.3 9.2 %collective-permute-start = (f32[6,8,3,128]{3,2,1,0:T(4,128)S(1)}, f32[6,8,3,128]{3,2,1,0:T(4,128)S(1)}, u32[]{:S(2)}, u32[]{:S(2)}) collective-permute-start(f32[6,8,3,128]{3,2,1,0:T(4,128)S(1)} %get-tuple-element.15), channel_id=1, source_target_pairs={{0,4},{4,8},{8,12},{1,5},{5,9},{9,13},{2,6},{6,10},{10,14},{3,7},{... | collective-permute-start | bytes 221192 | tf_op jit(solution)/shard_map/ppermute | solution.py:15
  12.8 13.9 %collective-permute-start.2 = (f32[6,8,14,3]{3,2,1,0:T(8,128)S(1)}, f32[6,8,14,3]{3,2,1,0:T(8,128)S(1)}, u32[]{:S(2)}, u32[]{:S(2)}) collective-permute-start(f32[6,8,14,3]{3,2,1,0:T(8,128)S(1)} %get-tuple-element.12), channel_id=1, source_target_pairs={{1,0},{2,1},{3,2},{5,4},{6,5},{7,6},{9,8},{10,9},{11,10},{13,12},{... | collective-permute-start | bytes 24200 | tf_op jit(solution)/shard_map/ppermute | solution.py:17
  14.1 12.7 %collective-permute-start.3 = (f32[6,8,14,3]{3,2,1,0:T(8,128)S(1)}, f32[6,8,14,3]{3,2,1,0:T(8,128)S(1)}, u32[]{:S(2)}, u32[]{:S(2)}) collective-permute-start(f32[6,8,14,3]{3,2,1,0:T(8,128)S(1)} %get-tuple-element.11), channel_id=1, source_target_pairs={{0,1},{1,2},{2,3},{4,5},{5,6},{6,7},{8,9},{9,10},{10,11},{12,13},{... | collective-permute-start | bytes 24200 | tf_op jit(solution)/shard_map/ppermute | solution.py:15
  26.7 1.1 %copy-start.3 = (f32[1,8,8,128]{3,2,1,0:T(8,128)S(1)}, f32[1,8,8,128]{3,2,1,0:T(8,128)}, u32[]{:S(2)}) copy-start(f32[1,8,8,128]{3,2,1,0:T(8,128)} %param.11) | copy-start | bytes 98308
  41.4 10.7 %all-to-all-start = ((f32[8,1,2048]{2,1,0:T(1,128)}), f32[8,1,2048]{2,1,0:T(1,128)S(1)}, u32[]{:S(2)}, u32[]{:S(2)}) async-start(f32[8,1,2048]{2,1,0:T(1,128)} %reshape.383), calls=%async_computation | async-start | bytes 131072 | tf_op jit(solution)/shard_map/all_to_all | solution.py:138
where the time goes:
time: 102 us
  blocking collectives  45.3 us (44%)
  local copies, waits for them, and re-layouts  17.4 us (17%)
  starting transfers between devices  17.4 us (17%)
  waiting for transfers between devices  13.4 us (13%)
  other arithmetic  7.91 us (8%)
    psum x1, blocking collectives, body(): lax.psum(jnp.sum(mass_weights[None] * tracer_field, axis=(1, 2, 3)), ('pa...  45.3 us
    gather x1, local copies, waits for them, and re-layouts, interpolate(): jnp.take(flat_field, spots, axis=1)  10.8 us
    ppermute x2, starting transfers between devices, with_halo(): lax.ppermute(tail, axis, [(i, (i + 1) % count) for i in range(ends)])  10.1 us
    ppermute x2, waiting for transfers between devices, with_halo(): lax.ppermute(head, axis, [((i + 1) % count, i) for i in range(ends)])  7.56 us
    all_to_all x1, waiting for transfers between devices, body(): lax.all_to_all(outgoing, ('panel', 'lat'), split_axis=1, concat_axis=1, t...  5.79 us
    all_to_all x1, starting transfers between devices, body(): lax.all_to_all(outgoing, ('panel', 'lat'), split_axis=1, concat_axis=1, t...  4.67 us
    ppermute x2, starting transfers between devices, with_halo(): lax.ppermute(head, axis, [((i + 1) % count, i) for i in range(ends)])  2.58 us
  transfers between devices with their start and end apart: 5, of which 2 were waited for; matrix products, arithmetic and copies ran while one was open for 4% of the time, Pallas kernels for 0%

commit v1 on v0

v1 whole, which is shorter than its diff:
```python
import functools

import jax
import jax.numpy as jnp
from jax import lax
from jax.experimental import pallas as pl
from jax.experimental.pallas import tpu as pltpu
from jax.sharding import PartitionSpec as P

HALO = 3


def row_of(table):
    return jnp.concatenate([table[i : i + 1] for i in range(table.shape[0])], axis=1)


def live_row(live, capacity):
    slots = lax.broadcasted_iota(jnp.int32, (1, capacity), 1)
    return jnp.concatenate(
        [(slots < live[:, i : i + 1]).astype(jnp.float32) for i in range(live.shape[1])], axis=1
    )


def one_hot(spots, extent):
    places = lax.broadcasted_iota(jnp.int32, (extent, spots.shape[1]), 0)
    return (places == spots).astype(jnp.float32)


def two_parts(value):
    high = value.astype(jnp.bfloat16)
    return high, (value - high.astype(jnp.float32)).astype(jnp.bfloat16)


def three_parts(value):
    high = value.astype(jnp.bfloat16)
    rest = value - high.astype(jnp.float32)
    return (high, *two_parts(rest))


def dot(left, right, transposed=False):
    return lax.dot_general(
        left,
        right,
        (((1,), (1 if transposed else 0,)), ((), ())),
        preferred_element_type=jnp.float32,
    )


def cubic_weights(fraction):
    return (
        -fraction * (fraction - 1.0) * (fraction - 2.0) / 6.0,
        (fraction + 1.0) * (fraction - 1.0) * (fraction - 2.0) / 2.0,
        -(fraction + 1.0) * fraction * (fraction - 2.0) / 2.0,
        (fraction + 1.0) * fraction * (fraction - 1.0) / 6.0,
    )


def stencil_weights(start, fraction, extent):
    step = lax.broadcasted_iota(jnp.int32, (extent, start.shape[1]), 0) - start
    spread = jnp.zeros(step.shape, jnp.float32)
    for at, weight in enumerate(cubic_weights(fraction)):
        spread = jnp.where(step == at, weight, spread)
    return spread


def face_flux(cells, number):
    edge_left, edge, edge_right = (
        7.0 / 12.0 * (cells[i + 1] + cells[i + 2]) - 1.0 / 12.0 * (cells[i] + cells[i + 3])
        for i in range(3)
    )
    positive = number > 0.0
    speed = jnp.abs(number)
    far = jnp.where(positive, edge_left, edge_right)
    cell = jnp.where(positive, cells[2], cells[3])
    curve = 6.0 * (cell - 0.5 * (far + edge))
    return number * (edge - 0.5 * speed * ((edge - far) - (1.0 - 2.0 / 3.0 * speed) * curve))


def pack_kernel(
    field, zonal, meridional, mass, target, live, columns, northward, southward, target_mass
):
    rows, width = target_mass.shape[-2], field.shape[1]
    levels = rows
    block_rows = zonal.shape[0] // levels
    fields = field.shape[0] // block_rows
    turned = jnp.concatenate([field[...], zonal[...]], axis=0).T
    columns[0:HALO] = turned[width - HALO : width]
    columns[HALO : 2 * HALO] = turned[0:HALO]
    columns[2 * HALO :] = jnp.zeros((columns.shape[0] - 2 * HALO, columns.shape[1]), jnp.float32)
    for i in range(HALO):
        northward[pl.ds(i * fields, fields), :] = field[
            pl.ds(block_rows - HALO + i, fields, stride=block_rows), :
        ]
        southward[pl.ds(i * fields, fields), :] = field[pl.ds(i, fields, stride=block_rows), :]
    southward[pl.ds(HALO * fields, levels), :] = meridional[pl.ds(0, levels, stride=block_rows), :]
    capacity = target.shape[1]
    spots = row_of(target[...])
    row_hot = one_hot(spots // width, block_rows)
    column_hot = one_hot(lax.rem(spots, width), width).astype(jnp.bfloat16)
    picked = sum(dot(part, column_hot) for part in three_parts(mass[...]))
    picked = jnp.sum(
        picked.reshape(levels, block_rows, spots.shape[1]) * row_hot[None], axis=1
    ) * live_row(live[...], capacity)
    mine = lax.axis_index("panel")
    for block in range(target.shape[0]):
        part = picked[:, block * capacity : (block + 1) * capacity]
        part = jnp.concatenate([part, jnp.zeros((levels, width - capacity), jnp.float32)], axis=1)
        for panel in range(2):
            target_mass[panel, block] = jnp.where(mine == panel, 0.0, part)


def main_kernel(
    field, zonal, meridional, mass, columns, from_west, from_east, from_south, from_north,
    donor, fraction, target, live, target_mass, advected, outgoing, edge_rows, flux_rows,
):
    total_rows, width = field.shape
    levels = target_mass.shape[-2]
    block_rows = zonal.shape[0] // levels
    fields = total_rows // block_rows
    tracers = fields // levels
    span = levels * block_rows
    east_cells = [from_east[HALO + i : HALO + i + 1, :total_rows] for i in range(HALO)]
    own_cells = [columns[i : i + 1, :total_rows] for i in range(HALO)]
    east_number = jnp.concatenate([from_east[HALO : HALO + 1, total_rows:]] * tracers, axis=1)
    east_flux = face_flux(own_cells + east_cells, east_number)
    gap = width - 2 * HALO - 1
    lanes = jnp.concatenate(
        [
            *east_cells,
            east_flux,
            jnp.zeros((gap, total_rows), jnp.float32),
            from_west[0:HALO, :total_rows],
        ],
        axis=0,
    ).T
    for i in range(HALO):
        edge_rows[pl.ds(block_rows - HALO + i, fields, stride=block_rows), :] = from_south[
            pl.ds(i * fields, fields), :
        ]
        edge_rows[pl.ds(i, fields, stride=block_rows), :] = from_north[
            pl.ds(i * fields, fields), :
        ]
    last_rows = [
        field[pl.ds(block_rows - HALO + i, fields, stride=block_rows), :] for i in range(HALO)
    ]
    next_rows = [from_north[pl.ds(i * fields, fields), :] for i in range(HALO)]
    north_number = jnp.concatenate([from_north[pl.ds(HALO * fields, levels), :]] * tracers, axis=0)
    north_flux = face_flux(last_rows + next_rows, north_number)
    column = lax.broadcasted_iota(jnp.int32, (span, width), 1)
    row = lax.broadcasted_iota(jnp.int32, (levels, block_rows, width), 1)
    flux_rows[pl.ds(0, fields, stride=block_rows), :] = north_flux

    capacity = target.shape[1]
    spots = row_of(target[...])
    alive = live_row(live[...], capacity)
    row_hit = (one_hot(spots // width, block_rows) * alive).astype(jnp.bfloat16)
    column_hot = one_hot(lax.rem(spots, width), width).astype(jnp.bfloat16)
    kept = 1.0 - dot(row_hit, column_hot, True)
    weights = mass[...].reshape(levels, block_rows, width)

    starts = row_of(donor[...])
    row_weight = stencil_weights(starts // width, row_of(fraction[0]), block_rows)
    column_weight = stencil_weights(lax.rem(starts, width), row_of(fraction[1]), width)
    weight_high, weight_low = two_parts(column_weight)
    arriving_mass = jnp.concatenate(
        [
            target_mass[0, i, :, 0:capacity] + target_mass[1, i, :, 0:capacity]
            for i in range(target_mass.shape[1])
        ],
        axis=1,
    )

    half = fields // 2
    for tracer in range(tracers):
        part = pl.ds(tracer * span, span)
        cells = field[part, :]
        halo = lanes[tracer * span : (tracer + 1) * span]
        number = zonal[...]
        along = []
        for shift in (3, 2, 1, 0, -1, -2):
            if shift > 0:
                along.append(
                    pltpu.roll(jnp.where(column >= width - shift, halo, cells), shift, 1)
                )
            elif shift < 0:
                along.append(
                    pltpu.roll(jnp.where(column < -shift, halo, cells), width + shift, 1)
                )
            else:
                along.append(cells)
        flux = face_flux(along, number)
        next_flux = pltpu.roll(
            jnp.where(column == 0, halo[:, HALO : HALO + 1], flux), width - 1, 1
        )
        result = cells - (next_flux - flux)
        cells3 = cells.reshape(levels, block_rows, width)
        halo3 = edge_rows[part, :].reshape(levels, block_rows, width)
        along = []
        for shift in (3, 2, 1, 0, -1, -2):
            if shift > 0:
                along.append(
                    pltpu.roll(jnp.where(row >= block_rows - shift, halo3, cells3), shift, 1)
                )
            elif shift < 0:
                along.append(
                    pltpu.roll(jnp.where(row < -shift, halo3, cells3), block_rows + shift, 1)
                )
            else:
                along.append(cells3)
        flux = face_flux(along, meridional[...].reshape(levels, block_rows, width))
        edge3 = flux_rows[part, :].reshape(levels, block_rows, width)
        next_flux = pltpu.roll(jnp.where(row == 0, edge3, flux), block_rows - 1, 1)
        result = result.reshape(levels, block_rows, width) - (next_flux - flux)
        flat = result.reshape(span, width)
        advected[part, :] = flat

        high, low = two_parts(flat)
        across = dot(high, weight_high) + (dot(high, weight_low) + dot(low, weight_high))
        payload = jnp.sum(
            across.reshape(levels, block_rows, starts.shape[1]) * row_weight[None], axis=1
        )
        before = jnp.sum(weights * cells3, axis=(0, 1))[None]
        after = jnp.sum(weights * result * kept[None], axis=(0, 1))[None]
        given = jnp.sum(arriving_mass * payload, axis=0, keepdims=True)
        for block in range(target.shape[0]):
            at = block * capacity
            piece = payload[:, at : at + capacity]
            base, side = (tracer * levels) % half, (tracer * levels) // half
            for panel in range(outgoing.shape[0]):
                for place in range(outgoing.shape[2]):
                    outgoing[
                        panel, block, place, base : base + levels,
                        side * capacity : (side + 1) * capacity,
                    ] = piece
        for at in range(0, given.shape[1], width):
            after = after + given[:, at : at + width]
        sums = jnp.broadcast_to(after, outgoing.shape[:3] + (1, width))
        outgoing[:, :, :, half + tracer : half + tracer + 1, :] = sums
        sums = jnp.broadcast_to(before, outgoing.shape[:3] + (1, width))
        outgoing[:, :, :, half + tracers + tracer : half + tracers + tracer + 1, :] = sums


def fill_kernel(advected, incoming, target, live, updated):
    panels, blocks, places, payload_rows, width = incoming.shape
    _, tracers, levels, block_rows, _ = updated.shape
    fields = tracers * levels
    half = fields // 2
    capacity = target.shape[1]
    other = 1 - lax.axis_index("panel")
    place = lax.axis_index("lon")
    arrived = []
    for block in range(blocks):
        piece = incoming[other, block, place, 0:half, :]
        arrived.append(
            jnp.concatenate([piece[:, :capacity], piece[:, capacity : 2 * capacity]], axis=0)
        )
    arrived = jnp.concatenate(arrived, axis=1)
    spots = row_of(target[...])
    row_hit = one_hot(spots // width, block_rows) * live_row(live[...], capacity)
    column_hot = one_hot(lax.rem(spots, width), width).astype(jnp.bfloat16)
    hit = dot(row_hit.astype(jnp.bfloat16), column_hot, True)
    sums = jnp.sum(incoming[:, :, :, half : half + 2 * tracers, :], axis=(0, 1, 2))
    sums = jnp.sum(sums, axis=1, keepdims=True)
    scale = sums[tracers:] / sums[:tracers]
    for tracer in range(tracers):
        values = arrived[tracer * levels : (tracer + 1) * levels]
        spread = (values[:, None, :] * row_hit[None]).reshape(levels * block_rows, -1)
        placed = sum(dot(part, column_hot, True) for part in three_parts(spread))
        kept = advected[pl.ds(tracer * levels * block_rows, levels * block_rows), :]
        merged = kept.reshape(levels, block_rows, width) * (1.0 - hit)[None] + placed.reshape(
            levels, block_rows, width
        )
        updated[0, tracer] = merged * scale[tracer : tracer + 1].reshape(1, 1, 1)


def shifted(value, axis, step):
    count = lax.axis_size(axis)
    pairs = [(i, i + step) for i in range(count) if 0 <= i + step < count]
    return lax.ppermute(value, axis, pairs)


def body(
    tracers, courant_lon, courant_lat, cell_mass, donor_cell, donor_frac, target_cell, live_count
):
    _, tracer_count, levels, rows, width = tracers.shape
    blocks, capacity = donor_cell.shape[3:]
    fields = tracer_count * levels
    places = lax.axis_size("lon")
    field = tracers.reshape(fields * rows, width)
    zonal = courant_lon.reshape(levels * rows, width)
    meridional = courant_lat.reshape(levels * rows, width)
    mass = cell_mass.reshape(levels * rows, width)
    donor = donor_cell.reshape(blocks, capacity)
    fraction = donor_frac.reshape(2, blocks, capacity)
    target = target_cell.reshape(blocks, capacity)
    live = live_count.reshape(1, blocks)
    f32 = jnp.float32
    columns, northward, southward, target_mass = pl.pallas_call(
        pack_kernel,
        out_shape=(
            jax.ShapeDtypeStruct((8, (fields + levels) * rows), f32),
            jax.ShapeDtypeStruct((HALO * fields, width), f32),
            jax.ShapeDtypeStruct((HALO * fields + levels, width), f32),
            jax.ShapeDtypeStruct((2, blocks, levels, width), f32),
        ),
        name="pack_edges",
    )(field, zonal, meridional, mass, target, live)
    from_south = shifted(northward, "lat", 1)
    from_north = shifted(southward, "lat", -1)
    from_west = shifted(columns, "lon", 1)
    from_east = shifted(columns, "lon", -1)
    target_mass = lax.all_to_all(
        target_mass.reshape(2 * blocks, levels, width), ("panel", "lat"), 0, 0, tiled=True
    ).reshape(2, blocks, levels, width)
    payload_rows = fields // 2 + 2 * tracer_count
    advected, outgoing = pl.pallas_call(
        main_kernel,
        out_shape=(
            jax.ShapeDtypeStruct((fields * rows, width), f32),
            jax.ShapeDtypeStruct((2, blocks, places, payload_rows, width), f32),
        ),
        scratch_shapes=[
            pltpu.VMEM((fields * rows, width), f32),
            pltpu.VMEM((fields * rows, width), f32),
        ],
        name="advect_and_interpolate",
    )(
        field, zonal, meridional, mass, columns, from_west, from_east, from_south, from_north,
        donor, fraction, target, live, target_mass,
    )
    incoming = lax.all_to_all(
        outgoing.reshape(2 * blocks * places, payload_rows, width),
        ("panel", "lat", "lon"), 0, 0, tiled=True,
    ).reshape(2, blocks, places, payload_rows, width)
    return pl.pallas_call(
        fill_kernel,
        out_shape=jax.ShapeDtypeStruct((1, tracer_count, levels, rows, width), f32),
        name="fill_and_scale",
    )(advected, incoming, target, live)


def solution(mesh):
    in_specs = (
        P("panel", None, None, "lat", "lon"),
        P("panel", None, "lat", "lon"),
        P("panel", None, "lat", "lon"),
        P("panel", None, "lat", "lon"),
        P("panel", "lat", "lon", None, None),
        P(None, "panel", "lat", "lon", None, None),
        P("panel", "lat", "lon", None, None),
        P("panel", "lat", "lon", None),
    )
    out_specs = P("panel", None, None, "lat", "lon")
    return jax.shard_map(body, mesh=mesh, in_specs=in_specs, out_specs=out_specs, check_vma=False)
```

time: 102 us -> 48.5 us (0.48)
  blocking collectives: 45.3 us -> 21 us
  local copies, waits for them, and re-layouts: 17.4 us -> 0.61 us
  waiting for transfers between devices: 13.4 us -> 1.38 us
  other arithmetic: 7.91 us -> 0 us
  Pallas kernels: 0 us -> 6.87 us
    psum x1 -> x0, blocking collectives: 45.3 us -> none  [body(): lax.psum(jnp.sum(mass_weights[None] * tracer_field, axis=(1, 2, 3)), ('pa...]
    all_to_all x0 -> x1, blocking collectives: none -> 21 us  [body(): lax.all_to_all(outgoing.reshape(2 * blocks * places, payload_rows, width)...]
    gather x1 -> x0, local copies, waits for them, and re-layouts: 10.8 us -> none  [interpolate(): jnp.take(flat_field, spots, axis=1)]
    pallas_call x0 -> x3, Pallas kernels: none -> 6.87 us  [the longest x1 2.76 us: body(): pl.pallas_call(main_kernel, out_shape=(jax.ShapeDtypeStruct((fields * row...]
    ppermute x4, waiting for transfers between devices: 7.57 us -> 1.37 us  [shifted(): return lax.ppermute(value, axis, pairs)]
    all_to_all x1, waiting for transfers between devices: 5.79 us -> 0.01 us  [body(): lax.all_to_all(target_mass.reshape(2 * blocks, levels, width), ('panel',...]
    concatenate x3 -> x0, other arithmetic: 2.08 us -> none  [the longest x2 1.09 us: with_halo(): jnp.concatenate([lax.ppermute(tail, axis, [(i, (i + 1) % count) for i in...]
    reduce_sum x4 -> x0, other arithmetic: 1.83 us -> none  [the longest x1 1.42 us: interpolate(): return jnp.sum(factors[None] * picked, axis=1)]
  transfers between devices with their start and end apart: 5 -> 5, of which waited for: 2 -> 1; matrix products, arithmetic and copies ran while one was open for 4% -> 0% of each run, Pallas kernels for 0% -> 0%
where the time goes in v1:
time: 48.5 us; the launch traced here: 48.1 us
  blocking collectives  21 us (43%)
  starting transfers between devices  18.1 us (37%)
  Pallas kernels  6.87 us (14%)
  waiting for transfers between devices  1.38 us (3%)
  local copies, waits for them, and re-layouts  0.61 us (1%)
    all_to_all x1, blocking collectives, body(): lax.all_to_all(outgoing.reshape(2 * blocks * places, payload_rows, width)...  21 us
    ppermute x4, starting transfers between devices, shifted(): return lax.ppermute(value, axis, pairs)  11.7 us
    all_to_all x1, starting transfers between devices, body(): lax.all_to_all(target_mass.reshape(2 * blocks, levels, width), ('panel',...  6.46 us
    pallas_call x1, Pallas kernels, body(): pl.pallas_call(main_kernel, out_shape=(jax.ShapeDtypeStruct((fields * row...  2.76 us
    pallas_call x1, Pallas kernels, body(): pl.pallas_call(fill_kernel, out_shape=jax.ShapeDtypeStruct((1, tracer_cou...  2.22 us
    pallas_call x1, Pallas kernels, body(): pl.pallas_call(pack_kernel, out_shape=(jax.ShapeDtypeStruct((8, (fields +...  1.89 us
    ppermute x4, waiting for transfers between devices, shifted(): return lax.ppermute(value, axis, pairs)  1.37 us
  transfers between devices with their start and end apart: 5, of which 1 were waited for; matrix products, arithmetic and copies ran while one was open for 0% of the time, Pallas kernels for 0%

profile of v1, /device:TPU:0, one launch (start us, length us, event | category | flops | bytes accessed | tf_op | source)
XLA Modules:
  0.0 48.1 jit_solution(12852236776151644848)
XLA Ops:
  0.0 1.9 %pack_edges.1 = (f32[8,320]{1,0:T(8,128)}, f32[96,128]{1,0:T(8,128)}, f32[104,128]{1,0:T(8,128)}, f32[2,4,8,128]{3,2,1,0:T(8,128)}) custom-call(f32[256,128]{1,0:T(8,128)} %bitcast.13, f32[64,128]{1,0:T(8,128)} %bitcast.16, f32[64,128]{1,0:T(8,128)} %bitcast.18, f32[64,128]{1,0:T(8,128)} %bitcast.20, s32[4,64]{1,0:T(4,128)} %bitcast.24, s32[1,4]{1,0:T(1,128)} %bitcast.27), custom_call_target="tpu_custom_call" | custom-call | tf_op jit(solution)/shard_map/pack_edges/pallas_call | solution.py:298
  1.9 0.0 copy-start.6
  1.9 0.0 copy-start.3
  1.9 6.5 %all-to-all-start = ((f32[8,8,128]{2,1,0:T(8,128)}), f32[8,8,128]{2,1,0:T(8,128)S(1)}, u32[]{:S(2)}, u32[]{:S(2)}) async-start(f32[8,8,128]{2,1,0:T(8,128)} %bitcast.23), calls=%async_computation | async-start | bytes 65536 | tf_op jit(solution)/shard_map/all_to_all | solution.py:312
  8.4 0.0 copy-done.6
  8.4 1.3 %collective-permute-start.3 = (f32[104,128]{1,0:T(8,128)S(1)}, f32[104,128]{1,0:T(8,128)S(1)}, u32[]{:S(2)}, u32[]{:S(2)}) collective-permute-start(f32[104,128]{1,0:T(8,128)S(1)} %copy-done.6), channel_id=1, source_target_pairs={{4,0},{8,4},{12,8},{5,1},{9,5},{13,9},{6,2},{10,6},{14,10},{7,3},{... | collective-permute-start | bytes 159752 | tf_op jit(solution)/shard_map/ppermute | solution.py:279
  9.7 4.5 %collective-permute-start.2 = (f32[96,128]{1,0:T(8,128)}, f32[96,128]{1,0:T(8,128)S(1)}, u32[]{:S(2)}, u32[]{:S(2)}) collective-permute-start(f32[96,128]{1,0:T(8,128)} %get-tuple-element.12), channel_id=1, source_target_pairs={{0,4},{4,8},{8,12},{1,5},{5,9},{9,13},{2,6},{6,10},{10,14},{3,7},{... | collective-permute-start | bytes 147464 | tf_op jit(solution)/shard_map/ppermute | solution.py:279
  14.2 0.0 copy-done.3
  14.2 1.3 %collective-permute-start.1 = (f32[8,320]{1,0:T(8,128)S(1)}, f32[8,320]{1,0:T(8,128)S(1)}, u32[]{:S(2)}, u32[]{:S(2)}) collective-permute-start(f32[8,320]{1,0:T(8,128)S(1)} %copy-done.3), channel_id=1, source_target_pairs={{1,0},{2,1},{3,2},{5,4},{6,5},{7,6},{9,8},{10,9},{11,10},{13,12},{... | collective-permute-start | bytes 30728 | tf_op jit(solution)/shard_map/ppermute | solution.py:279
  15.5 4.5 %collective-permute-start = (f32[8,320]{1,0:T(8,128)S(1)}, f32[8,320]{1,0:T(8,128)S(1)}, u32[]{:S(2)}, u32[]{:S(2)}) collective-permute-start(f32[8,320]{1,0:T(8,128)S(1)} %copy-done.3), channel_id=1, source_target_pairs={{0,1},{1,2},{2,3},{4,5},{5,6},{6,7},{8,9},{9,10},{10,11},{12,13},{... | collective-permute-start | bytes 30728 | tf_op jit(solution)/shard_map/ppermute | solution.py:279
  20.1 0.0 collective-permute-done.1.from_east
  20.1 0.0 copy-start.4
  20.1 1.4 %collective-permute-done.from_west = f32[8,320]{1,0:T(8,128)S(1)} collective-permute-done((f32[8,320]{1,0:T(8,128)S(1)}, f32[8,320]{1,0:T(8,128)S(1)}, u32[]{:S(2)}, u32[]{:S(2)}) %collective-permute-start) | collective-permute-done | bytes 10272 | tf_op jit(solution)/shard_map/ppermute | solution.py:279
  21.5 0.0 copy-start.5
  21.5 0.0 collective-permute-done.2.from_south
  21.5 0.0 copy-start.2
  21.5 0.0 collective-permute-done.3.from_north
  21.5 0.0 copy-start.1
  21.5 0.0 all-to-all-done
  21.5 0.0 copy-start
  21.5 0.0 copy-done.4
  21.5 0.5 %copy-done.5 = f32[8,320]{1,0:T(8,128)} copy-done((f32[8,320]{1,0:T(8,128)}, f32[8,320]{1,0:T(8,128)S(1)}, u32[]{:S(2)}) %copy-start.5) | copy-done | bytes 10264
  22.1 0.0 copy-done.2
  22.1 0.0 copy-done.1
  22.1 0.0 copy-done
  22.1 2.8 %advect_and_interpolate.1 = (f32[256,128]{1,0:T(8,128)}, f32[2,4,4,24,128]{4,3,2,1,0:T(8,128)}) custom-call(f32[256,128]{1,0:T(8,128)} %bitcast.14, f32[64,128]{1,0:T(8,128)} %bitcast.17, f32[64,128]{1,0:T(8,128)} %bitcast.19, f32[64,128]{1,0:T(8,128)} %bitcast.21, f32[8,320]{1,0:T(8,128)} %get-tuple-element.11.columns, f32[8,320]{1,0:T(8,128)} %copy-done.5, ...), custom_call_target="tpu_custom_call" | custom-call | tf_op jit(solution)/shard_map/advect_and_interpolate/pallas_call | solution.py:316
  24.9 21.0 %all_to_all.10 = f32[32,24,128]{2,1,0:T(8,128)} all-to-all(f32[32,24,128]{2,1,0:T(8,128)} %bitcast.15), channel_id=1, replica_groups=mesh['panel'=2,'lat'=4,'lon'=4] {'panel','lat','lon'}, dimensions={0} | all-to-all | bytes 786432 | tf_op jit(solution)/shard_map/all_to_all | solution.py:331
  45.8 2.2 %fill_and_scale.1 = f32[1,4,8,8,128]{4,3,2,1,0:T(8,128)} custom-call(f32[256,128]{1,0:T(8,128)} %get-tuple-element.15.advected, f32[2,4,4,24,128]{4,3,2,1,0:T(8,128)} %bitcast.12, s32[4,64]{1,0:T(4,128)} %bitcast.26, s32[1,4]{1,0:T(1,128)} %bitcast.29), custom_call_target="tpu_custom_call" | custom-call | tf_op jit(solution)/shard_map/fill_and_scale/pallas_call | solution.py:335
Async XLA Ops:
  1.9 6.5 %copy-start.6 = (f32[104,128]{1,0:T(8,128)S(1)}, f32[104,128]{1,0:T(8,128)}, u32[]{:S(2)}) copy-start(f32[104,128]{1,0:T(8,128)} %get-tuple-element.13) | copy-start | bytes 159748
  1.9 12.3 %copy-start.3 = (f32[8,320]{1,0:T(8,128)S(1)}, f32[8,320]{1,0:T(8,128)}, u32[]{:S(2)}) copy-start(f32[8,320]{1,0:T(8,128)} %get-tuple-element.11.columns) | copy-start | bytes 30724
  1.9 19.6 %all-to-all-start = ((f32[8,8,128]{2,1,0:T(8,128)}), f32[8,8,128]{2,1,0:T(8,128)S(1)}, u32[]{:S(2)}, u32[]{:S(2)}) async-start(f32[8,8,128]{2,1,0:T(8,128)} %bitcast.23), calls=%async_computation | async-start | bytes 65536 | tf_op jit(solution)/shard_map/all_to_all | solution.py:312
  8.4 13.1 %collective-permute-start.3 = (f32[104,128]{1,0:T(8,128)S(1)}, f32[104,128]{1,0:T(8,128)S(1)}, u32[]{:S(2)}, u32[]{:S(2)}) collective-permute-start(f32[104,128]{1,0:T(8,128)S(1)} %copy-done.6), channel_id=1, source_target_pairs={{4,0},{8,4},{12,8},{5,1},{9,5},{13,9},{6,2},{10,6},{14,10},{7,3},{... | collective-permute-start | bytes 159752 | tf_op jit(solution)/shard_map/ppermute | solution.py:279
  9.7 11.8 %collective-permute-start.2 = (f32[96,128]{1,0:T(8,128)}, f32[96,128]{1,0:T(8,128)S(1)}, u32[]{:S(2)}, u32[]{:S(2)}) collective-permute-start(f32[96,128]{1,0:T(8,128)} %get-tuple-element.12), channel_id=1, source_target_pairs={{0,4},{4,8},{8,12},{1,5},{5,9},{9,13},{2,6},{6,10},{10,14},{3,7},{... | collective-permute-start | bytes 147464 | tf_op jit(solution)/shard_map/ppermute | solution.py:279
  14.2 5.9 %collective-permute-start.1 = (f32[8,320]{1,0:T(8,128)S(1)}, f32[8,320]{1,0:T(8,128)S(1)}, u32[]{:S(2)}, u32[]{:S(2)}) collective-permute-start(f32[8,320]{1,0:T(8,128)S(1)} %copy-done.3), channel_id=1, source_target_pairs={{1,0},{2,1},{3,2},{5,4},{6,5},{7,6},{9,8},{10,9},{11,10},{13,12},{... | collective-permute-start | bytes 30728 | tf_op jit(solution)/shard_map/ppermute | solution.py:279
  15.5 5.9 %collective-permute-start = (f32[8,320]{1,0:T(8,128)S(1)}, f32[8,320]{1,0:T(8,128)S(1)}, u32[]{:S(2)}, u32[]{:S(2)}) collective-permute-start(f32[8,320]{1,0:T(8,128)S(1)} %copy-done.3), channel_id=1, source_target_pairs={{0,1},{1,2},{2,3},{4,5},{5,6},{6,7},{8,9},{9,10},{10,11},{12,13},{... | collective-permute-start | bytes 30728 | tf_op jit(solution)/shard_map/ppermute | solution.py:279
  20.1 1.4 %copy-start.4 = (f32[8,320]{1,0:T(8,128)}, f32[8,320]{1,0:T(8,128)S(1)}, u32[]{:S(2)}) copy-start(f32[8,320]{1,0:T(8,128)S(1)} %collective-permute-done.1.from_east) | copy-start | bytes 30724
  21.5 0.6 %copy-start.5 = (f32[8,320]{1,0:T(8,128)}, f32[8,320]{1,0:T(8,128)S(1)}, u32[]{:S(2)}) copy-start(f32[8,320]{1,0:T(8,128)S(1)} %collective-permute-done.from_west) | copy-start | bytes 30724
  21.5 0.6 %copy-start.2 = (f32[96,128]{1,0:T(8,128)}, f32[96,128]{1,0:T(8,128)S(1)}, u32[]{:S(2)}) copy-start(f32[96,128]{1,0:T(8,128)S(1)} %collective-permute-done.2.from_south) | copy-start | bytes 147460
  21.5 0.6 %copy-start.1 = (f32[104,128]{1,0:T(8,128)}, f32[104,128]{1,0:T(8,128)S(1)}, u32[]{:S(2)}) copy-start(f32[104,128]{1,0:T(8,128)S(1)} %collective-permute-done.3.from_north) | copy-start | bytes 159748
  21.5 0.6 %copy-start = (f32[8,8,128]{2,1,0:T(8,128)}, f32[8,8,128]{2,1,0:T(8,128)S(1)}, u32[]{:S(2)}) copy-start(f32[8,8,128]{2,1,0:T(8,128)S(1)} %all-to-all-done) | copy-start | bytes 98308

commit v2 on v1

v2 whole, which is shorter than its diff:
```python
import functools
from typing import NamedTuple

import jax
import jax.numpy as jnp
from jax import lax
from jax.experimental import pallas as pl
from jax.experimental.pallas import tpu as pltpu
from jax.sharding import PartitionSpec as P

HALO = 3


class Sizes(NamedTuple):
    tracers: int
    levels: int
    rows: int
    width: int
    blocks: int
    capacity: int
    places: int

    @property
    def fields(self):
        return self.tracers * self.levels

    @property
    def sides(self):
        return self.width // self.capacity

    @property
    def margin_rows(self):
        return self.fields // self.sides

    @property
    def halo_rows(self):
        return HALO * self.fields + self.levels

    def spot(self, tracer):
        start = tracer * self.levels
        return start % self.margin_rows, start // self.margin_rows * self.capacity


def row_of(table):
    return jnp.concatenate([table[i : i + 1] for i in range(table.shape[0])], axis=1)


def live_row(live, capacity):
    slots = lax.broadcasted_iota(jnp.int32, (1, capacity), 1)
    return jnp.concatenate(
        [(slots < live[:, i : i + 1]).astype(jnp.float32) for i in range(live.shape[1])], axis=1
    )


def one_hot(spots, extent):
    places = lax.broadcasted_iota(jnp.int32, (extent, spots.shape[1]), 0)
    return (places == spots).astype(jnp.float32)


def two_parts(value):
    high = value.astype(jnp.bfloat16)
    return high, (value - high.astype(jnp.float32)).astype(jnp.bfloat16)


def three_parts(value):
    high = value.astype(jnp.bfloat16)
    rest = value - high.astype(jnp.float32)
    return (high, *two_parts(rest))


def dot(left, right, transposed=False):
    return lax.dot_general(
        left,
        right,
        (((1,), (1 if transposed else 0,)), ((), ())),
        preferred_element_type=jnp.float32,
    )


def cubic_weights(fraction):
    return (
        -fraction * (fraction - 1.0) * (fraction - 2.0) / 6.0,
        (fraction + 1.0) * (fraction - 1.0) * (fraction - 2.0) / 2.0,
        -(fraction + 1.0) * fraction * (fraction - 2.0) / 2.0,
        (fraction + 1.0) * fraction * (fraction - 1.0) / 6.0,
    )


def stencil_weights(start, fraction, extent):
    step = lax.broadcasted_iota(jnp.int32, (extent, start.shape[1]), 0) - start
    spread = jnp.zeros(step.shape, jnp.float32)
    for at, weight in enumerate(cubic_weights(fraction)):
        spread = jnp.where(step == at, weight, spread)
    return spread


def face_flux(cells, number):
    edge_left, edge, edge_right = (
        7.0 / 12.0 * (cells[i + 1] + cells[i + 2]) - 1.0 / 12.0 * (cells[i] + cells[i + 3])
        for i in range(3)
    )
    positive = number > 0.0
    speed = jnp.abs(number)
    far = jnp.where(positive, edge_left, edge_right)
    cell = jnp.where(positive, cells[2], cells[3])
    curve = 6.0 * (cell - 0.5 * (far + edge))
    return number * (edge - 0.5 * speed * ((edge - far) - (1.0 - 2.0 / 3.0 * speed) * curve))


def pack_kernel(sizes, field, zonal, meridional, mass, target, live, columns, lat_blocks):
    _, levels, rows, width, blocks, capacity, _ = sizes
    fields = sizes.fields
    turned = jnp.concatenate([field[...], zonal[...]], axis=0).T
    columns[0:HALO] = turned[width - HALO : width]
    columns[HALO : 2 * HALO] = turned[0:HALO]
    columns[2 * HALO :] = jnp.zeros((columns.shape[0] - 2 * HALO, columns.shape[1]), jnp.float32)
    spots = row_of(target[...])
    row_hot = one_hot(spots // width, rows)
    column_hot = one_hot(lax.rem(spots, width), width).astype(jnp.bfloat16)
    picked = sum(dot(part, column_hot) for part in three_parts(mass[...]))
    picked = jnp.sum(
        picked.reshape(levels, rows, spots.shape[1]) * row_hot[None], axis=1
    ) * live_row(live[...], capacity)
    here = lax.axis_index("lat")
    for block in range(blocks):
        part = picked[:, block * capacity : (block + 1) * capacity]
        lat_blocks[block, pl.ds(sizes.halo_rows, levels), :] = jnp.concatenate(
            [part] * sizes.sides, axis=1
        )

        @pl.when(block > here)
        def northward():
            for i in range(HALO):
                lat_blocks[block, pl.ds(i * fields, fields), :] = field[
                    pl.ds(rows - HALO + i, fields, stride=rows), :
                ]
            lat_blocks[block, pl.ds(HALO * fields, levels), :] = jnp.zeros(
                (levels, width), jnp.float32
            )

        @pl.when(block <= here)
        def southward():
            for i in range(HALO):
                lat_blocks[block, pl.ds(i * fields, fields), :] = field[
                    pl.ds(i, fields, stride=rows), :
                ]
            lat_blocks[block, pl.ds(HALO * fields, levels), :] = meridional[
                pl.ds(0, levels, stride=rows), :
            ]


def main_kernel(
    sizes, field, zonal, meridional, mass, columns, from_west, from_east, from_lat,
    donor, fraction, target, live, advected, outgoing, edge_rows, flux_rows,
):
    tracers, levels, rows, width, blocks, capacity, _ = sizes
    fields, span, total = sizes.fields, levels * rows, sizes.fields * rows
    east_cells = [from_east[HALO + i : HALO + i + 1, :total] for i in range(HALO)]
    own_cells = [columns[i : i + 1, :total] for i in range(HALO)]
    east_number = jnp.concatenate([from_east[HALO : HALO + 1, total:]] * tracers, axis=1)
    east_flux = face_flux(own_cells + east_cells, east_number)
    lanes = jnp.concatenate(
        [
            *east_cells,
            east_flux,
            jnp.zeros((width - 2 * HALO - 1, total), jnp.float32),
            from_west[0:HALO, :total],
        ],
        axis=0,
    ).T
    here = lax.axis_index("lat")
    south, north = jnp.maximum(here - 1, 0), jnp.minimum(here + 1, blocks - 1)
    has_south, has_north = here > 0, here < blocks - 1
    next_rows = []
    for i in range(HALO):
        part = pl.ds(i * fields, fields)
        south_row = jnp.where(has_south, from_lat[south, part, :], 0.0)
        north_row = jnp.where(has_north, from_lat[north, part, :], 0.0)
        next_rows.append(north_row)
        edge_rows[pl.ds(rows - HALO + i, fields, stride=rows), :] = south_row
        edge_rows[pl.ds(i, fields, stride=rows), :] = north_row
    last_rows = [field[pl.ds(rows - HALO + i, fields, stride=rows), :] for i in range(HALO)]
    north_number = jnp.where(has_north, from_lat[north, pl.ds(HALO * fields, levels), :], 0.0)
    flux_rows[pl.ds(0, fields, stride=rows), :] = face_flux(
        last_rows + next_rows, jnp.concatenate([north_number] * tracers, axis=0)
    )
    column = lax.broadcasted_iota(jnp.int32, (span, width), 1)
    row = lax.broadcasted_iota(jnp.int32, (levels, rows, width), 1)

    spots = row_of(target[...])
    row_hit = one_hot(spots // width, rows) * live_row(live[...], capacity)
    column_hot = one_hot(lax.rem(spots, width), width).astype(jnp.bfloat16)
    kept = 1.0 - dot(row_hit.astype(jnp.bfloat16), column_hot, True)
    weights = mass[...].reshape(levels, rows, width)

    starts = row_of(donor[...])
    row_weight = stencil_weights(starts // width, row_of(fraction[0]), rows)
    column_weight = stencil_weights(lax.rem(starts, width), row_of(fraction[1]), width)
    weight_high, weight_low = two_parts(column_weight)

    sums = blocks * sizes.margin_rows
    for tracer in range(tracers):
        part = pl.ds(tracer * span, span)
        cells = field[part, :]
        halo = lanes[tracer * span : (tracer + 1) * span]
        along = []
        for shift in (3, 2, 1, 0, -1, -2):
            if shift > 0:
                along.append(
                    pltpu.roll(jnp.where(column >= width - shift, halo, cells), shift, 1)
                )
            elif shift < 0:
                along.append(
                    pltpu.roll(jnp.where(column < -shift, halo, cells), width + shift, 1)
                )
            else:
                along.append(cells)
        flux = face_flux(along, zonal[...])
        next_flux = pltpu.roll(
            jnp.where(column == 0, halo[:, HALO : HALO + 1], flux), width - 1, 1
        )
        result = cells - (next_flux - flux)
        cells3 = cells.reshape(levels, rows, width)
        halo3 = edge_rows[part, :].reshape(levels, rows, width)
        along = []
        for shift in (3, 2, 1, 0, -1, -2):
            if shift > 0:
                along.append(pltpu.roll(jnp.where(row >= rows - shift, halo3, cells3), shift, 1))
            elif shift < 0:
                along.append(pltpu.roll(jnp.where(row < -shift, halo3, cells3), rows + shift, 1))
            else:
                along.append(cells3)
        flux = face_flux(along, meridional[...].reshape(levels, rows, width))
        edge3 = flux_rows[part, :].reshape(levels, rows, width)
        next_flux = pltpu.roll(jnp.where(row == 0, edge3, flux), rows - 1, 1)
        result = result.reshape(levels, rows, width) - (next_flux - flux)
        flat = result.reshape(span, width)
        advected[part, :] = flat

        high, low = two_parts(flat)
        across = dot(high, weight_high) + (dot(high, weight_low) + dot(low, weight_high))
        payload = jnp.sum(
            across.reshape(levels, rows, starts.shape[1]) * row_weight[None], axis=1
        )
        base, lane = sizes.spot(tracer)
        for block in range(blocks):
            at = block * capacity
            outgoing[
                pl.ds(block * sizes.margin_rows + base, levels), lane : lane + capacity
            ] = payload[:, at : at + capacity]
        outgoing[sums + tracer : sums + tracer + 1, :] = jnp.sum(
            weights * result * kept[None], axis=(0, 1)
        )[None]
        outgoing[sums + tracers + tracer : sums + tracers + tracer + 1, :] = jnp.sum(
            weights * cells3, axis=(0, 1)
        )[None]


def blocks_kernel(sizes, own, given, from_lat, other_lat, lon_blocks):
    tracers, levels, _, width, blocks, capacity, places = sizes
    size = sizes.margin_rows
    sums = pl.ds(blocks * size, 2 * tracers)
    weighed = jnp.zeros((size, width), jnp.float32)
    for block in range(blocks):
        margin = given[pl.ds(block * size, size), :]
        for sent, masses in ((margin, from_lat), (own[pl.ds(block * size, size), :], other_lat)):
            mass = masses[block, pl.ds(sizes.halo_rows, levels), :]
            weighed = weighed + sent * jnp.concatenate([mass] * (size // levels), axis=0)
        lon_blocks[block, :, 0:size, :] = jnp.broadcast_to(margin[None], (places, size, width))
    column = lax.broadcasted_iota(jnp.int32, (1, width), 1)
    partial = own[sums, :] + given[sums, :]
    added = []
    for tracer in range(tracers):
        base, lane = sizes.spot(tracer)
        row = jnp.sum(weighed[base : base + levels], axis=0, keepdims=True)
        added.append(jnp.where((column >= lane) & (column < lane + capacity), row, 0.0))
    partial = partial + jnp.concatenate(
        added + [jnp.zeros((tracers, width), jnp.float32)], axis=0
    )
    lon_blocks[:, :, size:, :] = jnp.broadcast_to(
        partial[None, None], (blocks, places, 2 * tracers, width)
    )


def fill_kernel(sizes, advected, incoming, target, live, updated):
    tracers, levels, rows, width, blocks, capacity, _ = sizes
    size = sizes.margin_rows
    place = lax.axis_index("lon")
    arrived = []
    for block in range(blocks):
        piece = incoming[block, place, 0:size, :]
        arrived.append(
            jnp.concatenate(
                [piece[:, i * capacity : (i + 1) * capacity] for i in range(sizes.sides)], axis=0
            )
        )
    arrived = jnp.concatenate(arrived, axis=1)
    spots = row_of(target[...])
    row_hit = one_hot(spots // width, rows) * live_row(live[...], capacity)
    column_hot = one_hot(lax.rem(spots, width), width).astype(jnp.bfloat16)
    kept = 1.0 - dot(row_hit.astype(jnp.bfloat16), column_hot, True)
    sums = jnp.sum(incoming[:, :, size:, :], axis=(0, 1))
    sums = jnp.sum(sums, axis=1, keepdims=True)
    scale = sums[tracers:] / sums[:tracers]
    for tracer in range(tracers):
        values = arrived[tracer * levels : (tracer + 1) * levels]
        spread = (values[:, None, :] * row_hit[None]).reshape(levels * rows, -1)
        placed = sum(dot(part, column_hot, True) for part in three_parts(spread))
        old = advected[pl.ds(tracer * levels * rows, levels * rows), :]
        merged = old.reshape(levels, rows, width) * kept[None] + placed.reshape(
            levels, rows, width
        )
        updated[0, tracer] = merged * scale[tracer : tracer + 1].reshape(1, 1, 1)


def shifted(value, axis, step):
    count = lax.axis_size(axis)
    pairs = [(i, i + step) for i in range(count) if 0 <= i + step < count]
    return lax.ppermute(value, axis, pairs)


def body(
    tracers, courant_lon, courant_lat, cell_mass, donor_cell, donor_frac, target_cell, live_count
):
    sizes = Sizes(*tracers.shape[1:], *donor_cell.shape[3:], lax.axis_size("lon"))
    _, levels, rows, width, blocks, capacity, places = sizes
    fields = sizes.fields
    field = tracers.reshape(fields * rows, width)
    zonal = courant_lon.reshape(levels * rows, width)
    meridional = courant_lat.reshape(levels * rows, width)
    mass = cell_mass.reshape(levels * rows, width)
    donor = donor_cell.reshape(blocks, capacity)
    fraction = donor_frac.reshape(2, blocks, capacity)
    target = target_cell.reshape(blocks, capacity)
    live = live_count.reshape(1, blocks)

    def shape(*dims):
        return jax.ShapeDtypeStruct(dims, jnp.float32)

    columns, lat_blocks = pl.pallas_call(
        functools.partial(pack_kernel, sizes),
        out_shape=(
            shape(8, (fields + levels) * rows),
            shape(blocks, sizes.halo_rows + levels, width),
        ),
        name="pack_edges",
    )(field, zonal, meridional, mass, target, live)
    from_lat = lax.all_to_all(lat_blocks, "lat", 0, 0, tiled=True)
    other_lat = lax.ppermute(from_lat, "panel", [(0, 1), (1, 0)])
    from_west = shifted(columns, "lon", 1)
    from_east = shifted(columns, "lon", -1)
    payload_rows = sizes.margin_rows + 2 * sizes.tracers
    advected, outgoing = pl.pallas_call(
        functools.partial(main_kernel, sizes),
        out_shape=(
            shape(fields * rows, width),
            shape(blocks * sizes.margin_rows + 2 * sizes.tracers, width),
        ),
        scratch_shapes=[
            pltpu.VMEM((fields * rows, width), jnp.float32),
            pltpu.VMEM((fields * rows, width), jnp.float32),
        ],
        name="advect_and_interpolate",
    )(
        field, zonal, meridional, mass, columns, from_west, from_east, from_lat,
        donor, fraction, target, live,
    )
    given = lax.ppermute(outgoing, "panel", [(0, 1), (1, 0)])
    lon_blocks = pl.pallas_call(
        functools.partial(blocks_kernel, sizes),
        out_shape=shape(blocks, places, payload_rows, width),
        name="margin_blocks",
    )(outgoing, given, from_lat, other_lat)
    incoming = lax.all_to_all(
        lon_blocks.reshape(blocks * places, payload_rows, width), ("lat", "lon"), 0, 0, tiled=True
    ).reshape(blocks, places, payload_rows, width)
    return pl.pallas_call(
        functools.partial(fill_kernel, sizes),
        out_shape=shape(1, sizes.tracers, levels, rows, width),
        name="fill_and_scale",
    )(advected, incoming, target, live)


def solution(mesh):
    in_specs = (
        P("panel", None, None, "lat", "lon"),
        P("panel", None, "lat", "lon"),
        P("panel", None, "lat", "lon"),
        P("panel", None, "lat", "lon"),
        P("panel", "lat", "lon", None, None),
        P(None, "panel", "lat", "lon", None, None),
        P("panel", "lat", "lon", None, None),
        P("panel", "lat", "lon", None),
    )
    out_specs = P("panel", None, None, "lat", "lon")
    return jax.shard_map(body, mesh=mesh, in_specs=in_specs, out_specs=out_specs, check_vma=False)
```

time: 48.5 us -> 49.9 us (1.029)
  starting transfers between devices: 18.1 us -> 5.84 us
  blocking collectives: 21 us -> 30.1 us
  Pallas kernels: 6.87 us -> 8.74 us
  waiting for transfers between devices: 1.38 us -> 2.79 us
  local copies, waits for them, and re-layouts: 0.61 us -> 1.9 us
    all_to_all x1 -> x2, blocking collectives: 21 us -> 30.1 us  [the longest x1 15.5 us: body(): lax.all_to_all(lon_blocks.reshape(blocks * places, payload_rows, width),...]
    all_to_all x1 -> x0, starting transfers between devices: 6.46 us -> none  [body(): lax.all_to_all(target_mass.reshape(2 * blocks, levels, width), ('panel',...]
    ppermute x4 -> x2, starting transfers between devices: 11.7 us -> 5.84 us  [shifted(): return lax.ppermute(value, axis, pairs)]
    pallas_call x3 -> x4, Pallas kernels: 6.87 us -> 8.74 us  [the longest x1 2.67 us: body(): pl.pallas_call(functools.partial(main_kernel, sizes), out_shape=(shape(fi...]
    ppermute x0 -> x2, waiting for transfers between devices: none -> 1.42 us  [the longest x1 1.42 us: body(): given = lax.ppermute(outgoing, 'panel', [(0, 1), (1, 0)])]
    unnamed x14 -> x12, local copies, waits for them, and re-layouts: 0.61 us -> 1.9 us
    ppermute x4 -> x2, waiting for transfers between devices: 1.37 us -> 1.37 us  [shifted(): return lax.ppermute(value, axis, pairs)]
  transfers between devices with their start and end apart: 5 -> 4, of which waited for: 1 -> 2; matrix products, arithmetic and copies ran while one was open for 0% -> 0% of each run, Pallas kernels for 0% -> 5%
where the time goes in v2:
time: 49.9 us; the launch traced here: 49.4 us
  blocking collectives  30.1 us (60%)
  Pallas kernels  8.74 us (18%)
  starting transfers between devices  5.84 us (12%)
  waiting for transfers between devices  2.79 us (6%)
  local copies, waits for them, and re-layouts  1.9 us (4%)
    all_to_all x1, blocking collectives, body(): lax.all_to_all(lon_blocks.reshape(blocks * places, payload_rows, width),...  15.5 us
    all_to_all x1, blocking collectives, body(): from_lat = lax.all_to_all(lat_blocks, 'lat', 0, 0, tiled=True)  14.6 us
    ppermute x2, starting transfers between devices, shifted(): return lax.ppermute(value, axis, pairs)  5.84 us
    pallas_call x1, Pallas kernels, body(): pl.pallas_call(functools.partial(main_kernel, sizes), out_shape=(shape(fi...  2.67 us
    pallas_call x1, Pallas kernels, body(): pl.pallas_call(functools.partial(fill_kernel, sizes), out_shape=shape(1,...  2.19 us
    pallas_call x1, Pallas kernels, body(): pl.pallas_call(functools.partial(pack_kernel, sizes), out_shape=(shape(8,...  2.09 us
    unnamed x12, local copies, waits for them, and re-layouts  1.9 us
    pallas_call x1, Pallas kernels, body(): pl.pallas_call(functools.partial(blocks_kernel, sizes), out_shape=shape(b...  1.79 us
  transfers between devices with their start and end apart: 4, of which 2 were waited for; matrix products, arithmetic and copies ran while one was open for 0% of the time, Pallas kernels for 5%

profile of v2, /device:TPU:0, one launch (start us, length us, event | category | flops | bytes accessed | tf_op | source)
XLA Modules:
  0.0 49.4 jit_solution(14503754447503994016)
XLA Ops:
  0.0 2.1 %pack_edges.1 = (f32[8,320]{1,0:T(8,128)}, f32[4,112,128]{2,1,0:T(8,128)}) custom-call(f32[256,128]{1,0:T(8,128)} %bitcast.12, f32[64,128]{1,0:T(8,128)} %bitcast.14, f32[64,128]{1,0:T(8,128)} %bitcast.16, f32[64,128]{1,0:T(8,128)} %bitcast.18, s32[4,64]{1,0:T(4,128)} %bitcast.20, s32[1,4]{1,0:T(1,128)} %bitcast.23), custom_call_target="tpu_custom_call" | custom-call | tf_op jit(solution)/shard_map/pack_edges/pallas_call | solution.py:340
  2.1 0.0 copy-start.3
  2.1 14.6 %all_to_all.10.from_lat = f32[4,112,128]{2,1,0:T(8,128)S(1)} all-to-all(f32[4,112,128]{2,1,0:T(8,128)} %get-tuple-element.10), channel_id=1, replica_groups=mesh['panel'=2,'lat'=4,'lon'=4] {'lat'}, dimensions={0} | all-to-all | bytes 458752 | tf_op jit(solution)/shard_map/all_to_all | solution.py:348
  16.7 0.0 copy-start
  16.7 0.0 collective-permute-start.3
  16.7 0.0 copy-done.3
  16.7 1.3 %collective-permute-start.1 = (f32[8,320]{1,0:T(8,128)S(1)}, f32[8,320]{1,0:T(8,128)S(1)}, u32[]{:S(2)}, u32[]{:S(2)}) collective-permute-start(f32[8,320]{1,0:T(8,128)S(1)} %copy-done.3), channel_id=1, source_target_pairs={{1,0},{2,1},{3,2},{5,4},{6,5},{7,6},{9,8},{10,9},{11,10},{13,12},{... | collective-permute-start | bytes 30728 | tf_op jit(solution)/shard_map/ppermute | solution.py:319
  18.0 4.5 %collective-permute-start = (f32[8,320]{1,0:T(8,128)S(1)}, f32[8,320]{1,0:T(8,128)S(1)}, u32[]{:S(2)}, u32[]{:S(2)}) collective-permute-start(f32[8,320]{1,0:T(8,128)S(1)} %copy-done.3), channel_id=1, source_target_pairs={{0,1},{1,2},{2,3},{4,5},{5,6},{6,7},{8,9},{9,10},{10,11},{12,13},{... | collective-permute-start | bytes 30728 | tf_op jit(solution)/shard_map/ppermute | solution.py:319
  22.6 0.0 collective-permute-done.1.from_east
  22.6 0.0 copy-start.4
  22.6 1.4 %collective-permute-done.from_west = f32[8,320]{1,0:T(8,128)S(1)} collective-permute-done((f32[8,320]{1,0:T(8,128)S(1)}, f32[8,320]{1,0:T(8,128)S(1)}, u32[]{:S(2)}, u32[]{:S(2)}) %collective-permute-start) | collective-permute-done | bytes 10272 | tf_op jit(solution)/shard_map/ppermute | solution.py:319
  24.0 0.0 copy-start.5
  24.0 0.0 copy-done
  24.0 0.0 copy-done.4
  24.0 0.6 %copy-done.5 = f32[8,320]{1,0:T(8,128)} copy-done((f32[8,320]{1,0:T(8,128)}, f32[8,320]{1,0:T(8,128)S(1)}, u32[]{:S(2)}) %copy-start.5) | copy-done | bytes 10264
  24.6 2.7 %advect_and_interpolate.1 = (f32[256,128]{1,0:T(8,128)}, f32[72,128]{1,0:T(8,128)}) custom-call(f32[256,128]{1,0:T(8,128)} %bitcast.13, f32[64,128]{1,0:T(8,128)} %bitcast.15, f32[64,128]{1,0:T(8,128)} %bitcast.17, f32[64,128]{1,0:T(8,128)} %bitcast.19, f32[8,320]{1,0:T(8,128)} %get-tuple-element.9.columns, f32[8,320]{1,0:T(8,128)} %copy-done.5, ...), custom_call_target="tpu_custom_call" | custom-call | tf_op jit(solution)/shard_map/advect_and_interpolate/pallas_call | solution.py:353
  27.2 0.0 collective-permute-start.2
  27.3 1.4 %collective-permute-done.2.given = f32[72,128]{1,0:T(8,128)S(1)} collective-permute-done((f32[72,128]{1,0:T(8,128)}, f32[72,128]{1,0:T(8,128)S(1)}, u32[]{:S(2)}, u32[]{:S(2)}) %collective-permute-start.2) | collective-permute-done | bytes 36896 | tf_op jit(solution)/shard_map/ppermute | solution.py:368
  28.7 0.0 copy-start.2
  28.7 0.0 collective-permute-done.3.other_lat
  28.7 0.6 %copy-done.2 = f32[72,128]{1,0:T(8,128)} copy-done((f32[72,128]{1,0:T(8,128)}, f32[72,128]{1,0:T(8,128)S(1)}, u32[]{:S(2)}) %copy-start.2) | copy-done | bytes 36888
  29.3 0.0 copy-start.1
  29.3 0.7 %copy-done.1 = f32[4,112,128]{2,1,0:T(8,128)} copy-done((f32[4,112,128]{2,1,0:T(8,128)}, f32[4,112,128]{2,1,0:T(8,128)S(1)}, u32[]{:S(2)}) %copy-start.1) | copy-done | bytes 229400
  30.0 1.8 %margin_blocks.1 = f32[4,4,24,128]{3,2,1,0:T(8,128)} custom-call(f32[72,128]{1,0:T(8,128)} %get-tuple-element.12.own, f32[72,128]{1,0:T(8,128)} %copy-done.2, f32[4,112,128]{2,1,0:T(8,128)} %copy-done, f32[4,112,128]{2,1,0:T(8,128)} %copy-done.1), custom_call_target="tpu_custom_call" | custom-call | tf_op jit(solution)/shard_map/margin_blocks/pallas_call | solution.py:369
  31.8 15.5 %all_to_all.11 = f32[16,24,128]{2,1,0:T(8,128)} all-to-all(f32[16,24,128]{2,1,0:T(8,128)} %bitcast.11), channel_id=1, replica_groups=mesh['panel'=2,'lat'=4,'lon'=4] {'lat','lon'}, dimensions={0} | all-to-all | bytes 393216 | tf_op jit(solution)/shard_map/all_to_all | solution.py:374
  47.2 2.2 %fill_and_scale.1 = f32[1,4,8,8,128]{4,3,2,1,0:T(8,128)} custom-call(f32[256,128]{1,0:T(8,128)} %get-tuple-element.11.advected, f32[4,4,24,128]{3,2,1,0:T(8,128)} %bitcast.10, s32[4,64]{1,0:T(4,128)} %bitcast.22, s32[1,4]{1,0:T(1,128)} %bitcast.25), custom_call_target="tpu_custom_call" | custom-call | tf_op jit(solution)/shard_map/fill_and_scale/pallas_call | solution.py:377
Async XLA Ops:
  2.1 14.6 %copy-start.3 = (f32[8,320]{1,0:T(8,128)S(1)}, f32[8,320]{1,0:T(8,128)}, u32[]{:S(2)}) copy-start(f32[8,320]{1,0:T(8,128)} %get-tuple-element.9.columns) | copy-start | bytes 30724
  16.7 7.3 %copy-start = (f32[4,112,128]{2,1,0:T(8,128)}, f32[4,112,128]{2,1,0:T(8,128)S(1)}, u32[]{:S(2)}) copy-start(f32[4,112,128]{2,1,0:T(8,128)S(1)} %all_to_all.10.from_lat) | copy-start | bytes 688132
  16.7 12.0 %collective-permute-start.3 = (f32[4,112,128]{2,1,0:T(8,128)S(1)}, f32[4,112,128]{2,1,0:T(8,128)S(1)}, u32[]{:S(2)}, u32[]{:S(2)}) collective-permute-start(f32[4,112,128]{2,1,0:T(8,128)S(1)} %all_to_all.10.from_lat), channel_id=1, source_target_pairs={{0,16},{16,0},{1,17},{17,1},{2,18},{18,2},{3,19},{19,3},{4,20},{20... | collective-permute-start | bytes 688136 | tf_op jit(solution)/shard_map/ppermute | solution.py:349
  16.7 5.9 %collective-permute-start.1 = (f32[8,320]{1,0:T(8,128)S(1)}, f32[8,320]{1,0:T(8,128)S(1)}, u32[]{:S(2)}, u32[]{:S(2)}) collective-permute-start(f32[8,320]{1,0:T(8,128)S(1)} %copy-done.3), channel_id=1, source_target_pairs={{1,0},{2,1},{3,2},{5,4},{6,5},{7,6},{9,8},{10,9},{11,10},{13,12},{... | collective-permute-start | bytes 30728 | tf_op jit(solution)/shard_map/ppermute | solution.py:319
  18.0 5.9 %collective-permute-start = (f32[8,320]{1,0:T(8,128)S(1)}, f32[8,320]{1,0:T(8,128)S(1)}, u32[]{:S(2)}, u32[]{:S(2)}) collective-permute-start(f32[8,320]{1,0:T(8,128)S(1)} %copy-done.3), channel_id=1, source_target_pairs={{0,1},{1,2},{2,3},{4,5},{5,6},{6,7},{8,9},{9,10},{10,11},{12,13},{... | collective-permute-start | bytes 30728 | tf_op jit(solution)/shard_map/ppermute | solution.py:319
  22.6 1.4 %copy-start.4 = (f32[8,320]{1,0:T(8,128)}, f32[8,320]{1,0:T(8,128)S(1)}, u32[]{:S(2)}) copy-start(f32[8,320]{1,0:T(8,128)S(1)} %collective-permute-done.1.from_east) | copy-start | bytes 30724
  24.0 0.6 %copy-start.5 = (f32[8,320]{1,0:T(8,128)}, f32[8,320]{1,0:T(8,128)S(1)}, u32[]{:S(2)}) copy-start(f32[8,320]{1,0:T(8,128)S(1)} %collective-permute-done.from_west) | copy-start | bytes 30724
  27.2 1.4 %collective-permute-start.2 = (f32[72,128]{1,0:T(8,128)}, f32[72,128]{1,0:T(8,128)S(1)}, u32[]{:S(2)}, u32[]{:S(2)}) collective-permute-start(f32[72,128]{1,0:T(8,128)} %get-tuple-element.12.own), channel_id=1, source_target_pairs={{0,16},{16,0},{1,17},{17,1},{2,18},{18,2},{3,19},{19,3},{4,20},{20... | collective-permute-start | bytes 110600 | tf_op jit(solution)/shard_map/ppermute | solution.py:368
  28.7 0.6 %copy-start.2 = (f32[72,128]{1,0:T(8,128)}, f32[72,128]{1,0:T(8,128)S(1)}, u32[]{:S(2)}) copy-start(f32[72,128]{1,0:T(8,128)S(1)} %collective-permute-done.2.given) | copy-start | bytes 110596
  29.3 0.7 %copy-start.1 = (f32[4,112,128]{2,1,0:T(8,128)}, f32[4,112,128]{2,1,0:T(8,128)S(1)}, u32[]{:S(2)}) copy-start(f32[4,112,128]{2,1,0:T(8,128)S(1)} %collective-permute-done.3.other_lat) | copy-start | bytes 688132

commit v3 on v2

--- a/solution.py
+++ b/solution.py
@@ -335,7 +335,10 @@
     live = live_count.reshape(1, blocks)
 
     def shape(*dims):
-        return jax.ShapeDtypeStruct(dims, jnp.float32)
+        return pltpu.VMEM(dims, jnp.float32)
+
+    def near(*values):
+        return (pltpu.with_memory_space_constraint(value, pltpu.VMEM) for value in values)
 
     columns, lat_blocks = pl.pallas_call(
         functools.partial(pack_kernel, sizes),
@@ -346,9 +349,10 @@
         name="pack_edges",
     )(field, zonal, meridional, mass, target, live)
     from_lat = lax.all_to_all(lat_blocks, "lat", 0, 0, tiled=True)
-    other_lat = lax.ppermute(from_lat, "panel", [(0, 1), (1, 0)])
     from_west = shifted(columns, "lon", 1)
     from_east = shifted(columns, "lon", -1)
+    from_lat, from_west, from_east = lax.optimization_barrier((from_lat, from_west, from_east))
+    other_lat = lax.ppermute(from_lat, "panel", [(0, 1), (1, 0)])
     payload_rows = sizes.margin_rows + 2 * sizes.tracers
     advected, outgoing = pl.pallas_call(
         functools.partial(main_kernel, sizes),
@@ -362,7 +366,7 @@
         ],
         name="advect_and_interpolate",
     )(
-        field, zonal, meridional, mass, columns, from_west, from_east, from_lat,
+        field, zonal, meridional, mass, *near(columns, from_west, from_east, from_lat),
         donor, fraction, target, live,
     )
     given = lax.ppermute(outgoing, "panel", [(0, 1), (1, 0)])
@@ -370,15 +374,15 @@
         functools.partial(blocks_kernel, sizes),
         out_shape=shape(blocks, places, payload_rows, width),
         name="margin_blocks",
-    )(outgoing, given, from_lat, other_lat)
+    )(*near(outgoing, given, from_lat, other_lat))
     incoming = lax.all_to_all(
         lon_blocks.reshape(blocks * places, payload_rows, width), ("lat", "lon"), 0, 0, tiled=True
     ).reshape(blocks, places, payload_rows, width)
     return pl.pallas_call(
         functools.partial(fill_kernel, sizes),
-        out_shape=shape(1, sizes.tracers, levels, rows, width),
+        out_shape=jax.ShapeDtypeStruct((1, sizes.tracers, levels, rows, width), jnp.float32),
         name="fill_and_scale",
-    )(advected, incoming, target, live)
+    )(*near(advected, incoming), target, live)
 
 
 def solution(mesh):

time: 49.9 us -> 38.9 us (0.78)
  blocking collectives: 30.1 us -> 16.7 us
  starting transfers between devices: 5.84 us -> 12.7 us
  Pallas kernels: 8.74 us -> 5.88 us
  local copies, waits for them, and re-layouts: 1.9 us -> 0 us
    all_to_all x1 -> x0, blocking collectives: 14.6 us -> none  [body(): from_lat = lax.all_to_all(lat_blocks, 'lat', 0, 0, tiled=True)]
    all_to_all x0 -> x1, starting transfers between devices: none -> 6.33 us  [body(): from_lat = lax.all_to_all(lat_blocks, 'lat', 0, 0, tiled=True)]
    unnamed x12 -> x0, local copies, waits for them, and re-layouts: 1.9 us -> none
    pallas_call x1, Pallas kernels: 1.79 us -> 0.03 us  [body(): pl.pallas_call(functools.partial(blocks_kernel, sizes), out_shape=shape(b...]
    all_to_all x1, blocking collectives: 15.5 us -> 16.7 us  [body(): lax.all_to_all(lon_blocks.reshape(blocks * places, payload_rows, width),...]
    all_to_all x0 -> x1, waiting for transfers between devices: none -> 0.98 us  [body(): from_lat = lax.all_to_all(lat_blocks, 'lat', 0, 0, tiled=True)]
    pallas_call x1, Pallas kernels: 2.67 us -> 1.92 us  [body(): pl.pallas_call(functools.partial(main_kernel, sizes), out_shape=(shape(fi...]
    ppermute x1, waiting for transfers between devices: 1.42 us -> 0.87 us  [body(): given = lax.ppermute(outgoing, 'panel', [(0, 1), (1, 0)])]
  transfers between devices with their start and end apart: 4 -> 5, of which waited for: 2 -> 3; matrix products, arithmetic and copies ran while one was open for 0% -> 0% of each run, Pallas kernels for 5% -> 5%
where the time goes in v3:
time: 38.9 us; the launch traced here: 38.5 us
  blocking collectives  16.7 us (43%)
  starting transfers between devices  12.7 us (33%)
  Pallas kernels  5.88 us (15%)
  waiting for transfers between devices  3.23 us (8%)
    all_to_all x1, blocking collectives, body(): lax.all_to_all(lon_blocks.reshape(blocks * places, payload_rows, width),...  16.7 us
    all_to_all x1, starting transfers between devices, body(): from_lat = lax.all_to_all(lat_blocks, 'lat', 0, 0, tiled=True)  6.33 us
    ppermute x2, starting transfers between devices, shifted(): return lax.ppermute(value, axis, pairs)  5.83 us
    pallas_call x1, Pallas kernels, body(): pl.pallas_call(functools.partial(pack_kernel, sizes), out_shape=(shape(8,...  2.07 us
    pallas_call x1, Pallas kernels, body(): pl.pallas_call(functools.partial(main_kernel, sizes), out_shape=(shape(fi...  1.92 us
    pallas_call x1, Pallas kernels, body(): pl.pallas_call(functools.partial(fill_kernel, sizes), out_shape=jax.Shape...  1.87 us
    ppermute x2, waiting for transfers between devices, shifted(): return lax.ppermute(value, axis, pairs)  1.38 us
    all_to_all x1, waiting for transfers between devices, body(): from_lat = lax.all_to_all(lat_blocks, 'lat', 0, 0, tiled=True)  0.98 us
  transfers between devices with their start and end apart: 5, of which 3 were waited for; matrix products, arithmetic and copies ran while one was open for 0% of the time, Pallas kernels for 5%

profile of v3, /device:TPU:0, one launch (start us, length us, event | category | flops | bytes accessed | tf_op | source)
XLA Modules:
  0.0 38.5 jit_solution(13920620773683309257)
XLA Ops:
  0.0 2.1 %pack_edges.1 = (f32[8,320]{1,0:T(8,128)S(1)}, f32[4,112,128]{2,1,0:T(8,128)}) custom-call(f32[256,128]{1,0:T(8,128)} %bitcast.12, f32[64,128]{1,0:T(8,128)} %bitcast.14, f32[64,128]{1,0:T(8,128)} %bitcast.16, f32[64,128]{1,0:T(8,128)} %bitcast.18, s32[4,64]{1,0:T(4,128)} %bitcast.20, s32[1,4]{1,0:T(1,128)} %bitcast.23), custom_call_target="tpu_custom_call" | custom-call | tf_op jit(solution)/shard_map/pack_edges/pallas_call | solution.py:343
  2.1 6.3 %all-to-all-start = ((f32[4,112,128]{2,1,0:T(8,128)}), f32[4,112,128]{2,1,0:T(8,128)S(1)}, u32[]{:S(2)}, u32[]{:S(2)}) async-start(f32[4,112,128]{2,1,0:T(8,128)} %get-tuple-element.13), calls=%async_computation | async-start | bytes 458752 | tf_op jit(solution)/shard_map/all_to_all | solution.py:351
  8.4 1.3 %collective-permute-start.1 = (f32[8,320]{1,0:T(8,128)S(1)}, f32[8,320]{1,0:T(8,128)S(1)}, u32[]{:S(2)}, u32[]{:S(2)}) collective-permute-start(f32[8,320]{1,0:T(8,128)S(1)} %get-tuple-element.12.columns), channel_id=1, source_target_pairs={{1,0},{2,1},{3,2},{5,4},{6,5},{7,6},{9,8},{10,9},{11,10},{13,12},{... | collective-permute-start | bytes 30728 | tf_op jit(solution)/shard_map/ppermute | solution.py:319
  9.7 4.5 %collective-permute-start = (f32[8,320]{1,0:T(8,128)S(1)}, f32[8,320]{1,0:T(8,128)S(1)}, u32[]{:S(2)}, u32[]{:S(2)}) collective-permute-start(f32[8,320]{1,0:T(8,128)S(1)} %get-tuple-element.12.columns), channel_id=1, source_target_pairs={{0,1},{1,2},{2,3},{4,5},{5,6},{6,7},{8,9},{9,10},{10,11},{12,13},{... | collective-permute-start | bytes 30728 | tf_op jit(solution)/shard_map/ppermute | solution.py:319
  14.2 0.0 collective-permute-done.1.from_east
  14.3 1.4 %collective-permute-done.from_west = f32[8,320]{1,0:T(8,128)S(1)} collective-permute-done((f32[8,320]{1,0:T(8,128)S(1)}, f32[8,320]{1,0:T(8,128)S(1)}, u32[]{:S(2)}, u32[]{:S(2)}) %collective-permute-start) | collective-permute-done | bytes 10272 | tf_op jit(solution)/shard_map/ppermute | solution.py:319
  15.6 1.0 %all-to-all-done.from_lat = f32[4,112,128]{2,1,0:T(8,128)S(1)} async-done(((f32[4,112,128]{2,1,0:T(8,128)}), f32[4,112,128]{2,1,0:T(8,128)S(1)}, u32[]{:S(2)}, u32[]{:S(2)}) %all-to-all-start) | async-done | bytes 229408 | tf_op jit(solution)/shard_map/all_to_all | solution.py:351
  16.6 0.0 collective-permute-start.3
  16.6 1.9 %advect_and_interpolate.1 = (f32[256,128]{1,0:T(8,128)S(1)}, f32[72,128]{1,0:T(8,128)S(1)}) custom-call(f32[256,128]{1,0:T(8,128)} %bitcast.13, f32[64,128]{1,0:T(8,128)} %bitcast.15, f32[64,128]{1,0:T(8,128)} %bitcast.17, f32[64,128]{1,0:T(8,128)} %bitcast.19, f32[8,320]{1,0:T(8,128)S(1)} %get-tuple-element.12.columns, ...), custom_call_target="tpu_custom_call" | custom-call | tf_op jit(solution)/shard_map/advect_and_interpolate/pallas_call | solution.py:357
  18.5 0.5 %collective-permute-start.2 = (f32[72,128]{1,0:T(8,128)S(1)}, f32[72,128]{1,0:T(8,128)S(1)}, u32[]{:S(2)}, u32[]{:S(2)}) collective-permute-start(f32[72,128]{1,0:T(8,128)S(1)} %get-tuple-element.18.own), channel_id=1, source_target_pairs={{0,16},{16,0},{1,17},{17,1},{2,18},{18,2},{3,19},{19,3},{4,20},{20... | collective-permute-start | bytes 110600 | tf_op jit(solution)/shard_map/ppermute | solution.py:372
  19.1 0.9 %collective-permute-done.2.given = f32[72,128]{1,0:T(8,128)S(1)} collective-permute-done((f32[72,128]{1,0:T(8,128)S(1)}, f32[72,128]{1,0:T(8,128)S(1)}, u32[]{:S(2)}, u32[]{:S(2)}) %collective-permute-start.2) | collective-permute-done | bytes 36896 | tf_op jit(solution)/shard_map/ppermute | solution.py:372
  19.9 0.0 collective-permute-done.3.other_lat
  19.9 16.7 %all_to_all.10 = f32[16,24,128]{2,1,0:T(8,128)S(1)} all-to-all(f32[16,24,128]{2,1,0:T(8,128)S(1)} %bitcast.11), channel_id=1, replica_groups=mesh['panel'=2,'lat'=4,'lon'=4] {'lat','lon'}, dimensions={0} | all-to-all | bytes 393216 | tf_op jit(solution)/shard_map/all_to_all | solution.py:378
  36.7 1.9 %fill_and_scale.1 = f32[1,4,8,8,128]{4,3,2,1,0:T(8,128)} custom-call(f32[256,128]{1,0:T(8,128)S(1)} %get-tuple-element.17.advected, f32[4,4,24,128]{3,2,1,0:T(8,128)S(1)} %bitcast.10, s32[4,64]{1,0:T(4,128)} %bitcast.22, s32[1,4]{1,0:T(1,128)} %bitcast.25), custom_call_target="tpu_custom_call" | custom-call | tf_op jit(solution)/shard_map/fill_and_scale/pallas_call | solution.py:381
  (1 shorter events, 0.0 us)
Async XLA Ops:
  2.1 14.5 %all-to-all-start = ((f32[4,112,128]{2,1,0:T(8,128)}), f32[4,112,128]{2,1,0:T(8,128)S(1)}, u32[]{:S(2)}, u32[]{:S(2)}) async-start(f32[4,112,128]{2,1,0:T(8,128)} %get-tuple-element.13), calls=%async_computation | async-start | bytes 458752 | tf_op jit(solution)/shard_map/all_to_all | solution.py:351
  8.4 5.8 %collective-permute-start.1 = (f32[8,320]{1,0:T(8,128)S(1)}, f32[8,320]{1,0:T(8,128)S(1)}, u32[]{:S(2)}, u32[]{:S(2)}) collective-permute-start(f32[8,320]{1,0:T(8,128)S(1)} %get-tuple-element.12.columns), channel_id=1, source_target_pairs={{1,0},{2,1},{3,2},{5,4},{6,5},{7,6},{9,8},{10,9},{11,10},{13,12},{... | collective-permute-start | bytes 30728 | tf_op jit(solution)/shard_map/ppermute | solution.py:319
  9.7 5.9 %collective-permute-start = (f32[8,320]{1,0:T(8,128)S(1)}, f32[8,320]{1,0:T(8,128)S(1)}, u32[]{:S(2)}, u32[]{:S(2)}) collective-permute-start(f32[8,320]{1,0:T(8,128)S(1)} %get-tuple-element.12.columns), channel_id=1, source_target_pairs={{0,1},{1,2},{2,3},{4,5},{5,6},{6,7},{8,9},{9,10},{10,11},{12,13},{... | collective-permute-start | bytes 30728 | tf_op jit(solution)/shard_map/ppermute | solution.py:319
  16.6 3.3 %collective-permute-start.3 = (f32[4,112,128]{2,1,0:T(8,128)S(1)}, f32[4,112,128]{2,1,0:T(8,128)S(1)}, u32[]{:S(2)}, u32[]{:S(2)}) collective-permute-start(f32[4,112,128]{2,1,0:T(8,128)S(1)} %all-to-all-done.from_lat), channel_id=1, source_target_pairs={{0,16},{16,0},{1,17},{17,1},{2,18},{18,2},{3,19},{19,3},{4,20},{20... | collective-permute-start | bytes 688136 | tf_op jit(solution)/shard_map/ppermute | solution.py:355
  18.5 1.4 %collective-permute-start.2 = (f32[72,128]{1,0:T(8,128)S(1)}, f32[72,128]{1,0:T(8,128)S(1)}, u32[]{:S(2)}, u32[]{:S(2)}) collective-permute-start(f32[72,128]{1,0:T(8,128)S(1)} %get-tuple-element.18.own), channel_id=1, source_target_pairs={{0,16},{16,0},{1,17},{17,1},{2,18},{18,2},{3,19},{19,3},{4,20},{20... | collective-permute-start | bytes 110600 | tf_op jit(solution)/shard_map/ppermute | solution.py:372

commit v4 on v3

--- a/solution.py
+++ b/solution.py
@@ -107,13 +107,15 @@
     return number * (edge - 0.5 * speed * ((edge - far) - (1.0 - 2.0 / 3.0 * speed) * curve))
 
 
-def pack_kernel(sizes, field, zonal, meridional, mass, target, live, columns, lat_blocks):
+def pack_kernel(sizes, field, zonal, meridional, mass, target, live, columns, columns_odd, lat_blocks):
     _, levels, rows, width, blocks, capacity, _ = sizes
     fields = sizes.fields
     turned = jnp.concatenate([field[...], zonal[...]], axis=0).T
     columns[0:HALO] = turned[width - HALO : width]
     columns[HALO : 2 * HALO] = turned[0:HALO]
     columns[2 * HALO :] = jnp.zeros((columns.shape[0] - 2 * HALO, columns.shape[1]), jnp.float32)
+    columns_odd[0:8] = columns[...]
+    columns_odd[8:] = jnp.zeros((columns_odd.shape[0] - 8, columns.shape[1]), jnp.float32)
     spots = row_of(target[...])
     row_hot = one_hot(spots // width, rows)
     column_hot = one_hot(lax.rem(spots, width), width).astype(jnp.bfloat16)
@@ -150,14 +152,17 @@
 
 
 def main_kernel(
-    sizes, field, zonal, meridional, mass, columns, from_west, from_east, from_lat,
+    sizes, field, zonal, meridional, mass, columns, odd_pairs, even_pairs, from_lat,
     donor, fraction, target, live, advected, outgoing, edge_rows, flux_rows,
 ):
     tracers, levels, rows, width, blocks, capacity, _ = sizes
     fields, span, total = sizes.fields, levels * rows, sizes.fields * rows
-    east_cells = [from_east[HALO + i : HALO + i + 1, :total] for i in range(HALO)]
+    even = lax.rem(lax.axis_index("lon"), 2) == 0
+    from_west = jnp.where(even, odd_pairs[0:HALO], even_pairs[0:HALO])
+    from_east = jnp.where(even, even_pairs[HALO : 2 * HALO], odd_pairs[HALO : 2 * HALO])
+    east_cells = [from_east[i : i + 1, :total] for i in range(HALO)]
     own_cells = [columns[i : i + 1, :total] for i in range(HALO)]
-    east_number = jnp.concatenate([from_east[HALO : HALO + 1, total:]] * tracers, axis=1)
+    east_number = jnp.concatenate([from_east[0:1, total:]] * tracers, axis=1)
     east_flux = face_flux(own_cells + east_cells, east_number)
     lanes = jnp.concatenate(
         [
@@ -199,6 +204,10 @@
     weight_high, weight_low = two_parts(column_weight)
 
     sums = blocks * sizes.margin_rows
+    for block in range(blocks):
+        outgoing[pl.ds(sums + 2 * tracers + block * levels, levels), :] = from_lat[
+            block, pl.ds(sizes.halo_rows, levels), :
+        ]
     for tracer in range(tracers):
         part = pl.ds(tracer * span, span)
         cells = field[part, :]
@@ -256,16 +265,16 @@
         )[None]
 
 
-def blocks_kernel(sizes, own, given, from_lat, other_lat, lon_blocks):
+def blocks_kernel(sizes, own, given, lon_blocks):
     tracers, levels, _, width, blocks, capacity, places = sizes
     size = sizes.margin_rows
     sums = pl.ds(blocks * size, 2 * tracers)
     weighed = jnp.zeros((size, width), jnp.float32)
     for block in range(blocks):
         margin = given[pl.ds(block * size, size), :]
-        for sent, masses in ((margin, from_lat), (own[pl.ds(block * size, size), :], other_lat)):
-            mass = masses[block, pl.ds(sizes.halo_rows, levels), :]
-            weighed = weighed + sent * jnp.concatenate([mass] * (size // levels), axis=0)
+        masses = pl.ds(blocks * size + 2 * tracers + block * levels, levels)
+        for sent, mass in ((margin, own), (own[pl.ds(block * size, size), :], given)):
+            weighed = weighed + sent * jnp.concatenate([mass[masses, :]] * (size // levels), axis=0)
         lon_blocks[block, :, 0:size, :] = jnp.broadcast_to(margin[None], (places, size, width))
     column = lax.broadcasted_iota(jnp.int32, (1, width), 1)
     partial = own[sums, :] + given[sums, :]
@@ -313,9 +322,10 @@
         updated[0, tracer] = merged * scale[tracer : tracer + 1].reshape(1, 1, 1)
 
 
-def shifted(value, axis, step):
-    count = lax.axis_size(axis)
-    pairs = [(i, i + step) for i in range(count) if 0 <= i + step < count]
+def exchanged(value, axis, first):
+    pairs = []
+    for i in range(first, lax.axis_size(axis) - 1, 2):
+        pairs += [(i, i + 1), (i + 1, i)]
     return lax.ppermute(value, axis, pairs)
 
 
@@ -340,25 +350,25 @@
     def near(*values):
         return (pltpu.with_memory_space_constraint(value, pltpu.VMEM) for value in values)
 
-    columns, lat_blocks = pl.pallas_call(
+    columns, columns_odd, lat_blocks = pl.pallas_call(
         functools.partial(pack_kernel, sizes),
         out_shape=(
             shape(8, (fields + levels) * rows),
+            shape(32, (fields + levels) * rows),
             shape(blocks, sizes.halo_rows + levels, width),
         ),
         name="pack_edges",
     )(field, zonal, meridional, mass, target, live)
     from_lat = lax.all_to_all(lat_blocks, "lat", 0, 0, tiled=True)
-    from_west = shifted(columns, "lon", 1)
-    from_east = shifted(columns, "lon", -1)
-    from_lat, from_west, from_east = lax.optimization_barrier((from_lat, from_west, from_east))
-    other_lat = lax.ppermute(from_lat, "panel", [(0, 1), (1, 0)])
+    odd_pairs = exchanged(columns_odd, "lon", 1)
+    even_pairs = exchanged(columns, "lon", 0)
+    from_lat, odd_pairs, even_pairs = lax.optimization_barrier((from_lat, odd_pairs, even_pairs))
     payload_rows = sizes.margin_rows + 2 * sizes.tracers
     advected, outgoing = pl.pallas_call(
         functools.partial(main_kernel, sizes),
         out_shape=(
             shape(fields * rows, width),
-            shape(blocks * sizes.margin_rows + 2 * sizes.tracers, width),
+            shape(blocks * (sizes.margin_rows + levels) + 2 * sizes.tracers, width),
         ),
         scratch_shapes=[
             pltpu.VMEM((fields * rows, width), jnp.float32),
@@ -366,15 +376,17 @@
         ],
         name="advect_and_interpolate",
     )(
-        field, zonal, meridional, mass, *near(columns, from_west, from_east, from_lat),
-        donor, fraction, target, live,
+        *near(
+            field, zonal, meridional, mass, columns, odd_pairs, even_pairs, from_lat,
+            donor, fraction, target, live,
+        )
     )
     given = lax.ppermute(outgoing, "panel", [(0, 1), (1, 0)])
     lon_blocks = pl.pallas_call(
         functools.partial(blocks_kernel, sizes),
         out_shape=shape(blocks, places, payload_rows, width),
         name="margin_blocks",
-    )(*near(outgoing, given, from_lat, other_lat))
+    )(*near(outgoing, given))
     incoming = lax.all_to_all(
         lon_blocks.reshape(blocks * places, payload_rows, width), ("lat", "lon"), 0, 0, tiled=True
     ).reshape(blocks, places, payload_rows, width)
@@ -382,7 +394,7 @@
         functools.partial(fill_kernel, sizes),
         out_shape=jax.ShapeDtypeStruct((1, sizes.tracers, levels, rows, width), jnp.float32),
         name="fill_and_scale",
-    )(*near(advected, incoming), target, live)
+    )(*near(advected, incoming, target, live))
 
 
 def solution(mesh):

time: 38.9 us -> 35.2 us (0.905)
  blocking collectives: 16.7 us -> 14 us
  Pallas kernels: 5.88 us -> 4.29 us
  waiting for transfers between devices: 3.23 us -> 4.34 us
  starting transfers between devices: 12.7 us -> 11.6 us
  local copies, waits for them, and re-layouts: 0 us -> 0.64 us
    all_to_all x1, blocking collectives: 16.7 us -> 14 us  [body(): lax.all_to_all(lon_blocks.reshape(blocks * places, payload_rows, width),...]
    pallas_call x1, Pallas kernels: 1.92 us -> 1.01 us  [body(): pl.pallas_call(functools.partial(main_kernel, sizes), out_shape=(shape(fi...]
    ppermute x3 -> x2, starting transfers between devices: 5.83 us -> 5.08 us  [exchanged(): return lax.ppermute(value, axis, pairs)]
    ppermute x3 -> x2, waiting for transfers between devices: 1.38 us -> 2.1 us  [exchanged(): return lax.ppermute(value, axis, pairs)]
    pallas_call x1, Pallas kernels: 1.87 us -> 1.19 us  [body(): pl.pallas_call(functools.partial(fill_kernel, sizes), out_shape=jax.Shape...]
    unnamed x0 -> x16, local copies, waits for them, and re-layouts: none -> 0.64 us
    ppermute x1, starting transfers between devices: 0.51 us -> 0.01 us  [body(): given = lax.ppermute(outgoing, 'panel', [(0, 1), (1, 0)])]
  transfers between devices with their start and end apart: 5 -> 4, of which waited for: 3 -> 3; matrix products, arithmetic and copies ran while one was open for 0% -> 0% of each run, Pallas kernels for 5% -> 0%
where the time goes in v4:
time: 35.2 us; the launch traced here: 34.9 us
  blocking collectives  14 us (40%)
  starting transfers between devices  11.6 us (33%)
  waiting for transfers between devices  4.34 us (12%)
  Pallas kernels  4.29 us (12%)
  local copies, waits for them, and re-layouts  0.64 us (2%)
    all_to_all x1, blocking collectives, body(): lax.all_to_all(lon_blocks.reshape(blocks * places, payload_rows, width),...  14 us
    all_to_all x1, starting transfers between devices, body(): from_lat = lax.all_to_all(lat_blocks, 'lat', 0, 0, tiled=True)  6.47 us
    ppermute x2, starting transfers between devices, exchanged(): return lax.ppermute(value, axis, pairs)  5.08 us
    ppermute x2, waiting for transfers between devices, exchanged(): return lax.ppermute(value, axis, pairs)  2.1 us
    pallas_call x1, Pallas kernels, body(): pl.pallas_call(functools.partial(pack_kernel, sizes), out_shape=(shape(8,...  2.07 us
    ppermute x1, waiting for transfers between devices, body(): given = lax.ppermute(outgoing, 'panel', [(0, 1), (1, 0)])  1.22 us
    pallas_call x1, Pallas kernels, body(): pl.pallas_call(functools.partial(fill_kernel, sizes), out_shape=jax.Shape...  1.19 us
    all_to_all x1, waiting for transfers between devices, body(): from_lat = lax.all_to_all(lat_blocks, 'lat', 0, 0, tiled=True)  1.02 us
  transfers between devices with their start and end apart: 4, of which 3 were waited for; matrix products, arithmetic and copies ran while one was open for 0% of the time, Pallas kernels for 0%

profile of v4, /device:TPU:0, one launch (start us, length us, event | category | flops | bytes accessed | tf_op | source)
XLA Modules:
  0.0 34.9 jit_solution(11372902540876850953)
XLA Ops:
  0.0 2.1 %pack_edges.1 = (f32[8,320]{1,0:T(8,128)S(1)}, f32[32,320]{1,0:T(8,128)S(1)}, f32[4,112,128]{2,1,0:T(8,128)}) custom-call(f32[256,128]{1,0:T(8,128)} %bitcast.12, f32[64,128]{1,0:T(8,128)} %bitcast.14, f32[64,128]{1,0:T(8,128)} %bitcast.16, f32[64,128]{1,0:T(8,128)} %bitcast.18, s32[4,64]{1,0:T(4,128)} %bitcast.20, s32[1,4]{1,0:T(1,128)} %bitcast.23), custom_call_target="tpu_custom_call" | custom-call | tf_op jit(solution)/shard_map/pack_edges/pallas_call | solution.py:353
  2.1 0.0 copy-start
  2.1 0.0 copy-start.1
  2.1 0.0 copy-start.2
  2.1 0.0 copy-start.3
  2.1 0.0 copy-start.7
  2.1 6.5 %all-to-all-start = ((f32[4,112,128]{2,1,0:T(8,128)}), f32[4,112,128]{2,1,0:T(8,128)S(1)}, u32[]{:S(2)}, u32[]{:S(2)}) async-start(f32[4,112,128]{2,1,0:T(8,128)} %get-tuple-element.14), calls=%async_computation | async-start | bytes 458752 | tf_op jit(solution)/shard_map/all_to_all | solution.py:362
  8.6 0.0 copy-start.6
  8.6 0.8 %collective-permute-start = (f32[32,320]{1,0:T(8,128)S(1)}, f32[32,320]{1,0:T(8,128)S(1)}, u32[]{:S(2)}, u32[]{:S(2)}) collective-permute-start(f32[32,320]{1,0:T(8,128)S(1)} %get-tuple-element.15), channel_id=1, source_target_pairs={{1,2},{2,1},{5,6},{6,5},{9,10},{10,9},{13,14},{14,13},{17,18},{18,... | collective-permute-start | bytes 122888 | tf_op jit(solution)/shard_map/ppermute | solution.py:329
  9.4 0.0 copy-start.4
  9.4 4.3 %collective-permute-start.1 = (f32[8,320]{1,0:T(8,128)S(1)}, f32[8,320]{1,0:T(8,128)S(1)}, u32[]{:S(2)}, u32[]{:S(2)}) collective-permute-start(f32[8,320]{1,0:T(8,128)S(1)} %get-tuple-element.13.columns), channel_id=1, source_target_pairs={{0,1},{1,0},{2,3},{3,2},{4,5},{5,4},{6,7},{7,6},{8,9},{9,8},{10,11... | collective-permute-start | bytes 30728 | tf_op jit(solution)/shard_map/ppermute | solution.py:329
  13.7 2.1 %collective-permute-done.1.even_pairs = f32[8,320]{1,0:T(8,128)S(1)} collective-permute-done((f32[8,320]{1,0:T(8,128)S(1)}, f32[8,320]{1,0:T(8,128)S(1)}, u32[]{:S(2)}, u32[]{:S(2)}) %collective-permute-start.1) | collective-permute-done | bytes 10272 | tf_op jit(solution)/shard_map/ppermute | solution.py:329
  15.8 0.0 collective-permute-done.odd_pairs
  15.8 1.0 %all-to-all-done.from_lat = f32[4,112,128]{2,1,0:T(8,128)S(1)} async-done(((f32[4,112,128]{2,1,0:T(8,128)}), f32[4,112,128]{2,1,0:T(8,128)S(1)}, u32[]{:S(2)}, u32[]{:S(2)}) %all-to-all-start) | async-done | bytes 229408 | tf_op jit(solution)/shard_map/all_to_all | solution.py:362
  16.8 0.0 copy-start.5
  16.8 0.0 copy-done
  16.8 0.0 copy-done.1
  16.8 0.0 copy-done.2
  16.8 0.0 copy-done.3
  16.8 0.0 copy-done.7
  16.8 0.0 copy-done.6
  16.8 0.0 copy-done.4
  16.8 0.6 %copy-done.5 = s32[1,1,1,4]{3,2,1,0:T(1,128)S(1)} copy-done((s32[1,1,1,4]{3,2,1,0:T(1,128)S(1)}, s32[1,1,1,4]{3,2,1,0:T(1,128)}, u32[]{:S(2)}) %copy-start.5) | copy-done | bytes 40
  17.4 1.0 %advect_and_interpolate.1 = (f32[256,128]{1,0:T(8,128)S(1)}, f32[104,128]{1,0:T(8,128)S(1)}) custom-call(f32[256,128]{1,0:T(8,128)S(1)} %bitcast.13, f32[64,128]{1,0:T(8,128)S(1)} %bitcast.15, f32[64,128]{1,0:T(8,128)S(1)} %bitcast.17, f32[64,128]{1,0:T(8,128)S(1)} %bitcast.19, f32[8,320]{1,0:T(8,128)S(1)} %get-tuple-element.13.columns, ...), custom_call_target="tpu_custom_call" | custom-call | tf_op jit(solution)/shard_map/advect_and_interpolate/pallas_call | solution.py:367
  18.5 0.0 collective-permute-start.2
  18.5 1.2 %collective-permute-done.2.given = f32[104,128]{1,0:T(8,128)S(1)} collective-permute-done((f32[104,128]{1,0:T(8,128)S(1)}, f32[104,128]{1,0:T(8,128)S(1)}, u32[]{:S(2)}, u32[]{:S(2)}) %collective-permute-start.2) | collective-permute-done | bytes 53280 | tf_op jit(solution)/shard_map/ppermute | solution.py:384
  19.7 14.0 %all_to_all.10 = f32[16,24,128]{2,1,0:T(8,128)S(1)} all-to-all(f32[16,24,128]{2,1,0:T(8,128)S(1)} %bitcast.11), channel_id=1, replica_groups=mesh['panel'=2,'lat'=4,'lon'=4] {'lat','lon'}, dimensions={0} | all-to-all | bytes 393216 | tf_op jit(solution)/shard_map/all_to_all | solution.py:390
  33.7 1.2 %fill_and_scale.1 = f32[1,4,8,8,128]{4,3,2,1,0:T(8,128)} custom-call(f32[256,128]{1,0:T(8,128)S(1)} %get-tuple-element.19.advected, f32[4,4,24,128]{3,2,1,0:T(8,128)S(1)} %bitcast.10, s32[4,64]{1,0:T(4,128)S(1)} %bitcast.22, s32[1,4]{1,0:T(1,128)S(1)} %bitcast.25), custom_call_target="tpu_custom_call" | custom-call | tf_op jit(solution)/shard_map/fill_and_scale/pallas_call | solution.py:393
  (1 shorter events, 0.0 us)
Async XLA Ops:
  2.1 14.7 %copy-start = (f32[1,4,8,8,128]{4,3,2,1,0:T(8,128)S(1)}, f32[1,4,8,8,128]{4,3,2,1,0:T(8,128)}, u32[]{:S(2)}) copy-start(f32[1,4,8,8,128]{4,3,2,1,0:T(8,128)} %param.8) | copy-start | bytes 393220
  2.1 14.7 %copy-start.1 = (f32[1,8,8,128]{3,2,1,0:T(8,128)S(1)}, f32[1,8,8,128]{3,2,1,0:T(8,128)}, u32[]{:S(2)}) copy-start(f32[1,8,8,128]{3,2,1,0:T(8,128)} %param.9) | copy-start | bytes 98308
  2.1 14.7 %copy-start.2 = (f32[1,8,8,128]{3,2,1,0:T(8,128)S(1)}, f32[1,8,8,128]{3,2,1,0:T(8,128)}, u32[]{:S(2)}) copy-start(f32[1,8,8,128]{3,2,1,0:T(8,128)} %param.10) | copy-start | bytes 98308
  2.1 14.7 %copy-start.3 = (f32[1,8,8,128]{3,2,1,0:T(8,128)S(1)}, f32[1,8,8,128]{3,2,1,0:T(8,128)}, u32[]{:S(2)}) copy-start(f32[1,8,8,128]{3,2,1,0:T(8,128)} %param.11) | copy-start | bytes 98308
  2.1 14.7 %copy-start.7 = (s32[1,1,1,4,64]{4,3,2,1,0:T(4,128)S(1)}, s32[1,1,1,4,64]{4,3,2,1,0:T(4,128)}, u32[]{:S(2)}) copy-start(s32[1,1,1,4,64]{4,3,2,1,0:T(4,128)} %param.12) | copy-start | bytes 3076
  2.1 14.7 %all-to-all-start = ((f32[4,112,128]{2,1,0:T(8,128)}), f32[4,112,128]{2,1,0:T(8,128)S(1)}, u32[]{:S(2)}, u32[]{:S(2)}) async-start(f32[4,112,128]{2,1,0:T(8,128)} %get-tuple-element.14), calls=%async_computation | async-start | bytes 458752 | tf_op jit(solution)/shard_map/all_to_all | solution.py:362
  8.6 8.3 %copy-start.6 = (f32[2,1,1,1,4,64]{5,4,3,2,1,0:T(4,128)S(1)}, f32[2,1,1,1,4,64]{5,4,3,2,1,0:T(4,128)}, u32[]{:S(2)}) copy-start(f32[2,1,1,1,4,64]{5,4,3,2,1,0:T(4,128)} %param.13) | copy-start | bytes 6148
  8.6 7.2 %collective-permute-start = (f32[32,320]{1,0:T(8,128)S(1)}, f32[32,320]{1,0:T(8,128)S(1)}, u32[]{:S(2)}, u32[]{:S(2)}) collective-permute-start(f32[32,320]{1,0:T(8,128)S(1)} %get-tuple-element.15), channel_id=1, source_target_pairs={{1,2},{2,1},{5,6},{6,5},{9,10},{10,9},{13,14},{14,13},{17,18},{18,... | collective-permute-start | bytes 122888 | tf_op jit(solution)/shard_map/ppermute | solution.py:329
  9.4 7.5 %copy-start.4 = (s32[1,1,1,4,64]{4,3,2,1,0:T(4,128)S(1)}, s32[1,1,1,4,64]{4,3,2,1,0:T(4,128)}, u32[]{:S(2)}) copy-start(s32[1,1,1,4,64]{4,3,2,1,0:T(4,128)} %param.14) | copy-start | bytes 3076
  9.4 6.4 %collective-permute-start.1 = (f32[8,320]{1,0:T(8,128)S(1)}, f32[8,320]{1,0:T(8,128)S(1)}, u32[]{:S(2)}, u32[]{:S(2)}) collective-permute-start(f32[8,320]{1,0:T(8,128)S(1)} %get-tuple-element.13.columns), channel_id=1, source_target_pairs={{0,1},{1,0},{2,3},{3,2},{4,5},{5,4},{6,7},{7,6},{8,9},{9,8},{10,11... | collective-permute-start | bytes 30728 | tf_op jit(solution)/shard_map/ppermute | solution.py:329
  16.8 0.7 %copy-start.5 = (s32[1,1,1,4]{3,2,1,0:T(1,128)S(1)}, s32[1,1,1,4]{3,2,1,0:T(1,128)}, u32[]{:S(2)}) copy-start(s32[1,1,1,4]{3,2,1,0:T(1,128)} %param.15) | copy-start | bytes 52
  18.5 1.2 %collective-permute-start.2 = (f32[104,128]{1,0:T(8,128)S(1)}, f32[104,128]{1,0:T(8,128)S(1)}, u32[]{:S(2)}, u32[]{:S(2)}) collective-permute-start(f32[104,128]{1,0:T(8,128)S(1)} %get-tuple-element.20.own), channel_id=1, source_target_pairs={{0,16},{16,0},{1,17},{17,1},{2,18},{18,2},{3,19},{19,3},{4,20},{20... | collective-permute-start | bytes 159752 | tf_op jit(solution)/shard_map/ppermute | solution.py:384

commit v5 on v4

--- a/solution.py
+++ b/solution.py
@@ -107,15 +107,28 @@
     return number * (edge - 0.5 * speed * ((edge - far) - (1.0 - 2.0 / 3.0 * speed) * curve))
 
 
-def pack_kernel(sizes, field, zonal, meridional, mass, target, live, columns, columns_odd, lat_blocks):
+def pack_kernel(
+    sizes, field, zonal, meridional, mass, target, live, columns, columns_odd, lat_blocks,
+    north_stage, south_stage, mass_stage, sems,
+):
     _, levels, rows, width, blocks, capacity, _ = sizes
-    fields = sizes.fields
-    turned = jnp.concatenate([field[...], zonal[...]], axis=0).T
-    columns[0:HALO] = turned[width - HALO : width]
-    columns[HALO : 2 * HALO] = turned[0:HALO]
-    columns[2 * HALO :] = jnp.zeros((columns.shape[0] - 2 * HALO, columns.shape[1]), jnp.float32)
-    columns_odd[0:8] = columns[...]
-    columns_odd[8:] = jnp.zeros((columns_odd.shape[0] - 8, columns.shape[1]), jnp.float32)
+    fields, halo_rows = sizes.fields, sizes.halo_rows
+    here = lax.axis_index("lat")
+    for i in range(HALO):
+        part = pl.ds(i * fields, fields)
+        north_stage[part, :] = field[pl.ds(rows - HALO + i, fields, stride=rows), :]
+        south_stage[part, :] = field[pl.ds(i, fields, stride=rows), :]
+    south_stage[pl.ds(HALO * fields, levels), :] = meridional[pl.ds(0, levels, stride=rows), :]
+    north = jnp.minimum(here + 1, blocks - 1)
+    south = jnp.maximum(here - 1, 0)
+    copies = [
+        pltpu.make_async_copy(
+            north_stage, lat_blocks.at[north, pl.ds(0, HALO * fields)], sems.at[0]
+        ),
+        pltpu.make_async_copy(south_stage, lat_blocks.at[south, pl.ds(0, halo_rows)], sems.at[1]),
+    ]
+    for copy in copies:
+        copy.start()
     spots = row_of(target[...])
     row_hot = one_hot(spots // width, rows)
     column_hot = one_hot(lax.rem(spots, width), width).astype(jnp.bfloat16)
@@ -123,37 +136,50 @@
     picked = jnp.sum(
         picked.reshape(levels, rows, spots.shape[1]) * row_hot[None], axis=1
     ) * live_row(live[...], capacity)
-    here = lax.axis_index("lat")
     for block in range(blocks):
         part = picked[:, block * capacity : (block + 1) * capacity]
-        lat_blocks[block, pl.ds(sizes.halo_rows, levels), :] = jnp.concatenate(
-            [part] * sizes.sides, axis=1
-        )
-
-        @pl.when(block > here)
-        def northward():
-            for i in range(HALO):
-                lat_blocks[block, pl.ds(i * fields, fields), :] = field[
-                    pl.ds(rows - HALO + i, fields, stride=rows), :
-                ]
-            lat_blocks[block, pl.ds(HALO * fields, levels), :] = jnp.zeros(
-                (levels, width), jnp.float32
-            )
-
-        @pl.when(block <= here)
-        def southward():
-            for i in range(HALO):
-                lat_blocks[block, pl.ds(i * fields, fields), :] = field[
-                    pl.ds(i, fields, stride=rows), :
-                ]
-            lat_blocks[block, pl.ds(HALO * fields, levels), :] = meridional[
-                pl.ds(0, levels, stride=rows), :
-            ]
+        mass_stage[block] = jnp.concatenate([part] * sizes.sides, axis=1)
+    copy = pltpu.make_async_copy(
+        mass_stage, lat_blocks.at[:, pl.ds(halo_rows, levels)], sems.at[2]
+    )
+    copy.start()
+    copies.append(copy)
+    turned = jnp.concatenate([field[...], zonal[...]], axis=0).T
+    edges = jnp.concatenate(
+        [
+            turned[width - HALO : width],
+            turned[0:HALO],
+            jnp.zeros((columns.shape[0] - 2 * HALO, columns.shape[1]), jnp.float32),
+        ],
+        axis=0,
+    )
+    columns[...] = edges
+    columns_odd[0 : columns.shape[0]] = edges
+    columns_odd[columns.shape[0] :] = jnp.zeros(
+        (columns_odd.shape[0] - columns.shape[0], columns.shape[1]), jnp.float32
+    )
+    for copy in copies:
+        copy.wait()
+
+
+def tables_kernel(
+    sizes, donor, fraction, target, live, kept, row_hit, column_hot, row_weight, high, low
+):
+    _, _, rows, width, _, capacity, _ = sizes
+    spots = row_of(target[...])
+    row_hit[...] = one_hot(spots // width, rows) * live_row(live[...], capacity)
+    column_hot[...] = one_hot(lax.rem(spots, width), width).astype(jnp.bfloat16)
+    kept[...] = 1.0 - dot(row_hit[...].astype(jnp.bfloat16), column_hot[...], True)
+    starts = row_of(donor[...])
+    row_weight[...] = stencil_weights(starts // width, row_of(fraction[0]), rows)
+    high[...], low[...] = two_parts(
+        stencil_weights(lax.rem(starts, width), row_of(fraction[1]), width)
+    )
 
 
 def main_kernel(
     sizes, field, zonal, meridional, mass, columns, odd_pairs, even_pairs, from_lat,
-    donor, fraction, target, live, advected, outgoing, edge_rows, flux_rows,
+    kept, row_weight, weight_high, weight_low, advected, outgoing, edge_rows, flux_rows,
 ):
     tracers, levels, rows, width, blocks, capacity, _ = sizes
     fields, span, total = sizes.fields, levels * rows, sizes.fields * rows
@@ -192,17 +218,7 @@
     column = lax.broadcasted_iota(jnp.int32, (span, width), 1)
     row = lax.broadcasted_iota(jnp.int32, (levels, rows, width), 1)
 
-    spots = row_of(target[...])
-    row_hit = one_hot(spots // width, rows) * live_row(live[...], capacity)
-    column_hot = one_hot(lax.rem(spots, width), width).astype(jnp.bfloat16)
-    kept = 1.0 - dot(row_hit.astype(jnp.bfloat16), column_hot, True)
     weights = mass[...].reshape(levels, rows, width)
-
-    starts = row_of(donor[...])
-    row_weight = stencil_weights(starts // width, row_of(fraction[0]), rows)
-    column_weight = stencil_weights(lax.rem(starts, width), row_of(fraction[1]), width)
-    weight_high, weight_low = two_parts(column_weight)
-
     sums = blocks * sizes.margin_rows
     for block in range(blocks):
         outgoing[pl.ds(sums + 2 * tracers + block * levels, levels), :] = from_lat[
@@ -244,13 +260,14 @@
         next_flux = pltpu.roll(jnp.where(row == 0, edge3, flux), rows - 1, 1)
         result = result.reshape(levels, rows, width) - (next_flux - flux)
         flat = result.reshape(span, width)
-        advected[part, :] = flat
+        remaining = result * kept[...][None]
+        advected[part, :] = remaining.reshape(span, width)
 
         high, low = two_parts(flat)
-        across = dot(high, weight_high) + (dot(high, weight_low) + dot(low, weight_high))
-        payload = jnp.sum(
-            across.reshape(levels, rows, starts.shape[1]) * row_weight[None], axis=1
+        across = dot(high, weight_high[...]) + (
+            dot(high, weight_low[...]) + dot(low, weight_high[...])
         )
+        payload = jnp.sum(across.reshape(levels, rows, -1) * row_weight[...][None], axis=1)
         base, lane = sizes.spot(tracer)
         for block in range(blocks):
             at = block * capacity
@@ -258,7 +275,7 @@
                 pl.ds(block * sizes.margin_rows + base, levels), lane : lane + capacity
             ] = payload[:, at : at + capacity]
         outgoing[sums + tracer : sums + tracer + 1, :] = jnp.sum(
-            weights * result * kept[None], axis=(0, 1)
+            weights * remaining, axis=(0, 1)
         )[None]
         outgoing[sums + tracers + tracer : sums + tracers + tracer + 1, :] = jnp.sum(
             weights * cells3, axis=(0, 1)
@@ -275,7 +292,8 @@
         masses = pl.ds(blocks * size + 2 * tracers + block * levels, levels)
         for sent, mass in ((margin, own), (own[pl.ds(block * size, size), :], given)):
             weighed = weighed + sent * jnp.concatenate([mass[masses, :]] * (size // levels), axis=0)
-        lon_blocks[block, :, 0:size, :] = jnp.broadcast_to(margin[None], (places, size, width))
+        for place in range(places):
+            lon_blocks[pl.ds((block * places + place) * (size + 1), size), :] = margin
     column = lax.broadcasted_iota(jnp.int32, (1, width), 1)
     partial = own[sums, :] + given[sums, :]
     added = []
@@ -286,40 +304,37 @@
     partial = partial + jnp.concatenate(
         added + [jnp.zeros((tracers, width), jnp.float32)], axis=0
     )
-    lon_blocks[:, :, size:, :] = jnp.broadcast_to(
-        partial[None, None], (blocks, places, 2 * tracers, width)
-    )
-
-
-def fill_kernel(sizes, advected, incoming, target, live, updated):
-    tracers, levels, rows, width, blocks, capacity, _ = sizes
+    totals = jnp.sum(partial, axis=1, keepdims=True)
+    line = jnp.zeros((1, width), jnp.float32)
+    for i in range(2 * tracers):
+        line = jnp.where(column == i, totals[i : i + 1], line)
+    for block in range(blocks * places):
+        lon_blocks[pl.ds(block * (size + 1) + size, 1), :] = line
+
+
+def fill_kernel(sizes, advected, incoming, row_hit, column_hot, updated):
+    tracers, levels, rows, width, blocks, capacity, places = sizes
     size = sizes.margin_rows
     place = lax.axis_index("lon")
     arrived = []
     for block in range(blocks):
-        piece = incoming[block, place, 0:size, :]
+        piece = incoming[pl.ds((block * places + place) * (size + 1), size), :]
         arrived.append(
             jnp.concatenate(
                 [piece[:, i * capacity : (i + 1) * capacity] for i in range(sizes.sides)], axis=0
             )
         )
     arrived = jnp.concatenate(arrived, axis=1)
-    spots = row_of(target[...])
-    row_hit = one_hot(spots // width, rows) * live_row(live[...], capacity)
-    column_hot = one_hot(lax.rem(spots, width), width).astype(jnp.bfloat16)
-    kept = 1.0 - dot(row_hit.astype(jnp.bfloat16), column_hot, True)
-    sums = jnp.sum(incoming[:, :, size:, :], axis=(0, 1))
-    sums = jnp.sum(sums, axis=1, keepdims=True)
-    scale = sums[tracers:] / sums[:tracers]
+    line = jnp.sum(
+        incoming[pl.ds(size, blocks * places, stride=size + 1), :], axis=0, keepdims=True
+    )
     for tracer in range(tracers):
         values = arrived[tracer * levels : (tracer + 1) * levels]
-        spread = (values[:, None, :] * row_hit[None]).reshape(levels * rows, -1)
-        placed = sum(dot(part, column_hot, True) for part in three_parts(spread))
+        spread = (values[:, None, :] * row_hit[...][None]).reshape(levels * rows, -1)
+        placed = sum(dot(part, column_hot[...], True) for part in three_parts(spread))
         old = advected[pl.ds(tracer * levels * rows, levels * rows), :]
-        merged = old.reshape(levels, rows, width) * kept[None] + placed.reshape(
-            levels, rows, width
-        )
-        updated[0, tracer] = merged * scale[tracer : tracer + 1].reshape(1, 1, 1)
+        scale = line[:, tracers + tracer : tracers + tracer + 1] / line[:, tracer : tracer + 1]
+        updated[0, tracer] = ((old + placed) * scale).reshape(levels, rows, width)
 
 
 def exchanged(value, axis, first):
@@ -350,20 +365,43 @@
     def near(*values):
         return (pltpu.with_memory_space_constraint(value, pltpu.VMEM) for value in values)
 
+    slots = blocks * capacity
     columns, columns_odd, lat_blocks = pl.pallas_call(
         functools.partial(pack_kernel, sizes),
         out_shape=(
             shape(8, (fields + levels) * rows),
             shape(32, (fields + levels) * rows),
-            shape(blocks, sizes.halo_rows + levels, width),
+            jax.ShapeDtypeStruct((blocks, sizes.halo_rows + levels, width), jnp.float32),
         ),
+        out_specs=(
+            pl.BlockSpec(memory_space=pltpu.VMEM),
+            pl.BlockSpec(memory_space=pltpu.VMEM),
+            pl.BlockSpec(memory_space=pl.ANY),
+        ),
+        scratch_shapes=[
+            pltpu.VMEM((HALO * fields, width), jnp.float32),
+            pltpu.VMEM((sizes.halo_rows, width), jnp.float32),
+            pltpu.VMEM((blocks, levels, width), jnp.float32),
+            pltpu.SemaphoreType.DMA((3,)),
+        ],
         name="pack_edges",
     )(field, zonal, meridional, mass, target, live)
     from_lat = lax.all_to_all(lat_blocks, "lat", 0, 0, tiled=True)
     odd_pairs = exchanged(columns_odd, "lon", 1)
     even_pairs = exchanged(columns, "lon", 0)
+    kept, row_hit, column_hot, *weights = pl.pallas_call(
+        functools.partial(tables_kernel, sizes),
+        out_shape=(
+            shape(rows, width),
+            shape(rows, slots),
+            pltpu.VMEM((width, slots), jnp.bfloat16),
+            shape(rows, slots),
+            pltpu.VMEM((width, slots), jnp.bfloat16),
+            pltpu.VMEM((width, slots), jnp.bfloat16),
+        ),
+        name="index_tables",
+    )(donor, fraction, target, live)
     from_lat, odd_pairs, even_pairs = lax.optimization_barrier((from_lat, odd_pairs, even_pairs))
-    payload_rows = sizes.margin_rows + 2 * sizes.tracers
     advected, outgoing = pl.pallas_call(
         functools.partial(main_kernel, sizes),
         out_shape=(
@@ -378,23 +416,24 @@
     )(
         *near(
             field, zonal, meridional, mass, columns, odd_pairs, even_pairs, from_lat,
-            donor, fraction, target, live,
+            kept, *weights,
         )
     )
     given = lax.ppermute(outgoing, "panel", [(0, 1), (1, 0)])
+    block_rows = sizes.margin_rows + 1
     lon_blocks = pl.pallas_call(
         functools.partial(blocks_kernel, sizes),
-        out_shape=shape(blocks, places, payload_rows, width),
+        out_shape=shape(blocks * places * block_rows, width),
         name="margin_blocks",
     )(*near(outgoing, given))
     incoming = lax.all_to_all(
-        lon_blocks.reshape(blocks * places, payload_rows, width), ("lat", "lon"), 0, 0, tiled=True
-    ).reshape(blocks, places, payload_rows, width)
+        lon_blocks.reshape(blocks * places, 1, block_rows * width), ("lat", "lon"), 0, 0, tiled=True
+    ).reshape(blocks * places * block_rows, width)
     return pl.pallas_call(
         functools.partial(fill_kernel, sizes),
         out_shape=jax.ShapeDtypeStruct((1, sizes.tracers, levels, rows, width), jnp.float32),
         name="fill_and_scale",
-    )(*near(advected, incoming, target, live))
+    )(*near(advected, incoming, row_hit, column_hot))
 
 
 def solution(mesh):

time: 35.2 us -> 33.2 us (0.943)
  blocking collectives: 14 us -> 12.8 us
  Pallas kernels: 4.29 us -> 5.12 us
  waiting for transfers between devices: 4.34 us -> 3.51 us
  local copies, waits for them, and re-layouts: 0.64 us -> 0.03 us
    all_to_all x1, blocking collectives: 14 us -> 12.8 us  [body(): lax.all_to_all(lon_blocks.reshape(blocks * places, 1, block_rows * width)...]
    pallas_call x0 -> x1, Pallas kernels: none -> 0.97 us  [body(): pl.pallas_call(functools.partial(tables_kernel, sizes), out_shape=(shape(...]
    ppermute x2, waiting for transfers between devices: 2.1 us -> 1.14 us  [exchanged(): return lax.ppermute(value, axis, pairs)]
    unnamed x16 -> x8, local copies, waits for them, and re-layouts: 0.64 us -> 0.03 us
  transfers between devices with their start and end apart: 4 -> 4, of which waited for: 3 -> 3; matrix products, arithmetic and copies ran while one was open for 0% -> 0% of each run, Pallas kernels for 0% -> 3%
where the time goes in v5:
time: 33.2 us; the launch traced here: 32.9 us
  blocking collectives  12.8 us (39%)
  starting transfers between devices  11.4 us (34%)
  Pallas kernels  5.12 us (15%)
  waiting for transfers between devices  3.51 us (11%)
    all_to_all x1, blocking collectives, body(): lax.all_to_all(lon_blocks.reshape(blocks * places, 1, block_rows * width)...  12.8 us
    all_to_all x1, starting transfers between devices, body(): from_lat = lax.all_to_all(lat_blocks, 'lat', 0, 0, tiled=True)  6.47 us
    ppermute x2, starting transfers between devices, exchanged(): return lax.ppermute(value, axis, pairs)  4.94 us
    pallas_call x1, Pallas kernels, body(): pl.pallas_call(functools.partial(pack_kernel, sizes), out_shape=(shape(8,...  1.94 us
    ppermute x1, waiting for transfers between devices, body(): given = lax.ppermute(outgoing, 'panel', [(0, 1), (1, 0)])  1.22 us
    all_to_all x1, waiting for transfers between devices, body(): from_lat = lax.all_to_all(lat_blocks, 'lat', 0, 0, tiled=True)  1.15 us
    ppermute x2, waiting for transfers between devices, exchanged(): return lax.ppermute(value, axis, pairs)  1.14 us
    pallas_call x1, Pallas kernels, body(): pl.pallas_call(functools.partial(fill_kernel, sizes), out_shape=jax.Shape...  1.11 us
  transfers between devices with their start and end apart: 4, of which 3 were waited for; matrix products, arithmetic and copies ran while one was open for 0% of the time, Pallas kernels for 3%

profile of v5, /device:TPU:0, one launch (start us, length us, event | category | flops | bytes accessed | tf_op | source)
XLA Modules:
  0.0 32.9 jit_solution(4431244725176759704)
XLA Ops:
  0.0 1.9 %pack_edges.1 = (f32[8,320]{1,0:T(8,128)S(1)}, f32[32,320]{1,0:T(8,128)S(1)}, f32[4,112,128]{2,1,0:T(8,128)}) custom-call(f32[256,128]{1,0:T(8,128)} %bitcast.12, f32[64,128]{1,0:T(8,128)} %bitcast.14, f32[64,128]{1,0:T(8,128)} %bitcast.16, f32[64,128]{1,0:T(8,128)} %bitcast.18, s32[4,64]{1,0:T(4,128)} %bitcast.20, s32[1,4]{1,0:T(1,128)} %bitcast.23), custom_call_target="tpu_custom_call" | custom-call | tf_op jit(solution)/shard_map/pack_edges/pallas_call | solution.py:369
  1.9 0.0 copy-start
  2.0 0.0 copy-start.1
  2.0 0.0 copy-start.2
  2.0 0.0 copy-start.3
  2.0 6.5 %all-to-all-start = ((f32[4,112,128]{2,1,0:T(8,128)}), f32[4,112,128]{2,1,0:T(8,128)S(1)}, u32[]{:S(2)}, u32[]{:S(2)}) async-start(f32[4,112,128]{2,1,0:T(8,128)} %get-tuple-element.20), calls=%async_computation | async-start | bytes 458752 | tf_op jit(solution)/shard_map/all_to_all | solution.py:389
  8.5 0.7 %collective-permute-start = (f32[32,320]{1,0:T(8,128)S(1)}, f32[32,320]{1,0:T(8,128)S(1)}, u32[]{:S(2)}, u32[]{:S(2)}) collective-permute-start(f32[32,320]{1,0:T(8,128)S(1)} %get-tuple-element.21), channel_id=1, source_target_pairs={{1,2},{2,1},{5,6},{6,5},{9,10},{10,9},{13,14},{14,13},{17,18},{18,... | collective-permute-start | bytes 122888 | tf_op jit(solution)/shard_map/ppermute | solution.py:344
  9.1 4.3 %collective-permute-start.1 = (f32[8,320]{1,0:T(8,128)S(1)}, f32[8,320]{1,0:T(8,128)S(1)}, u32[]{:S(2)}, u32[]{:S(2)}) collective-permute-start(f32[8,320]{1,0:T(8,128)S(1)} %get-tuple-element.19.columns), channel_id=1, source_target_pairs={{0,1},{1,0},{2,3},{3,2},{4,5},{5,4},{6,7},{7,6},{8,9},{9,8},{10,11... | collective-permute-start | bytes 30728 | tf_op jit(solution)/shard_map/ppermute | solution.py:344
  13.4 1.0 %index_tables.1 = (f32[8,128]{1,0:T(8,128)S(1)}, f32[8,256]{1,0:T(8,128)S(1)}, bf16[128,256]{1,0:T(8,128)(2,1)S(1)}, f32[8,256]{1,0:T(8,128)S(1)}, bf16[128,256]...) custom-call(s32[4,64]{1,0:T(4,128)} %bitcast.25, f32[2,4,64]{2,1,0:T(4,128)} %bitcast.22, s32[4,64]{1,0:T(4,128)} %bitcast.21, ...), custom_call_target="tpu_custom_call" | custom-call | tf_op jit(solution)/shard_map/index_tables/pallas_call | solution.py:392
  14.4 1.1 %collective-permute-done.1.even_pairs = f32[8,320]{1,0:T(8,128)S(1)} collective-permute-done((f32[8,320]{1,0:T(8,128)S(1)}, f32[8,320]{1,0:T(8,128)S(1)}, u32[]{:S(2)}, u32[]{:S(2)}) %collective-permute-start.1) | collective-permute-done | bytes 10272 | tf_op jit(solution)/shard_map/ppermute | solution.py:344
  15.5 0.0 collective-permute-done.odd_pairs
  15.5 1.2 %all-to-all-done.from_lat = f32[4,112,128]{2,1,0:T(8,128)S(1)} async-done(((f32[4,112,128]{2,1,0:T(8,128)}), f32[4,112,128]{2,1,0:T(8,128)S(1)}, u32[]{:S(2)}, u32[]{:S(2)}) %all-to-all-start) | async-done | bytes 229408 | tf_op jit(solution)/shard_map/all_to_all | solution.py:389
  16.7 0.0 copy-done
  16.7 0.0 copy-done.1
  16.7 0.0 copy-done.2
  16.7 0.0 copy-done.3
  16.7 1.0 %advect_and_interpolate.1 = (f32[256,128]{1,0:T(8,128)S(1)}, f32[104,128]{1,0:T(8,128)S(1)}) custom-call(f32[256,128]{1,0:T(8,128)S(1)} %bitcast.13, f32[64,128]{1,0:T(8,128)S(1)} %bitcast.15, f32[64,128]{1,0:T(8,128)S(1)} %bitcast.17, f32[64,128]{1,0:T(8,128)S(1)} %bitcast.19, f32[8,320]{1,0:T(8,128)S(1)} %get-tuple-element.19.columns, ...), custom_call_target="tpu_custom_call" | custom-call | tf_op jit(solution)/shard_map/advect_and_interpolate/pallas_call | solution.py:405
  17.7 0.0 collective-permute-start.2
  17.7 1.2 %collective-permute-done.2.given = f32[104,128]{1,0:T(8,128)S(1)} collective-permute-done((f32[104,128]{1,0:T(8,128)S(1)}, f32[104,128]{1,0:T(8,128)S(1)}, u32[]{:S(2)}, u32[]{:S(2)}) %collective-permute-start.2) | collective-permute-done | bytes 53280 | tf_op jit(solution)/shard_map/ppermute | solution.py:422
  18.9 0.1 margin_blocks.1
  19.1 12.8 %all_to_all.10 = f32[16,1,2176]{2,1,0:T(1,128)S(1)} all-to-all(f32[16,1,2176]{2,1,0:T(1,128)S(1)} %bitcast.11), channel_id=1, replica_groups=mesh['panel'=2,'lat'=4,'lon'=4] {'lat','lon'}, dimensions={0} | all-to-all | bytes 278528 | tf_op jit(solution)/shard_map/all_to_all | solution.py:429
  31.8 1.1 %fill_and_scale.1 = f32[1,4,8,8,128]{4,3,2,1,0:T(8,128)} custom-call(f32[256,128]{1,0:T(8,128)S(1)} %get-tuple-element.29.advected, f32[272,128]{1,0:T(8,128)S(1)} %bitcast.10, f32[8,256]{1,0:T(8,128)S(1)} %get-tuple-element.31.row_hit, bf16[128,256]{1,0:T(8,128)(2,1)S(1)} %get-tuple-element.32.column_hot), custom_call_target="tpu_custom_call" | custom-call | tf_op jit(solution)/shard_map/fill_and_scale/pallas_call | solution.py:432
Async XLA Ops:
  1.9 14.7 %copy-start = (f32[1,4,8,8,128]{4,3,2,1,0:T(8,128)S(1)}, f32[1,4,8,8,128]{4,3,2,1,0:T(8,128)}, u32[]{:S(2)}) copy-start(f32[1,4,8,8,128]{4,3,2,1,0:T(8,128)} %param.8) | copy-start | bytes 393220
  2.0 14.7 %copy-start.1 = (f32[1,8,8,128]{3,2,1,0:T(8,128)S(1)}, f32[1,8,8,128]{3,2,1,0:T(8,128)}, u32[]{:S(2)}) copy-start(f32[1,8,8,128]{3,2,1,0:T(8,128)} %param.9) | copy-start | bytes 98308
  2.0 14.7 %copy-start.2 = (f32[1,8,8,128]{3,2,1,0:T(8,128)S(1)}, f32[1,8,8,128]{3,2,1,0:T(8,128)}, u32[]{:S(2)}) copy-start(f32[1,8,8,128]{3,2,1,0:T(8,128)} %param.10) | copy-start | bytes 98308
  2.0 14.7 %copy-start.3 = (f32[1,8,8,128]{3,2,1,0:T(8,128)S(1)}, f32[1,8,8,128]{3,2,1,0:T(8,128)}, u32[]{:S(2)}) copy-start(f32[1,8,8,128]{3,2,1,0:T(8,128)} %param.11) | copy-start | bytes 98308
  2.0 14.7 %all-to-all-start = ((f32[4,112,128]{2,1,0:T(8,128)}), f32[4,112,128]{2,1,0:T(8,128)S(1)}, u32[]{:S(2)}, u32[]{:S(2)}) async-start(f32[4,112,128]{2,1,0:T(8,128)} %get-tuple-element.20), calls=%async_computation | async-start | bytes 458752 | tf_op jit(solution)/shard_map/all_to_all | solution.py:389
  8.5 7.1 %collective-permute-start = (f32[32,320]{1,0:T(8,128)S(1)}, f32[32,320]{1,0:T(8,128)S(1)}, u32[]{:S(2)}, u32[]{:S(2)}) collective-permute-start(f32[32,320]{1,0:T(8,128)S(1)} %get-tuple-element.21), channel_id=1, source_target_pairs={{1,2},{2,1},{5,6},{6,5},{9,10},{10,9},{13,14},{14,13},{17,18},{18,... | collective-permute-start | bytes 122888 | tf_op jit(solution)/shard_map/ppermute | solution.py:344
  9.1 6.4 %collective-permute-start.1 = (f32[8,320]{1,0:T(8,128)S(1)}, f32[8,320]{1,0:T(8,128)S(1)}, u32[]{:S(2)}, u32[]{:S(2)}) collective-permute-start(f32[8,320]{1,0:T(8,128)S(1)} %get-tuple-element.19.columns), channel_id=1, source_target_pairs={{0,1},{1,0},{2,3},{3,2},{4,5},{5,4},{6,7},{7,6},{8,9},{9,8},{10,11... | collective-permute-start | bytes 30728 | tf_op jit(solution)/shard_map/ppermute | solution.py:344
  17.7 1.2 %collective-permute-start.2 = (f32[104,128]{1,0:T(8,128)S(1)}, f32[104,128]{1,0:T(8,128)S(1)}, u32[]{:S(2)}, u32[]{:S(2)}) collective-permute-start(f32[104,128]{1,0:T(8,128)S(1)} %get-tuple-element.30.own), channel_id=1, source_target_pairs={{0,16},{16,0},{1,17},{17,1},{2,18},{18,2},{3,19},{19,3},{4,20},{20... | collective-permute-start | bytes 159752 | tf_op jit(solution)/shard_map/ppermute | solution.py:422

commit v6 on v5

--- a/solution.py
+++ b/solution.py
@@ -9,6 +9,7 @@
 from jax.sharding import PartitionSpec as P
 
 HALO = 3
+MASS_ROWS = 64
 
 
 class Sizes(NamedTuple):
@@ -108,27 +109,24 @@
 
 
 def pack_kernel(
-    sizes, field, zonal, meridional, mass, target, live, columns, columns_odd, lat_blocks,
-    north_stage, south_stage, mass_stage, sems,
+    sizes, field, zonal, meridional, mass, target, live, donor, fraction,
+    columns, columns_odd, lat_even, lat_odd, masses, *index_copies,
 ):
     _, levels, rows, width, blocks, capacity, _ = sizes
-    fields, halo_rows = sizes.fields, sizes.halo_rows
+    fields = sizes.fields
     here = lax.axis_index("lat")
+    for copy, source in zip(index_copies, (donor, fraction, target, live), strict=True):
+        copy[...] = source[...]
+    even = lax.rem(here, 2) == 0
     for i in range(HALO):
         part = pl.ds(i * fields, fields)
-        north_stage[part, :] = field[pl.ds(rows - HALO + i, fields, stride=rows), :]
-        south_stage[part, :] = field[pl.ds(i, fields, stride=rows), :]
-    south_stage[pl.ds(HALO * fields, levels), :] = meridional[pl.ds(0, levels, stride=rows), :]
-    north = jnp.minimum(here + 1, blocks - 1)
-    south = jnp.maximum(here - 1, 0)
-    copies = [
-        pltpu.make_async_copy(
-            north_stage, lat_blocks.at[north, pl.ds(0, HALO * fields)], sems.at[0]
-        ),
-        pltpu.make_async_copy(south_stage, lat_blocks.at[south, pl.ds(0, halo_rows)], sems.at[1]),
-    ]
-    for copy in copies:
-        copy.start()
+        northward = field[pl.ds(rows - HALO + i, fields, stride=rows), :]
+        southward = field[pl.ds(i, fields, stride=rows), :]
+        lat_even[part, :] = jnp.where(even, northward, southward)
+        lat_odd[part, :] = jnp.where(even, southward, northward)
+    number = meridional[pl.ds(0, levels, stride=rows), :]
+    lat_even[pl.ds(HALO * fields, levels), :] = number
+    lat_odd[pl.ds(HALO * fields, levels), :] = number
     spots = row_of(target[...])
     row_hot = one_hot(spots // width, rows)
     column_hot = one_hot(lax.rem(spots, width), width).astype(jnp.bfloat16)
@@ -138,12 +136,13 @@
     ) * live_row(live[...], capacity)
     for block in range(blocks):
         part = picked[:, block * capacity : (block + 1) * capacity]
-        mass_stage[block] = jnp.concatenate([part] * sizes.sides, axis=1)
-    copy = pltpu.make_async_copy(
-        mass_stage, lat_blocks.at[:, pl.ds(halo_rows, levels)], sems.at[2]
-    )
-    copy.start()
-    copies.append(copy)
+        masses[pl.ds(block * levels, levels), :] = jnp.concatenate([part] * sizes.sides, axis=1)
+    if two_hops(sizes):
+        for i, step in enumerate((1, 3)):
+            block = pl.multiple_of((here ^ step) * levels, levels)
+            lat_even[pl.ds(sizes.halo_rows + i * levels, levels), :] = masses[
+                pl.ds(block, levels), :
+            ]
     turned = jnp.concatenate([field[...], zonal[...]], axis=0).T
     edges = jnp.concatenate(
         [
@@ -158,8 +157,33 @@
     columns_odd[columns.shape[0] :] = jnp.zeros(
         (columns_odd.shape[0] - columns.shape[0], columns.shape[1]), jnp.float32
     )
-    for copy in copies:
-        copy.wait()
+
+
+def two_hops(sizes):
+    return sizes.blocks == 4
+
+
+def forward_kernel(sizes, masses, lat_even, forwarded):
+    levels = sizes.levels
+    block = pl.multiple_of((lax.axis_index("lat") ^ 2) * levels, levels)
+    forwarded[0:levels, :] = masses[pl.ds(block, levels), :]
+    forwarded[levels:, :] = lat_even[pl.ds(sizes.halo_rows + levels, levels), :]
+
+
+def masses_kernel(sizes, masses, lat_even, forwarded, received):
+    levels = sizes.levels
+    here = lax.axis_index("lat")
+    own = pl.multiple_of(here * levels, levels)
+    pieces = (
+        masses[pl.ds(own, levels), :],
+        lat_even[pl.ds(sizes.halo_rows, levels), :],
+        forwarded[0:levels, :],
+        forwarded[levels:, :],
+    )
+    spare = received.shape[0] - len(pieces) * levels
+    received[pl.ds(len(pieces) * levels, spare), :] = jnp.zeros((spare, sizes.width), jnp.float32)
+    for step, piece in enumerate(pieces):
+        received[pl.ds(pl.multiple_of((here ^ step) * levels, levels), levels), :] = piece
 
 
 def tables_kernel(
@@ -178,7 +202,7 @@
 
 
 def main_kernel(
-    sizes, field, zonal, meridional, mass, columns, odd_pairs, even_pairs, from_lat,
+    sizes, field, zonal, meridional, mass, columns, odd_pairs, even_pairs, lat_odd, lat_even,
     kept, row_weight, weight_high, weight_low, advected, outgoing, edge_rows, flux_rows,
 ):
     tracers, levels, rows, width, blocks, capacity, _ = sizes
@@ -199,19 +223,18 @@
         ],
         axis=0,
     ).T
-    here = lax.axis_index("lat")
-    south, north = jnp.maximum(here - 1, 0), jnp.minimum(here + 1, blocks - 1)
-    has_south, has_north = here > 0, here < blocks - 1
+    even = lax.rem(lax.axis_index("lat"), 2) == 0
     next_rows = []
     for i in range(HALO):
         part = pl.ds(i * fields, fields)
-        south_row = jnp.where(has_south, from_lat[south, part, :], 0.0)
-        north_row = jnp.where(has_north, from_lat[north, part, :], 0.0)
+        first, second = lat_even[part, :], lat_odd[part, :]
+        north_row = jnp.where(even, first, second)
         next_rows.append(north_row)
-        edge_rows[pl.ds(rows - HALO + i, fields, stride=rows), :] = south_row
+        edge_rows[pl.ds(rows - HALO + i, fields, stride=rows), :] = jnp.where(even, second, first)
         edge_rows[pl.ds(i, fields, stride=rows), :] = north_row
     last_rows = [field[pl.ds(rows - HALO + i, fields, stride=rows), :] for i in range(HALO)]
-    north_number = jnp.where(has_north, from_lat[north, pl.ds(HALO * fields, levels), :], 0.0)
+    part = pl.ds(HALO * fields, levels)
+    north_number = jnp.where(even, lat_even[part, :], lat_odd[part, :])
     flux_rows[pl.ds(0, fields, stride=rows), :] = face_flux(
         last_rows + next_rows, jnp.concatenate([north_number] * tracers, axis=0)
     )
@@ -220,10 +243,6 @@
 
     weights = mass[...].reshape(levels, rows, width)
     sums = blocks * sizes.margin_rows
-    for block in range(blocks):
-        outgoing[pl.ds(sums + 2 * tracers + block * levels, levels), :] = from_lat[
-            block, pl.ds(sizes.halo_rows, levels), :
-        ]
     for tracer in range(tracers):
         part = pl.ds(tracer * span, span)
         cells = field[part, :]
@@ -282,16 +301,19 @@
         )[None]
 
 
-def blocks_kernel(sizes, own, given, lon_blocks):
+def blocks_kernel(sizes, own, given, own_masses, given_masses, lon_blocks):
     tracers, levels, _, width, blocks, capacity, places = sizes
     size = sizes.margin_rows
     sums = pl.ds(blocks * size, 2 * tracers)
     weighed = jnp.zeros((size, width), jnp.float32)
     for block in range(blocks):
         margin = given[pl.ds(block * size, size), :]
-        masses = pl.ds(blocks * size + 2 * tracers + block * levels, levels)
-        for sent, mass in ((margin, own), (own[pl.ds(block * size, size), :], given)):
-            weighed = weighed + sent * jnp.concatenate([mass[masses, :]] * (size // levels), axis=0)
+        part = pl.ds(block * levels, levels)
+        for sent, mass in (
+            (margin, own_masses[part, :]),
+            (own[pl.ds(block * size, size), :], given_masses[part, :]),
+        ):
+            weighed = weighed + sent * jnp.concatenate([mass] * (size // levels), axis=0)
         for place in range(places):
             lon_blocks[pl.ds((block * places + place) * (size + 1), size), :] = margin
     column = lax.broadcasted_iota(jnp.int32, (1, width), 1)
@@ -366,29 +388,42 @@
         return (pltpu.with_memory_space_constraint(value, pltpu.VMEM) for value in values)
 
     slots = blocks * capacity
-    columns, columns_odd, lat_blocks = pl.pallas_call(
+    columns, columns_odd, lat_even, lat_odd, masses, *index_copies = pl.pallas_call(
         functools.partial(pack_kernel, sizes),
         out_shape=(
             shape(8, (fields + levels) * rows),
-            shape(32, (fields + levels) * rows),
-            jax.ShapeDtypeStruct((blocks, sizes.halo_rows + levels, width), jnp.float32),
+            shape(16, (fields + levels) * rows),
+            shape(sizes.halo_rows + (2 * levels if two_hops(sizes) else 0), width),
+            shape(sizes.halo_rows, width),
+            shape(blocks * levels, width),
+            pltpu.VMEM(donor.shape, donor.dtype),
+            pltpu.VMEM(fraction.shape, fraction.dtype),
+            pltpu.VMEM(target.shape, target.dtype),
+            pltpu.VMEM(live.shape, live.dtype),
         ),
-        out_specs=(
-            pl.BlockSpec(memory_space=pltpu.VMEM),
-            pl.BlockSpec(memory_space=pltpu.VMEM),
-            pl.BlockSpec(memory_space=pl.ANY),
-        ),
-        scratch_shapes=[
-            pltpu.VMEM((HALO * fields, width), jnp.float32),
-            pltpu.VMEM((sizes.halo_rows, width), jnp.float32),
-            pltpu.VMEM((blocks, levels, width), jnp.float32),
-            pltpu.SemaphoreType.DMA((3,)),
-        ],
         name="pack_edges",
-    )(field, zonal, meridional, mass, target, live)
-    from_lat = lax.all_to_all(lat_blocks, "lat", 0, 0, tiled=True)
+    )(field, zonal, meridional, mass, target, live, donor, fraction)
+    lat_even = exchanged(lat_even, "lat", 0)
     odd_pairs = exchanged(columns_odd, "lon", 1)
+    lat_odd = exchanged(lat_odd, "lat", 1)
     even_pairs = exchanged(columns, "lon", 0)
+    if two_hops(sizes):
+        forwarded = pl.pallas_call(
+            functools.partial(forward_kernel, sizes),
+            out_shape=shape(2 * levels, width),
+            name="forward_masses",
+        )(*near(masses, lat_even))
+        forwarded = lax.ppermute(forwarded, "lat", [(i, i ^ 2) for i in range(blocks)])
+        masses = pl.pallas_call(
+            functools.partial(masses_kernel, sizes),
+            out_shape=shape(MASS_ROWS, width),
+            name="gather_masses",
+        )(*near(masses, lat_even, forwarded))
+    else:
+        masses = lax.all_to_all(
+            masses.reshape(blocks, levels, width), "lat", 0, 0, tiled=True
+        ).reshape(blocks * levels, width)
+    given_masses = lax.ppermute(masses, "panel", [(0, 1), (1, 0)])
     kept, row_hit, column_hot, *weights = pl.pallas_call(
         functools.partial(tables_kernel, sizes),
         out_shape=(
@@ -400,13 +435,12 @@
             pltpu.VMEM((width, slots), jnp.bfloat16),
         ),
         name="index_tables",
-    )(donor, fraction, target, live)
-    from_lat, odd_pairs, even_pairs = lax.optimization_barrier((from_lat, odd_pairs, even_pairs))
+    )(*near(*index_copies))
     advected, outgoing = pl.pallas_call(
         functools.partial(main_kernel, sizes),
         out_shape=(
             shape(fields * rows, width),
-            shape(blocks * (sizes.margin_rows + levels) + 2 * sizes.tracers, width),
+            shape(blocks * sizes.margin_rows + 2 * sizes.tracers, width),
         ),
         scratch_shapes=[
             pltpu.VMEM((fields * rows, width), jnp.float32),
@@ -415,7 +449,7 @@
         name="advect_and_interpolate",
     )(
         *near(
-            field, zonal, meridional, mass, columns, odd_pairs, even_pairs, from_lat,
+            field, zonal, meridional, mass, columns, odd_pairs, even_pairs, lat_odd, lat_even,
             kept, *weights,
         )
     )
@@ -425,7 +459,7 @@
         functools.partial(blocks_kernel, sizes),
         out_shape=shape(blocks * places * block_rows, width),
         name="margin_blocks",
-    )(*near(outgoing, given))
+    )(*near(outgoing, given, masses, given_masses))
     incoming = lax.all_to_all(
         lon_blocks.reshape(blocks * places, 1, block_rows * width), ("lat", "lon"), 0, 0, tiled=True
     ).reshape(blocks * places * block_rows, width)

time: 33.2 us -> 31.8 us (0.958)
  waiting for transfers between devices: 3.51 us -> 1.22 us
  starting transfers between devices: 11.4 us -> 12.9 us
  Pallas kernels: 5.12 us -> 3.94 us
  blocking collectives: 12.8 us -> 13.4 us
    all_to_all x1 -> x0, starting transfers between devices: 6.47 us -> none  [body(): from_lat = lax.all_to_all(lat_blocks, 'lat', 0, 0, tiled=True)]
    ppermute x0 -> x2, starting transfers between devices: none -> 4.19 us  [the longest x1 3.91 us: body(): lax.ppermute(forwarded, 'lat', [(i, i ^ 2) for i in range(blocks)])]
    ppermute x2 -> x4, starting transfers between devices: 4.94 us -> 8.7 us  [exchanged(): return lax.ppermute(value, axis, pairs)]
    all_to_all x1 -> x0, waiting for transfers between devices: 1.15 us -> none  [body(): from_lat = lax.all_to_all(lat_blocks, 'lat', 0, 0, tiled=True)]
    ppermute x2 -> x4, waiting for transfers between devices: 1.14 us -> 0.01 us  [exchanged(): return lax.ppermute(value, axis, pairs)]
    pallas_call x1, Pallas kernels: 0.97 us -> 0.26 us  [body(): pl.pallas_call(functools.partial(tables_kernel, sizes), out_shape=(shape(...]
    all_to_all x1, blocking collectives: 12.8 us -> 13.4 us  [body(): lax.all_to_all(lon_blocks.reshape(blocks * places, 1, block_rows * width)...]
    ppermute x1, waiting for transfers between devices: 1.22 us -> 0.63 us  [body(): given = lax.ppermute(outgoing, 'panel', [(0, 1), (1, 0)])]
  transfers between devices with their start and end apart: 4 -> 7, of which waited for: 3 -> 3; matrix products, arithmetic and copies ran while one was open for 0% -> 0% of each run, Pallas kernels for 3% -> 4%
where the time goes in v6:
time: 31.8 us; the launch traced here: 31.6 us
  blocking collectives  13.4 us (42%)
  starting transfers between devices  12.9 us (41%)
  Pallas kernels  3.94 us (12%)
  waiting for transfers between devices  1.22 us (4%)
    all_to_all x1, blocking collectives, body(): lax.all_to_all(lon_blocks.reshape(blocks * places, 1, block_rows * width)...  13.4 us
    ppermute x4, starting transfers between devices, exchanged(): return lax.ppermute(value, axis, pairs)  8.7 us
    ppermute x1, starting transfers between devices, body(): lax.ppermute(forwarded, 'lat', [(i, i ^ 2) for i in range(blocks)])  3.91 us
    pallas_call x1, Pallas kernels, body(): pl.pallas_call(functools.partial(pack_kernel, sizes), out_shape=(shape(8,...  1.43 us
    pallas_call x1, Pallas kernels, body(): pl.pallas_call(functools.partial(fill_kernel, sizes), out_shape=jax.Shape...  1.11 us
    pallas_call x1, Pallas kernels, body(): pl.pallas_call(functools.partial(main_kernel, sizes), out_shape=(shape(fi...  1.01 us
  transfers between devices with their start and end apart: 7, of which 3 were waited for; matrix products, arithmetic and copies ran while one was open for 0% of the time, Pallas kernels for 4%

profile of v6, /device:TPU:0, one launch (start us, length us, event | category | flops | bytes accessed | tf_op | source)
XLA Modules:
  0.0 31.6 jit_solution(11251137011992785793)
XLA Ops:
  0.0 0.0 copy-start
  0.0 1.4 %pack_edges.1 = (f32[8,320]{1,0:T(8,128)S(1)}, f32[16,320]{1,0:T(8,128)S(1)}, f32[120,128]{1,0:T(8,128)S(1)}, f32[104,128]{1,0:T(8,128)S(1)}, f32[32,128]{1,0:T(...) custom-call(f32[256,128]{1,0:T(8,128)} %bitcast.12, ...), custom_call_target="tpu_custom_call" | custom-call | tf_op jit(solution)/shard_map/pack_edges/pallas_call | solution.py:391
  1.4 3.1 %collective-permute-start.3 = (f32[120,128]{1,0:T(8,128)S(1)}, f32[120,128]{1,0:T(8,128)S(1)}, u32[]{:S(2)}, u32[]{:S(2)}) collective-permute-start(f32[120,128]{1,0:T(8,128)S(1)} %get-tuple-element.25), channel_id=1, source_target_pairs={{0,4},{4,0},{8,12},{12,8},{1,5},{5,1},{9,13},{13,9},{2,6},{6,2},{1... | collective-permute-start | bytes 184328 | tf_op jit(solution)/shard_map/ppermute | solution.py:366
  4.5 0.7 %collective-permute-start.2 = (f32[104,128]{1,0:T(8,128)S(1)}, f32[104,128]{1,0:T(8,128)S(1)}, u32[]{:S(2)}, u32[]{:S(2)}) collective-permute-start(f32[104,128]{1,0:T(8,128)S(1)} %get-tuple-element.24), channel_id=1, source_target_pairs={{4,8},{8,4},{5,9},{9,5},{6,10},{10,6},{7,11},{11,7},{20,24},{24,20... | collective-permute-start | bytes 159752 | tf_op jit(solution)/shard_map/ppermute | solution.py:366
  5.2 0.7 %collective-permute-start = (f32[16,320]{1,0:T(8,128)S(1)}, f32[16,320]{1,0:T(8,128)S(1)}, u32[]{:S(2)}, u32[]{:S(2)}) collective-permute-start(f32[16,320]{1,0:T(8,128)S(1)} %get-tuple-element.23), channel_id=1, source_target_pairs={{1,2},{2,1},{5,6},{6,5},{9,10},{10,9},{13,14},{14,13},{17,18},{18,... | collective-permute-start | bytes 61448 | tf_op jit(solution)/shard_map/ppermute | solution.py:366
  5.9 4.3 %collective-permute-start.1 = (f32[8,320]{1,0:T(8,128)S(1)}, f32[8,320]{1,0:T(8,128)S(1)}, u32[]{:S(2)}, u32[]{:S(2)}) collective-permute-start(f32[8,320]{1,0:T(8,128)S(1)} %get-tuple-element.22.columns), channel_id=1, source_target_pairs={{0,1},{1,0},{2,3},{3,2},{4,5},{5,4},{6,7},{7,6},{8,9},{9,8},{10,11... | collective-permute-start | bytes 30728 | tf_op jit(solution)/shard_map/ppermute | solution.py:366
  10.2 0.0 collective-permute-done.3.lat_even
  10.2 0.0 copy-start.1
  10.2 0.0 copy-start.2
  10.2 0.0 copy-start.3
  10.2 3.9 %collective-permute-start.5 = (f32[16,128]{1,0:T(8,128)S(1)}, f32[16,128]{1,0:T(8,128)S(1)}, u32[]{:S(2)}, u32[]{:S(2)}) collective-permute-start(f32[16,128]{1,0:T(8,128)S(1)} %forward_masses.1), channel_id=1, source_target_pairs={{0,8},{4,12},{8,0},{12,4},{1,9},{5,13},{9,1},{13,5},{2,10},{6,14},... | collective-permute-start | bytes 24584 | tf_op jit(solution)/shard_map/ppermute | solution.py:416
  14.1 0.3 index_tables.1
  14.4 0.0 collective-permute-done.1.even_pairs
  14.4 0.0 collective-permute-done.odd_pairs
  14.4 0.0 collective-permute-done.2.lat_odd
  14.4 0.0 copy-done
  14.4 0.0 copy-done.1
  14.4 0.0 copy-done.2
  14.4 0.0 copy-done.3
  14.4 1.0 %advect_and_interpolate.1 = (f32[256,128]{1,0:T(8,128)S(1)}, f32[72,128]{1,0:T(8,128)S(1)}) custom-call(f32[256,128]{1,0:T(8,128)S(1)} %bitcast.13, f32[64,128]{1,0:T(8,128)S(1)} %bitcast.15, f32[64,128]{1,0:T(8,128)S(1)} %bitcast.17, f32[64,128]{1,0:T(8,128)S(1)} %bitcast.19, f32[8,320]{1,0:T(8,128)S(1)} %get-tuple-element.22.columns, ...), custom_call_target="tpu_custom_call" | custom-call | tf_op jit(solution)/shard_map/advect_and_interpolate/pallas_call | solution.py:439
  15.4 0.0 collective-permute-start.4
  15.5 0.3 collective-permute-done.5.forwarded
  15.7 0.3 collective-permute-start.6
  16.0 0.6 %collective-permute-done.4.given = f32[72,128]{1,0:T(8,128)S(1)} collective-permute-done((f32[72,128]{1,0:T(8,128)S(1)}, f32[72,128]{1,0:T(8,128)S(1)}, u32[]{:S(2)}, u32[]{:S(2)}) %collective-permute-start.4) | collective-permute-done | bytes 36896 | tf_op jit(solution)/shard_map/ppermute | solution.py:456
  16.7 0.3 collective-permute-done.6.given_masses
  16.9 0.1 margin_blocks.1
  17.1 13.4 %all_to_all.5 = f32[16,1,2176]{2,1,0:T(1,128)S(1)} all-to-all(f32[16,1,2176]{2,1,0:T(1,128)S(1)} %bitcast.11), channel_id=1, replica_groups=mesh['panel'=2,'lat'=4,'lon'=4] {'lat','lon'}, dimensions={0} | all-to-all | bytes 278528 | tf_op jit(solution)/shard_map/all_to_all | solution.py:463
  30.4 1.1 %fill_and_scale.1 = f32[1,4,8,8,128]{4,3,2,1,0:T(8,128)} custom-call(f32[256,128]{1,0:T(8,128)S(1)} %get-tuple-element.34.advected, f32[272,128]{1,0:T(8,128)S(1)} %bitcast.10, f32[8,256]{1,0:T(8,128)S(1)} %get-tuple-element.37.row_hit, bf16[128,256]{1,0:T(8,128)(2,1)S(1)} %get-tuple-element.38.column_hot), custom_call_target="tpu_custom_call" | custom-call | tf_op jit(solution)/shard_map/fill_and_scale/pallas_call | solution.py:466
  (2 shorter events, 0.0 us)
Async XLA Ops:
  0.0 14.4 %copy-start = (f32[1,4,8,8,128]{4,3,2,1,0:T(8,128)S(1)}, f32[1,4,8,8,128]{4,3,2,1,0:T(8,128)}, u32[]{:S(2)}) copy-start(f32[1,4,8,8,128]{4,3,2,1,0:T(8,128)} %param.8) | copy-start | bytes 393220
  1.4 8.7 %collective-permute-start.3 = (f32[120,128]{1,0:T(8,128)S(1)}, f32[120,128]{1,0:T(8,128)S(1)}, u32[]{:S(2)}, u32[]{:S(2)}) collective-permute-start(f32[120,128]{1,0:T(8,128)S(1)} %get-tuple-element.25), channel_id=1, source_target_pairs={{0,4},{4,0},{8,12},{12,8},{1,5},{5,1},{9,13},{13,9},{2,6},{6,2},{1... | collective-permute-start | bytes 184328 | tf_op jit(solution)/shard_map/ppermute | solution.py:366
  4.5 9.8 %collective-permute-start.2 = (f32[104,128]{1,0:T(8,128)S(1)}, f32[104,128]{1,0:T(8,128)S(1)}, u32[]{:S(2)}, u32[]{:S(2)}) collective-permute-start(f32[104,128]{1,0:T(8,128)S(1)} %get-tuple-element.24), channel_id=1, source_target_pairs={{4,8},{8,4},{5,9},{9,5},{6,10},{10,6},{7,11},{11,7},{20,24},{24,20... | collective-permute-start | bytes 159752 | tf_op jit(solution)/shard_map/ppermute | solution.py:366
  5.2 9.2 %collective-permute-start = (f32[16,320]{1,0:T(8,128)S(1)}, f32[16,320]{1,0:T(8,128)S(1)}, u32[]{:S(2)}, u32[]{:S(2)}) collective-permute-start(f32[16,320]{1,0:T(8,128)S(1)} %get-tuple-element.23), channel_id=1, source_target_pairs={{1,2},{2,1},{5,6},{6,5},{9,10},{10,9},{13,14},{14,13},{17,18},{18,... | collective-permute-start | bytes 61448 | tf_op jit(solution)/shard_map/ppermute | solution.py:366
  5.9 8.5 %collective-permute-start.1 = (f32[8,320]{1,0:T(8,128)S(1)}, f32[8,320]{1,0:T(8,128)S(1)}, u32[]{:S(2)}, u32[]{:S(2)}) collective-permute-start(f32[8,320]{1,0:T(8,128)S(1)} %get-tuple-element.22.columns), channel_id=1, source_target_pairs={{0,1},{1,0},{2,3},{3,2},{4,5},{5,4},{6,7},{7,6},{8,9},{9,8},{10,11... | collective-permute-start | bytes 30728 | tf_op jit(solution)/shard_map/ppermute | solution.py:366
  10.2 4.2 %copy-start.1 = (f32[1,8,8,128]{3,2,1,0:T(8,128)S(1)}, f32[1,8,8,128]{3,2,1,0:T(8,128)}, u32[]{:S(2)}) copy-start(f32[1,8,8,128]{3,2,1,0:T(8,128)} %param.9) | copy-start | bytes 98308
  10.2 4.2 %copy-start.2 = (f32[1,8,8,128]{3,2,1,0:T(8,128)S(1)}, f32[1,8,8,128]{3,2,1,0:T(8,128)}, u32[]{:S(2)}) copy-start(f32[1,8,8,128]{3,2,1,0:T(8,128)} %param.10) | copy-start | bytes 98308
  10.2 4.2 %copy-start.3 = (f32[1,8,8,128]{3,2,1,0:T(8,128)S(1)}, f32[1,8,8,128]{3,2,1,0:T(8,128)}, u32[]{:S(2)}) copy-start(f32[1,8,8,128]{3,2,1,0:T(8,128)} %param.11) | copy-start | bytes 98308
  10.2 5.5 %collective-permute-start.5 = (f32[16,128]{1,0:T(8,128)S(1)}, f32[16,128]{1,0:T(8,128)S(1)}, u32[]{:S(2)}, u32[]{:S(2)}) collective-permute-start(f32[16,128]{1,0:T(8,128)S(1)} %forward_masses.1), channel_id=1, source_target_pairs={{0,8},{4,12},{8,0},{12,4},{1,9},{5,13},{9,1},{13,5},{2,10},{6,14},... | collective-permute-start | bytes 24584 | tf_op jit(solution)/shard_map/ppermute | solution.py:416
  15.4 1.2 %collective-permute-start.4 = (f32[72,128]{1,0:T(8,128)S(1)}, f32[72,128]{1,0:T(8,128)S(1)}, u32[]{:S(2)}, u32[]{:S(2)}) collective-permute-start(f32[72,128]{1,0:T(8,128)S(1)} %get-tuple-element.35.own), channel_id=1, source_target_pairs={{0,16},{16,0},{1,17},{17,1},{2,18},{18,2},{3,19},{19,3},{4,20},{20... | collective-permute-start | bytes 110600 | tf_op jit(solution)/shard_map/ppermute | solution.py:456
  15.7 1.2 %collective-permute-start.6 = (f32[64,128]{1,0:T(8,128)S(1)}, f32[64,128]{1,0:T(8,128)S(1)}, u32[]{:S(2)}, u32[]{:S(2)}) collective-permute-start(f32[64,128]{1,0:T(8,128)S(1)} %gather_masses.1.own_masses), channel_id=1, source_target_pairs={{0,16},{16,0},{1,17},{17,1},{2,18},{18,2},{3,19},{19,3},{4,20},{20... | collective-permute-start | bytes 98312 | tf_op jit(solution)/shard_map/ppermute | solution.py:426

commit v7 on v6

--- a/solution.py
+++ b/solution.py
@@ -9,7 +9,7 @@
 from jax.sharding import PartitionSpec as P
 
 HALO = 3
-MASS_ROWS = 64
+FORWARD_ROWS = 68
 
 
 class Sizes(NamedTuple):
@@ -167,7 +167,10 @@
     levels = sizes.levels
     block = pl.multiple_of((lax.axis_index("lat") ^ 2) * levels, levels)
     forwarded[0:levels, :] = masses[pl.ds(block, levels), :]
-    forwarded[levels:, :] = lat_even[pl.ds(sizes.halo_rows + levels, levels), :]
+    forwarded[levels : 2 * levels, :] = lat_even[pl.ds(sizes.halo_rows + levels, levels), :]
+    spare = forwarded.shape[0] - 2 * levels
+    if spare:
+        forwarded[pl.ds(2 * levels, spare), :] = jnp.zeros((spare, sizes.width), jnp.float32)
 
 
 def masses_kernel(sizes, masses, lat_even, forwarded, received):
@@ -178,10 +181,8 @@
         masses[pl.ds(own, levels), :],
         lat_even[pl.ds(sizes.halo_rows, levels), :],
         forwarded[0:levels, :],
-        forwarded[levels:, :],
-    )
-    spare = received.shape[0] - len(pieces) * levels
-    received[pl.ds(len(pieces) * levels, spare), :] = jnp.zeros((spare, sizes.width), jnp.float32)
+        forwarded[levels : 2 * levels, :],
+    )
     for step, piece in enumerate(pieces):
         received[pl.ds(pl.multiple_of((here ^ step) * levels, levels), levels), :] = piece
 
@@ -203,7 +204,8 @@
 
 def main_kernel(
     sizes, field, zonal, meridional, mass, columns, odd_pairs, even_pairs, lat_odd, lat_even,
-    kept, row_weight, weight_high, weight_low, advected, outgoing, edge_rows, flux_rows,
+    kept, row_weight, weight_high, weight_low,
+    advected, outgoing, partial, edge_rows, flux_rows,
 ):
     tracers, levels, rows, width, blocks, capacity, _ = sizes
     fields, span, total = sizes.fields, levels * rows, sizes.fields * rows
@@ -242,7 +244,6 @@
     row = lax.broadcasted_iota(jnp.int32, (levels, rows, width), 1)
 
     weights = mass[...].reshape(levels, rows, width)
-    sums = blocks * sizes.margin_rows
     for tracer in range(tracers):
         part = pl.ds(tracer * span, span)
         cells = field[part, :]
@@ -293,54 +294,57 @@
             outgoing[
                 pl.ds(block * sizes.margin_rows + base, levels), lane : lane + capacity
             ] = payload[:, at : at + capacity]
-        outgoing[sums + tracer : sums + tracer + 1, :] = jnp.sum(
+        partial[tracer : tracer + 1, :] = jnp.sum(
             weights * remaining, axis=(0, 1)
         )[None]
-        outgoing[sums + tracers + tracer : sums + tracers + tracer + 1, :] = jnp.sum(
+        partial[tracers + tracer : tracers + tracer + 1, :] = jnp.sum(
             weights * cells3, axis=(0, 1)
         )[None]
 
 
-def blocks_kernel(sizes, own, given, own_masses, given_masses, lon_blocks):
+def blocks_kernel(sizes, own, given, partial, masses, all_blocks):
     tracers, levels, _, width, blocks, capacity, places = sizes
     size = sizes.margin_rows
-    sums = pl.ds(blocks * size, 2 * tracers)
+    half = size // 2
+    mine = lax.axis_index("panel")
     weighed = jnp.zeros((size, width), jnp.float32)
     for block in range(blocks):
         margin = given[pl.ds(block * size, size), :]
-        part = pl.ds(block * levels, levels)
-        for sent, mass in (
-            (margin, own_masses[part, :]),
-            (own[pl.ds(block * size, size), :], given_masses[part, :]),
-        ):
-            weighed = weighed + sent * jnp.concatenate([mass] * (size // levels), axis=0)
-        for place in range(places):
-            lon_blocks[pl.ds((block * places + place) * (size + 1), size), :] = margin
+        mass = masses[pl.ds(block * levels, levels), :]
+        weighed = weighed + margin * jnp.concatenate([mass] * (size // levels), axis=0)
+        made = own[pl.ds(block * size, half), :]
+        for panel, piece in ((mine, margin[half:]), (1 - mine, made)):
+            for place in range(places):
+                start = ((panel * blocks + block) * places + place) * (half + 1)
+                all_blocks[pl.ds(start, half), :] = piece
     column = lax.broadcasted_iota(jnp.int32, (1, width), 1)
-    partial = own[sums, :] + given[sums, :]
     added = []
     for tracer in range(tracers):
         base, lane = sizes.spot(tracer)
         row = jnp.sum(weighed[base : base + levels], axis=0, keepdims=True)
         added.append(jnp.where((column >= lane) & (column < lane + capacity), row, 0.0))
-    partial = partial + jnp.concatenate(
+    sums = partial[...] + jnp.concatenate(
         added + [jnp.zeros((tracers, width), jnp.float32)], axis=0
     )
-    totals = jnp.sum(partial, axis=1, keepdims=True)
+    totals = jnp.sum(sums, axis=1, keepdims=True)
     line = jnp.zeros((1, width), jnp.float32)
     for i in range(2 * tracers):
         line = jnp.where(column == i, totals[i : i + 1], line)
-    for block in range(blocks * places):
-        lon_blocks[pl.ds(block * (size + 1) + size, 1), :] = line
-
-
-def fill_kernel(sizes, advected, incoming, row_hit, column_hot, updated):
+    for block in range(2 * blocks * places):
+        all_blocks[pl.ds(block * (half + 1) + half, 1), :] = line
+
+
+def fill_kernel(sizes, advected, incoming, row_hit, column_hot, updated, stage, sems):
     tracers, levels, rows, width, blocks, capacity, places = sizes
-    size = sizes.margin_rows
-    place = lax.axis_index("lon")
+    half = sizes.margin_rows // 2
+    place, mine = lax.axis_index("lon"), lax.axis_index("panel")
     arrived = []
     for block in range(blocks):
-        piece = incoming[pl.ds((block * places + place) * (size + 1), size), :]
+        halves = []
+        for panel in (1 - mine, mine):
+            start = ((panel * blocks + block) * places + place) * (half + 1)
+            halves.append(incoming[pl.ds(start, half), :])
+        piece = jnp.concatenate(halves, axis=0)
         arrived.append(
             jnp.concatenate(
                 [piece[:, i * capacity : (i + 1) * capacity] for i in range(sizes.sides)], axis=0
@@ -348,15 +352,20 @@
         )
     arrived = jnp.concatenate(arrived, axis=1)
     line = jnp.sum(
-        incoming[pl.ds(size, blocks * places, stride=size + 1), :], axis=0, keepdims=True
-    )
+        incoming[pl.ds(half, 2 * blocks * places, stride=half + 1), :], axis=0, keepdims=True
+    )
+    copies = []
     for tracer in range(tracers):
         values = arrived[tracer * levels : (tracer + 1) * levels]
         spread = (values[:, None, :] * row_hit[...][None]).reshape(levels * rows, -1)
-        placed = sum(dot(part, column_hot[...], True) for part in three_parts(spread))
+        placed = sum(dot(part, column_hot[...], True) for part in two_parts(spread))
         old = advected[pl.ds(tracer * levels * rows, levels * rows), :]
         scale = line[:, tracers + tracer : tracers + tracer + 1] / line[:, tracer : tracer + 1]
-        updated[0, tracer] = ((old + placed) * scale).reshape(levels, rows, width)
+        stage[tracer] = ((old + placed) * scale).reshape(levels, rows, width)
+        copies.append(pltpu.make_async_copy(stage.at[tracer], updated.at[0, tracer], sems.at[tracer]))
+        copies[-1].start()
+    for copy in copies:
+        copy.wait()
 
 
 def exchanged(value, axis, first):
@@ -410,20 +419,19 @@
     if two_hops(sizes):
         forwarded = pl.pallas_call(
             functools.partial(forward_kernel, sizes),
-            out_shape=shape(2 * levels, width),
+            out_shape=shape(FORWARD_ROWS, width),
             name="forward_masses",
         )(*near(masses, lat_even))
         forwarded = lax.ppermute(forwarded, "lat", [(i, i ^ 2) for i in range(blocks)])
         masses = pl.pallas_call(
             functools.partial(masses_kernel, sizes),
-            out_shape=shape(MASS_ROWS, width),
+            out_shape=shape(blocks * levels, width),
             name="gather_masses",
         )(*near(masses, lat_even, forwarded))
     else:
         masses = lax.all_to_all(
             masses.reshape(blocks, levels, width), "lat", 0, 0, tiled=True
         ).reshape(blocks * levels, width)
-    given_masses = lax.ppermute(masses, "panel", [(0, 1), (1, 0)])
     kept, row_hit, column_hot, *weights = pl.pallas_call(
         functools.partial(tables_kernel, sizes),
         out_shape=(
@@ -436,11 +444,12 @@
         ),
         name="index_tables",
     )(*near(*index_copies))
-    advected, outgoing = pl.pallas_call(
+    advected, outgoing, partial = pl.pallas_call(
         functools.partial(main_kernel, sizes),
         out_shape=(
             shape(fields * rows, width),
-            shape(blocks * sizes.margin_rows + 2 * sizes.tracers, width),
+            shape(blocks * sizes.margin_rows, width),
+            shape(2 * sizes.tracers, width),
         ),
         scratch_shapes=[
             pltpu.VMEM((fields * rows, width), jnp.float32),
@@ -454,18 +463,23 @@
         )
     )
     given = lax.ppermute(outgoing, "panel", [(0, 1), (1, 0)])
-    block_rows = sizes.margin_rows + 1
-    lon_blocks = pl.pallas_call(
+    block_rows, devices = sizes.margin_rows // 2 + 1, 2 * blocks * places
+    all_blocks = pl.pallas_call(
         functools.partial(blocks_kernel, sizes),
-        out_shape=shape(blocks * places * block_rows, width),
+        out_shape=shape(devices * block_rows, width),
         name="margin_blocks",
-    )(*near(outgoing, given, masses, given_masses))
+    )(*near(outgoing, given, partial, masses))
     incoming = lax.all_to_all(
-        lon_blocks.reshape(blocks * places, 1, block_rows * width), ("lat", "lon"), 0, 0, tiled=True
-    ).reshape(blocks * places * block_rows, width)
+        all_blocks.reshape(devices, 1, block_rows * width), ("panel", "lat", "lon"), 0, 0, tiled=True
+    ).reshape(devices * block_rows, width)
     return pl.pallas_call(
         functools.partial(fill_kernel, sizes),
         out_shape=jax.ShapeDtypeStruct((1, sizes.tracers, levels, rows, width), jnp.float32),
+        out_specs=pl.BlockSpec(memory_space=pl.ANY),
+        scratch_shapes=[
+            pltpu.VMEM((sizes.tracers, levels, rows, width), jnp.float32),
+            pltpu.SemaphoreType.DMA((sizes.tracers,)),
+        ],
         name="fill_and_scale",
     )(*near(advected, incoming, row_hit, column_hot))
 

time: 31.8 us -> 30.1 us (0.947)
  blocking collectives: 13.4 us -> 12.1 us
    all_to_all x1, blocking collectives: 13.4 us -> 12.1 us  [body(): lax.all_to_all(all_blocks.reshape(devices, 1, block_rows * width), ('pane...]
  transfers between devices with their start and end apart: 7 -> 6, of which waited for: 3 -> 2; matrix products, arithmetic and copies ran while one was open for 0% -> 0% of each run, Pallas kernels for 4% -> 4%
where the time goes in v7:
time: 30.1 us; the launch traced here: 29.9 us
  starting transfers between devices  12.6 us (42%)
  blocking collectives  12.1 us (40%)
  Pallas kernels  3.81 us (13%)
  waiting for transfers between devices  1.2 us (4%)
    all_to_all x1, blocking collectives, body(): lax.all_to_all(all_blocks.reshape(devices, 1, block_rows * width), ('pane...  12.1 us
    ppermute x4, starting transfers between devices, exchanged(): return lax.ppermute(value, axis, pairs)  8.72 us
    ppermute x1, starting transfers between devices, body(): lax.ppermute(forwarded, 'lat', [(i, i ^ 2) for i in range(blocks)])  3.91 us
    pallas_call x1, Pallas kernels, body(): pl.pallas_call(functools.partial(pack_kernel, sizes), out_shape=(shape(8,...  1.41 us
    pallas_call x1, Pallas kernels, body(): pl.pallas_call(functools.partial(fill_kernel, sizes), out_shape=jax.Shape...  1.02 us
    pallas_call x1, Pallas kernels, body(): pl.pallas_call(functools.partial(main_kernel, sizes), out_shape=(shape(fi...  1 us
  transfers between devices with their start and end apart: 6, of which 2 were waited for; matrix products, arithmetic and copies ran while one was open for 0% of the time, Pallas kernels for 4%

profile of v7, /device:TPU:0, one launch (start us, length us, event | category | flops | bytes accessed | tf_op | source)
XLA Modules:
  0.0 29.9 jit_solution(2129381126164882536)
XLA Ops:
  0.0 0.0 copy-start.1
  0.0 0.0 copy-start.2
  0.0 0.0 copy-start.3
  0.0 1.4 %pack_edges.1 = (f32[8,320]{1,0:T(8,128)S(1)}, f32[16,320]{1,0:T(8,128)S(1)}, f32[120,128]{1,0:T(8,128)S(1)}, f32[104,128]{1,0:T(8,128)S(1)}, f32[32,128]{1,0:T(...) custom-call(f32[256,128]{1,0:T(8,128)} %bitcast.12, ...), custom_call_target="tpu_custom_call" | custom-call | tf_op jit(solution)/shard_map/pack_edges/pallas_call | solution.py:400
  1.4 0.0 copy-start
  1.4 3.1 %collective-permute-start.3 = (f32[120,128]{1,0:T(8,128)S(1)}, f32[120,128]{1,0:T(8,128)S(1)}, u32[]{:S(2)}, u32[]{:S(2)}) collective-permute-start(f32[120,128]{1,0:T(8,128)S(1)} %get-tuple-element.26), channel_id=1, source_target_pairs={{0,4},{4,0},{8,12},{12,8},{1,5},{5,1},{9,13},{13,9},{2,6},{6,2},{1... | collective-permute-start | bytes 184328 | tf_op jit(solution)/shard_map/ppermute | solution.py:375
  4.6 0.7 %collective-permute-start.2 = (f32[104,128]{1,0:T(8,128)S(1)}, f32[104,128]{1,0:T(8,128)S(1)}, u32[]{:S(2)}, u32[]{:S(2)}) collective-permute-start(f32[104,128]{1,0:T(8,128)S(1)} %get-tuple-element.25), channel_id=1, source_target_pairs={{4,8},{8,4},{5,9},{9,5},{6,10},{10,6},{7,11},{11,7},{20,24},{24,20... | collective-permute-start | bytes 159752 | tf_op jit(solution)/shard_map/ppermute | solution.py:375
  5.2 0.7 %collective-permute-start = (f32[16,320]{1,0:T(8,128)S(1)}, f32[16,320]{1,0:T(8,128)S(1)}, u32[]{:S(2)}, u32[]{:S(2)}) collective-permute-start(f32[16,320]{1,0:T(8,128)S(1)} %get-tuple-element.24), channel_id=1, source_target_pairs={{1,2},{2,1},{5,6},{6,5},{9,10},{10,9},{13,14},{14,13},{17,18},{18,... | collective-permute-start | bytes 61448 | tf_op jit(solution)/shard_map/ppermute | solution.py:375
  5.9 4.3 %collective-permute-start.1 = (f32[8,320]{1,0:T(8,128)S(1)}, f32[8,320]{1,0:T(8,128)S(1)}, u32[]{:S(2)}, u32[]{:S(2)}) collective-permute-start(f32[8,320]{1,0:T(8,128)S(1)} %get-tuple-element.23.columns), channel_id=1, source_target_pairs={{0,1},{1,0},{2,3},{3,2},{4,5},{5,4},{6,7},{7,6},{8,9},{9,8},{10,11... | collective-permute-start | bytes 30728 | tf_op jit(solution)/shard_map/ppermute | solution.py:375
  10.2 0.0 collective-permute-done.3.lat_even
  10.2 3.9 %collective-permute-start.5 = (f32[68,128]{1,0:T(8,128)S(1)}, f32[68,128]{1,0:T(8,128)S(1)}, u32[]{:S(2)}, u32[]{:S(2)}) collective-permute-start(f32[68,128]{1,0:T(8,128)S(1)} %forward_masses.1), channel_id=1, source_target_pairs={{0,8},{4,12},{8,0},{12,4},{1,9},{5,13},{9,1},{13,5},{2,10},{6,14},... | collective-permute-start | bytes 104456 | tf_op jit(solution)/shard_map/ppermute | solution.py:425
  14.1 0.3 index_tables.1
  14.3 0.0 collective-permute-done.1.even_pairs
  14.3 0.0 collective-permute-done.odd_pairs
  14.4 0.0 collective-permute-done.2.lat_odd
  14.4 0.0 copy-done.1
  14.4 0.0 copy-done.2
  14.4 0.0 copy-done.3
  14.4 0.0 copy-done
  14.4 1.0 %advect_and_interpolate.1 = (f32[256,128]{1,0:T(8,128)S(1)}, f32[64,128]{1,0:T(8,128)S(1)}, f32[8,128]{1,0:T(8,128)S(1)}) custom-call(f32[256,128]{1,0:T(8,128)S(1)} %bitcast.13, f32[64,128]{1,0:T(8,128)S(1)} %bitcast.15, f32[64,128]{1,0:T(8,128)S(1)} %bitcast.17, f32[64,128]{1,0:T(8,128)S(1)} %bitcast.19, f32[8,320]{1,0:T(8,128)S(1)} %get-tuple-element.23.columns, ...), custom_call_target="tpu_custom_call" | custom-call | tf_op jit(solution)/shard_map/advect_and_interpolate/pallas_call | solution.py:447
  15.4 0.0 collective-permute-start.4
  15.4 0.6 %collective-permute-done.5.forwarded = f32[68,128]{1,0:T(8,128)S(1)} collective-permute-done((f32[68,128]{1,0:T(8,128)S(1)}, f32[68,128]{1,0:T(8,128)S(1)}, u32[]{:S(2)}, u32[]{:S(2)}) %collective-permute-start.5) | collective-permute-done | bytes 34848 | tf_op jit(solution)/shard_map/ppermute | solution.py:425
  16.0 0.6 %collective-permute-done.4.given = f32[64,128]{1,0:T(8,128)S(1)} collective-permute-done((f32[64,128]{1,0:T(8,128)S(1)}, f32[64,128]{1,0:T(8,128)S(1)}, u32[]{:S(2)}, u32[]{:S(2)}) %collective-permute-start.4) | collective-permute-done | bytes 32800 | tf_op jit(solution)/shard_map/ppermute | solution.py:465
  16.6 0.1 margin_blocks.1
  16.7 12.1 %all_to_all.5 = f32[32,1,1152]{2,1,0:T(1,128)S(1)} all-to-all(f32[32,1,1152]{2,1,0:T(1,128)S(1)} %bitcast.10), channel_id=1, replica_groups=mesh['panel'=2,'lat'=4,'lon'=4] {'panel','lat','lon'}, dimensions={0} | all-to-all | bytes 294912 | tf_op jit(solution)/shard_map/all_to_all | solution.py:472
  28.9 1.0 %fill_and_scale.1 = f32[1,4,8,8,128]{4,3,2,1,0:T(8,128)} custom-call(f32[256,128]{1,0:T(8,128)S(1)} %get-tuple-element.35.advected, f32[288,128]{1,0:T(8,128)S(1)} %bitcast.11, f32[8,256]{1,0:T(8,128)S(1)} %get-tuple-element.39.row_hit, bf16[128,256]{1,0:T(8,128)(2,1)S(1)} %get-tuple-element.40.column_hot), custom_call_target="tpu_custom_call" | custom-call | tf_op jit(solution)/shard_map/fill_and_scale/pallas_call | solution.py:475
  (2 shorter events, 0.0 us)
Async XLA Ops:
  0.0 14.4 %copy-start.1 = (f32[1,8,8,128]{3,2,1,0:T(8,128)S(1)}, f32[1,8,8,128]{3,2,1,0:T(8,128)}, u32[]{:S(2)}) copy-start(f32[1,8,8,128]{3,2,1,0:T(8,128)} %param.9) | copy-start | bytes 98308
  0.0 14.4 %copy-start.2 = (f32[1,8,8,128]{3,2,1,0:T(8,128)S(1)}, f32[1,8,8,128]{3,2,1,0:T(8,128)}, u32[]{:S(2)}) copy-start(f32[1,8,8,128]{3,2,1,0:T(8,128)} %param.10) | copy-start | bytes 98308
  0.0 14.4 %copy-start.3 = (f32[1,8,8,128]{3,2,1,0:T(8,128)S(1)}, f32[1,8,8,128]{3,2,1,0:T(8,128)}, u32[]{:S(2)}) copy-start(f32[1,8,8,128]{3,2,1,0:T(8,128)} %param.11) | copy-start | bytes 98308
  1.4 13.0 %copy-start = (f32[1,4,8,8,128]{4,3,2,1,0:T(8,128)S(1)}, f32[1,4,8,8,128]{4,3,2,1,0:T(8,128)}, u32[]{:S(2)}) copy-start(f32[1,4,8,8,128]{4,3,2,1,0:T(8,128)} %param.8) | copy-start | bytes 393220
  1.4 8.7 %collective-permute-start.3 = (f32[120,128]{1,0:T(8,128)S(1)}, f32[120,128]{1,0:T(8,128)S(1)}, u32[]{:S(2)}, u32[]{:S(2)}) collective-permute-start(f32[120,128]{1,0:T(8,128)S(1)} %get-tuple-element.26), channel_id=1, source_target_pairs={{0,4},{4,0},{8,12},{12,8},{1,5},{5,1},{9,13},{13,9},{2,6},{6,2},{1... | collective-permute-start | bytes 184328 | tf_op jit(solution)/shard_map/ppermute | solution.py:375
  4.6 9.8 %collective-permute-start.2 = (f32[104,128]{1,0:T(8,128)S(1)}, f32[104,128]{1,0:T(8,128)S(1)}, u32[]{:S(2)}, u32[]{:S(2)}) collective-permute-start(f32[104,128]{1,0:T(8,128)S(1)} %get-tuple-element.25), channel_id=1, source_target_pairs={{4,8},{8,4},{5,9},{9,5},{6,10},{10,6},{7,11},{11,7},{20,24},{24,20... | collective-permute-start | bytes 159752 | tf_op jit(solution)/shard_map/ppermute | solution.py:375
  5.2 9.1 %collective-permute-start = (f32[16,320]{1,0:T(8,128)S(1)}, f32[16,320]{1,0:T(8,128)S(1)}, u32[]{:S(2)}, u32[]{:S(2)}) collective-permute-start(f32[16,320]{1,0:T(8,128)S(1)} %get-tuple-element.24), channel_id=1, source_target_pairs={{1,2},{2,1},{5,6},{6,5},{9,10},{10,9},{13,14},{14,13},{17,18},{18,... | collective-permute-start | bytes 61448 | tf_op jit(solution)/shard_map/ppermute | solution.py:375
  5.9 8.5 %collective-permute-start.1 = (f32[8,320]{1,0:T(8,128)S(1)}, f32[8,320]{1,0:T(8,128)S(1)}, u32[]{:S(2)}, u32[]{:S(2)}) collective-permute-start(f32[8,320]{1,0:T(8,128)S(1)} %get-tuple-element.23.columns), channel_id=1, source_target_pairs={{0,1},{1,0},{2,3},{3,2},{4,5},{5,4},{6,7},{7,6},{8,9},{9,8},{10,11... | collective-permute-start | bytes 30728 | tf_op jit(solution)/shard_map/ppermute | solution.py:375
  10.2 5.8 %collective-permute-start.5 = (f32[68,128]{1,0:T(8,128)S(1)}, f32[68,128]{1,0:T(8,128)S(1)}, u32[]{:S(2)}, u32[]{:S(2)}) collective-permute-start(f32[68,128]{1,0:T(8,128)S(1)} %forward_masses.1), channel_id=1, source_target_pairs={{0,8},{4,12},{8,0},{12,4},{1,9},{5,13},{9,1},{13,5},{2,10},{6,14},... | collective-permute-start | bytes 104456 | tf_op jit(solution)/shard_map/ppermute | solution.py:425
  15.4 1.2 %collective-permute-start.4 = (f32[64,128]{1,0:T(8,128)S(1)}, f32[64,128]{1,0:T(8,128)S(1)}, u32[]{:S(2)}, u32[]{:S(2)}) collective-permute-start(f32[64,128]{1,0:T(8,128)S(1)} %get-tuple-element.36.own), channel_id=1, source_target_pairs={{0,16},{16,0},{1,17},{17,1},{2,18},{18,2},{3,19},{19,3},{4,20},{20... | collective-permute-start | bytes 98312 | tf_op jit(solution)/shard_map/ppermute | solution.py:465

commit v8 on v7

--- a/solution.py
+++ b/solution.py
@@ -9,6 +9,7 @@
 from jax.sharding import PartitionSpec as P
 
 HALO = 3
+COLUMN_ROWS = 48
 FORWARD_ROWS = 68
 
 
@@ -110,7 +111,7 @@
 
 def pack_kernel(
     sizes, field, zonal, meridional, mass, target, live, donor, fraction,
-    columns, columns_odd, lat_even, lat_odd, masses, *index_copies,
+    columns, lat_even, lat_odd, masses, *index_copies,
 ):
     _, levels, rows, width, blocks, capacity, _ = sizes
     fields = sizes.fields
@@ -153,10 +154,10 @@
         axis=0,
     )
     columns[...] = edges
-    columns_odd[0 : columns.shape[0]] = edges
-    columns_odd[columns.shape[0] :] = jnp.zeros(
-        (columns_odd.shape[0] - columns.shape[0], columns.shape[1]), jnp.float32
-    )
+
+
+def relay_kernel(columns, relayed):
+    relayed[...] = columns[0 : relayed.shape[0], :]
 
 
 def two_hops(sizes):
@@ -209,9 +210,12 @@
 ):
     tracers, levels, rows, width, blocks, capacity, _ = sizes
     fields, span, total = sizes.fields, levels * rows, sizes.fields * rows
-    even = lax.rem(lax.axis_index("lon"), 2) == 0
-    from_west = jnp.where(even, odd_pairs[0:HALO], even_pairs[0:HALO])
-    from_east = jnp.where(even, even_pairs[HALO : 2 * HALO], odd_pairs[HALO : 2 * HALO])
+    place = lax.axis_index("lon")
+    even = lax.rem(place, 2) == 0
+    inner = (place > 0) & (place < sizes.places - 1)
+    second = jnp.where(inner, odd_pairs[...], 0.0)
+    from_west = jnp.where(even, second[0:HALO], even_pairs[0:HALO])
+    from_east = jnp.where(even, even_pairs[HALO : 2 * HALO], second[HALO : 2 * HALO])
     east_cells = [from_east[i : i + 1, :total] for i in range(HALO)]
     own_cells = [columns[i : i + 1, :total] for i in range(HALO)]
     east_number = jnp.concatenate([from_east[0:1, total:]] * tracers, axis=1)
@@ -397,11 +401,10 @@
         return (pltpu.with_memory_space_constraint(value, pltpu.VMEM) for value in values)
 
     slots = blocks * capacity
-    columns, columns_odd, lat_even, lat_odd, masses, *index_copies = pl.pallas_call(
+    columns, lat_even, lat_odd, masses, *index_copies = pl.pallas_call(
         functools.partial(pack_kernel, sizes),
         out_shape=(
-            shape(8, (fields + levels) * rows),
-            shape(16, (fields + levels) * rows),
+            shape(COLUMN_ROWS, (fields + levels) * rows),
             shape(sizes.halo_rows + (2 * levels if two_hops(sizes) else 0), width),
             shape(sizes.halo_rows, width),
             shape(blocks * levels, width),
@@ -413,9 +416,17 @@
         name="pack_edges",
     )(field, zonal, meridional, mass, target, live, donor, fraction)
     lat_even = exchanged(lat_even, "lat", 0)
-    odd_pairs = exchanged(columns_odd, "lon", 1)
     lat_odd = exchanged(lat_odd, "lat", 1)
     even_pairs = exchanged(columns, "lon", 0)
+    if places == 4:
+        relayed = pl.pallas_call(
+            relay_kernel,
+            out_shape=shape(8, even_pairs.shape[1]),
+            name="relay_columns",
+        )(*near(even_pairs))
+        odd_pairs = lax.ppermute(relayed, "lon", [(i, i ^ 2) for i in range(places)])
+    else:
+        odd_pairs = exchanged(columns, "lon", 1)
     if two_hops(sizes):
         forwarded = pl.pallas_call(
             functools.partial(forward_kernel, sizes),

time: 30.1 us -> 28.3 us (0.940)
  starting transfers between devices: 12.6 us -> 10.7 us
    ppermute x4 -> x3, starting transfers between devices: 8.72 us -> 5.23 us  [exchanged(): return lax.ppermute(value, axis, pairs)]
    ppermute x0 -> x1, starting transfers between devices: none -> 2.05 us  [body(): lax.ppermute(relayed, 'lon', [(i, i ^ 2) for i in range(places)])]
    ppermute x1, starting transfers between devices: 3.91 us -> 3.37 us  [body(): lax.ppermute(forwarded, 'lat', [(i, i ^ 2) for i in range(blocks)])]
    pallas_call x1 -> x2, Pallas kernels: 1.41 us -> 1.36 us  [the longest x1 1.36 us: body(): pl.pallas_call(functools.partial(pack_kernel, sizes), out_shape=(shape(CO...]
  transfers between devices with their start and end apart: 6 -> 6, of which waited for: 2 -> 3; matrix products, arithmetic and copies ran while one was open for 0% -> 0% of each run, Pallas kernels for 4% -> 5%
where the time goes in v8:
time: 28.3 us; the launch traced here: 28.1 us
  blocking collectives  12.3 us (43%)
  starting transfers between devices  10.7 us (38%)
  Pallas kernels  3.77 us (13%)
  waiting for transfers between devices  1.29 us (5%)
    all_to_all x1, blocking collectives, body(): lax.all_to_all(all_blocks.reshape(devices, 1, block_rows * width), ('pane...  12.3 us
    ppermute x3, starting transfers between devices, exchanged(): return lax.ppermute(value, axis, pairs)  5.23 us
    ppermute x1, starting transfers between devices, body(): lax.ppermute(forwarded, 'lat', [(i, i ^ 2) for i in range(blocks)])  3.37 us
    ppermute x1, starting transfers between devices, body(): lax.ppermute(relayed, 'lon', [(i, i ^ 2) for i in range(places)])  2.05 us
    pallas_call x1, Pallas kernels, body(): pl.pallas_call(functools.partial(pack_kernel, sizes), out_shape=(shape(CO...  1.36 us
    pallas_call x1, Pallas kernels, body(): pl.pallas_call(functools.partial(fill_kernel, sizes), out_shape=jax.Shape...  1.02 us
    pallas_call x1, Pallas kernels, body(): pl.pallas_call(functools.partial(main_kernel, sizes), out_shape=(shape(fi...  1 us
    ppermute x1, waiting for transfers between devices, body(): lax.ppermute(forwarded, 'lat', [(i, i ^ 2) for i in range(blocks)])  0.61 us
  transfers between devices with their start and end apart: 6, of which 3 were waited for; matrix products, arithmetic and copies ran while one was open for 0% of the time, Pallas kernels for 5%

profile of v8, /device:TPU:0, one launch (start us, length us, event | category | flops | bytes accessed | tf_op | source)
XLA Modules:
  0.0 28.1 jit_solution(11434278199827232773)
XLA Ops:
  0.0 1.4 %pack_edges.1 = (f32[48,320]{1,0:T(8,128)S(1)}, f32[120,128]{1,0:T(8,128)S(1)}, f32[104,128]{1,0:T(8,128)S(1)}, f32[32,128]{1,0:T(8,128)S(1)}, s32[4,64]{1,0:T(4...) custom-call(f32[256,128]{1,0:T(8,128)} %bitcast.12, f32[64,128]{1,0:T(8,128)} %bitcast.14, ...), custom_call_target="tpu_custom_call" | custom-call | tf_op jit(solution)/shard_map/pack_edges/pallas_call | solution.py:404
  1.4 0.0 copy-start
  1.4 3.0 %collective-permute-start = (f32[48,320]{1,0:T(8,128)S(1)}, f32[48,320]{1,0:T(8,128)S(1)}, u32[]{:S(2)}, u32[]{:S(2)}) collective-permute-start(f32[48,320]{1,0:T(8,128)S(1)} %get-tuple-element.22.columns), channel_id=1, source_target_pairs={{0,1},{1,0},{2,3},{3,2},{4,5},{5,4},{6,7},{7,6},{8,9},{9,8},{10,11... | collective-permute-start | bytes 184328 | tf_op jit(solution)/shard_map/ppermute | solution.py:379
  4.4 1.6 %collective-permute-start.3 = (f32[120,128]{1,0:T(8,128)S(1)}, f32[120,128]{1,0:T(8,128)S(1)}, u32[]{:S(2)}, u32[]{:S(2)}) collective-permute-start(f32[120,128]{1,0:T(8,128)S(1)} %get-tuple-element.24), channel_id=1, source_target_pairs={{0,4},{4,0},{8,12},{12,8},{1,5},{5,1},{9,13},{13,9},{2,6},{6,2},{1... | collective-permute-start | bytes 184328 | tf_op jit(solution)/shard_map/ppermute | solution.py:379
  6.0 0.7 %collective-permute-start.2 = (f32[104,128]{1,0:T(8,128)S(1)}, f32[104,128]{1,0:T(8,128)S(1)}, u32[]{:S(2)}, u32[]{:S(2)}) collective-permute-start(f32[104,128]{1,0:T(8,128)S(1)} %get-tuple-element.23), channel_id=1, source_target_pairs={{4,8},{8,4},{5,9},{9,5},{6,10},{10,6},{7,11},{11,7},{20,24},{24,20... | collective-permute-start | bytes 159752 | tf_op jit(solution)/shard_map/ppermute | solution.py:379
  6.6 0.1 collective-permute-done.columns.even_pairs
  6.7 2.0 %collective-permute-start.1 = (f32[8,320]{1,0:T(8,128)S(1)}, f32[8,320]{1,0:T(8,128)S(1)}, u32[]{:S(2)}, u32[]{:S(2)}) collective-permute-start(f32[8,320]{1,0:T(8,128)S(1)} %relay_columns.1), channel_id=1, source_target_pairs={{0,2},{1,3},{2,0},{3,1},{4,6},{5,7},{6,4},{7,5},{8,10},{9,11},{10,... | collective-permute-start | bytes 30728 | tf_op jit(solution)/shard_map/ppermute | solution.py:427
  8.8 0.0 collective-permute-done.3.lat_even
  8.8 0.0 copy-start.1
  8.8 0.0 copy-start.2
  8.8 0.0 copy-start.3
  8.8 3.4 %collective-permute-start.5 = (f32[68,128]{1,0:T(8,128)S(1)}, f32[68,128]{1,0:T(8,128)S(1)}, u32[]{:S(2)}, u32[]{:S(2)}) collective-permute-start(f32[68,128]{1,0:T(8,128)S(1)} %forward_masses.1), channel_id=1, source_target_pairs={{0,8},{4,12},{8,0},{12,4},{1,9},{5,13},{9,1},{13,5},{2,10},{6,14},... | collective-permute-start | bytes 104456 | tf_op jit(solution)/shard_map/ppermute | solution.py:436
  12.2 0.3 index_tables.1
  12.4 0.0 collective-permute-done.2.lat_odd
  12.4 0.0 collective-permute-done.1.odd_pairs
  12.4 0.0 copy-done
  12.5 0.0 copy-done.1
  12.5 0.0 copy-done.2
  12.5 0.0 copy-done.3
  12.5 1.0 %advect_and_interpolate.1 = (f32[256,128]{1,0:T(8,128)S(1)}, f32[64,128]{1,0:T(8,128)S(1)}, f32[8,128]{1,0:T(8,128)S(1)}) custom-call(f32[256,128]{1,0:T(8,128)S(1)} %bitcast.13, f32[64,128]{1,0:T(8,128)S(1)} %bitcast.15, f32[64,128]{1,0:T(8,128)S(1)} %bitcast.17, f32[64,128]{1,0:T(8,128)S(1)} %bitcast.19, f32[48,320]{1,0:T(8,128)S(1)} %get-tuple-element.22.columns, ...), custom_call_target="tpu_custom_call" | custom-call | tf_op jit(solution)/shard_map/advect_and_interpolate/pallas_call | solution.py:458
  13.5 0.0 collective-permute-start.4
  13.5 0.6 %collective-permute-done.5.forwarded = f32[68,128]{1,0:T(8,128)S(1)} collective-permute-done((f32[68,128]{1,0:T(8,128)S(1)}, f32[68,128]{1,0:T(8,128)S(1)}, u32[]{:S(2)}, u32[]{:S(2)}) %collective-permute-start.5) | collective-permute-done | bytes 34848 | tf_op jit(solution)/shard_map/ppermute | solution.py:436
  14.1 0.6 %collective-permute-done.4.given = f32[64,128]{1,0:T(8,128)S(1)} collective-permute-done((f32[64,128]{1,0:T(8,128)S(1)}, f32[64,128]{1,0:T(8,128)S(1)}, u32[]{:S(2)}, u32[]{:S(2)}) %collective-permute-start.4) | collective-permute-done | bytes 32800 | tf_op jit(solution)/shard_map/ppermute | solution.py:476
  14.7 0.1 margin_blocks.1
  14.8 12.3 %all_to_all.5 = f32[32,1,1152]{2,1,0:T(1,128)S(1)} all-to-all(f32[32,1,1152]{2,1,0:T(1,128)S(1)} %bitcast.10), channel_id=1, replica_groups=mesh['panel'=2,'lat'=4,'lon'=4] {'panel','lat','lon'}, dimensions={0} | all-to-all | bytes 294912 | tf_op jit(solution)/shard_map/all_to_all | solution.py:483
  27.1 1.0 %fill_and_scale.1 = f32[1,4,8,8,128]{4,3,2,1,0:T(8,128)} custom-call(f32[256,128]{1,0:T(8,128)S(1)} %get-tuple-element.33.advected, f32[288,128]{1,0:T(8,128)S(1)} %bitcast.11, f32[8,256]{1,0:T(8,128)S(1)} %get-tuple-element.37.row_hit, bf16[128,256]{1,0:T(8,128)(2,1)S(1)} %get-tuple-element.38.column_hot), custom_call_target="tpu_custom_call" | custom-call | tf_op jit(solution)/shard_map/fill_and_scale/pallas_call | solution.py:486
  (3 shorter events, 0.0 us)
Async XLA Ops:
  1.4 11.1 %copy-start = (f32[1,4,8,8,128]{4,3,2,1,0:T(8,128)S(1)}, f32[1,4,8,8,128]{4,3,2,1,0:T(8,128)}, u32[]{:S(2)}) copy-start(f32[1,4,8,8,128]{4,3,2,1,0:T(8,128)} %param.8) | copy-start | bytes 393220
  1.4 5.3 %collective-permute-start = (f32[48,320]{1,0:T(8,128)S(1)}, f32[48,320]{1,0:T(8,128)S(1)}, u32[]{:S(2)}, u32[]{:S(2)}) collective-permute-start(f32[48,320]{1,0:T(8,128)S(1)} %get-tuple-element.22.columns), channel_id=1, source_target_pairs={{0,1},{1,0},{2,3},{3,2},{4,5},{5,4},{6,7},{7,6},{8,9},{9,8},{10,11... | collective-permute-start | bytes 184328 | tf_op jit(solution)/shard_map/ppermute | solution.py:379
  4.4 4.4 %collective-permute-start.3 = (f32[120,128]{1,0:T(8,128)S(1)}, f32[120,128]{1,0:T(8,128)S(1)}, u32[]{:S(2)}, u32[]{:S(2)}) collective-permute-start(f32[120,128]{1,0:T(8,128)S(1)} %get-tuple-element.24), channel_id=1, source_target_pairs={{0,4},{4,0},{8,12},{12,8},{1,5},{5,1},{9,13},{13,9},{2,6},{6,2},{1... | collective-permute-start | bytes 184328 | tf_op jit(solution)/shard_map/ppermute | solution.py:379
  6.0 6.5 %collective-permute-start.2 = (f32[104,128]{1,0:T(8,128)S(1)}, f32[104,128]{1,0:T(8,128)S(1)}, u32[]{:S(2)}, u32[]{:S(2)}) collective-permute-start(f32[104,128]{1,0:T(8,128)S(1)} %get-tuple-element.23), channel_id=1, source_target_pairs={{4,8},{8,4},{5,9},{9,5},{6,10},{10,6},{7,11},{11,7},{20,24},{24,20... | collective-permute-start | bytes 159752 | tf_op jit(solution)/shard_map/ppermute | solution.py:379
  6.7 5.7 %collective-permute-start.1 = (f32[8,320]{1,0:T(8,128)S(1)}, f32[8,320]{1,0:T(8,128)S(1)}, u32[]{:S(2)}, u32[]{:S(2)}) collective-permute-start(f32[8,320]{1,0:T(8,128)S(1)} %relay_columns.1), channel_id=1, source_target_pairs={{0,2},{1,3},{2,0},{3,1},{4,6},{5,7},{6,4},{7,5},{8,10},{9,11},{10,... | collective-permute-start | bytes 30728 | tf_op jit(solution)/shard_map/ppermute | solution.py:427
  8.8 3.7 %copy-start.1 = (f32[1,8,8,128]{3,2,1,0:T(8,128)S(1)}, f32[1,8,8,128]{3,2,1,0:T(8,128)}, u32[]{:S(2)}) copy-start(f32[1,8,8,128]{3,2,1,0:T(8,128)} %param.9) | copy-start | bytes 98308
  8.8 3.7 %copy-start.2 = (f32[1,8,8,128]{3,2,1,0:T(8,128)S(1)}, f32[1,8,8,128]{3,2,1,0:T(8,128)}, u32[]{:S(2)}) copy-start(f32[1,8,8,128]{3,2,1,0:T(8,128)} %param.10) | copy-start | bytes 98308
  8.8 3.7 %copy-start.3 = (f32[1,8,8,128]{3,2,1,0:T(8,128)S(1)}, f32[1,8,8,128]{3,2,1,0:T(8,128)}, u32[]{:S(2)}) copy-start(f32[1,8,8,128]{3,2,1,0:T(8,128)} %param.11) | copy-start | bytes 98308
  8.8 5.3 %collective-permute-start.5 = (f32[68,128]{1,0:T(8,128)S(1)}, f32[68,128]{1,0:T(8,128)S(1)}, u32[]{:S(2)}, u32[]{:S(2)}) collective-permute-start(f32[68,128]{1,0:T(8,128)S(1)} %forward_masses.1), channel_id=1, source_target_pairs={{0,8},{4,12},{8,0},{12,4},{1,9},{5,13},{9,1},{13,5},{2,10},{6,14},... | collective-permute-start | bytes 104456 | tf_op jit(solution)/shard_map/ppermute | solution.py:436
  13.5 1.2 %collective-permute-start.4 = (f32[64,128]{1,0:T(8,128)S(1)}, f32[64,128]{1,0:T(8,128)S(1)}, u32[]{:S(2)}, u32[]{:S(2)}) collective-permute-start(f32[64,128]{1,0:T(8,128)S(1)} %get-tuple-element.34.own), channel_id=1, source_target_pairs={{0,16},{16,0},{1,17},{17,1},{2,18},{18,2},{3,19},{19,3},{4,20},{20... | collective-permute-start | bytes 98312 | tf_op jit(solution)/shard_map/ppermute | solution.py:476

commit v9 on v8

--- a/solution.py
+++ b/solution.py
@@ -9,8 +9,8 @@
 from jax.sharding import PartitionSpec as P
 
 HALO = 3
-COLUMN_ROWS = 48
-FORWARD_ROWS = 68
+COLUMN_ROWS = 44
+FORWARD_ROWS = 36
 
 
 class Sizes(NamedTuple):
@@ -79,6 +79,12 @@
     )
 
 
+def dot_parts(parts, right, transposed=False):
+    rows = parts[0].shape[0]
+    product = dot(jnp.concatenate(parts, axis=0), right, transposed)
+    return sum(product[i * rows : (i + 1) * rows] for i in range(len(parts)))
+
+
 def cubic_weights(fraction):
     return (
         -fraction * (fraction - 1.0) * (fraction - 2.0) / 6.0,
@@ -111,7 +117,7 @@
 
 def pack_kernel(
     sizes, field, zonal, meridional, mass, target, live, donor, fraction,
-    columns, lat_even, lat_odd, masses, *index_copies,
+    columns, sides, lat_even, lat_odd, masses, *index_copies,
 ):
     _, levels, rows, width, blocks, capacity, _ = sizes
     fields = sizes.fields
@@ -131,7 +137,7 @@
     spots = row_of(target[...])
     row_hot = one_hot(spots // width, rows)
     column_hot = one_hot(lax.rem(spots, width), width).astype(jnp.bfloat16)
-    picked = sum(dot(part, column_hot) for part in three_parts(mass[...]))
+    picked = dot_parts(three_parts(mass[...]), column_hot)
     picked = jnp.sum(
         picked.reshape(levels, rows, spots.shape[1]) * row_hot[None], axis=1
     ) * live_row(live[...], capacity)
@@ -154,6 +160,8 @@
         axis=0,
     )
     columns[...] = edges
+    sides[0 : 2 * HALO] = turned[0 : 2 * HALO]
+    sides[2 * HALO : 4 * HALO] = turned[width - 2 * HALO : width]
 
 
 def relay_kernel(columns, relayed):
@@ -203,10 +211,24 @@
     )
 
 
+def zonal_kernel(sizes, field, zonal, moved):
+    tracers, levels, rows, width, *_ = sizes
+    span = levels * rows
+    for tracer in range(tracers):
+        part = pl.ds(tracer * span, span)
+        cells = field[part, :]
+        along = [
+            pltpu.roll(cells, shift % width, 1) if shift else cells
+            for shift in (3, 2, 1, 0, -1, -2)
+        ]
+        flux = face_flux(along, zonal[...])
+        moved[part, :] = cells - (pltpu.roll(flux, width - 1, 1) - flux)
+
+
 def main_kernel(
-    sizes, field, zonal, meridional, mass, columns, odd_pairs, even_pairs, lat_odd, lat_even,
-    kept, row_weight, weight_high, weight_low,
-    advected, outgoing, partial, edge_rows, flux_rows,
+    sizes, field, moved, meridional, sides, odd_pairs, even_pairs, lat_odd, lat_even,
+    row_weight, weight_high, weight_low,
+    advected, first_half, second_half, edge_rows, flux_rows,
 ):
     tracers, levels, rows, width, blocks, capacity, _ = sizes
     fields, span, total = sizes.fields, levels * rows, sizes.fields * rows
@@ -216,16 +238,25 @@
     second = jnp.where(inner, odd_pairs[...], 0.0)
     from_west = jnp.where(even, second[0:HALO], even_pairs[0:HALO])
     from_east = jnp.where(even, even_pairs[HALO : 2 * HALO], second[HALO : 2 * HALO])
-    east_cells = [from_east[i : i + 1, :total] for i in range(HALO)]
-    own_cells = [columns[i : i + 1, :total] for i in range(HALO)]
-    east_number = jnp.concatenate([from_east[0:1, total:]] * tracers, axis=1)
-    east_flux = face_flux(own_cells + east_cells, east_number)
+    west = jnp.concatenate([from_west, sides[0 : 2 * HALO]], axis=0)
+    east = jnp.concatenate([sides[2 * HALO : 4 * HALO], from_east], axis=0)
+    faces = HALO + 1
+    number = jnp.concatenate(
+        [west[HALO : HALO + faces, total:], east[HALO : HALO + faces, total:]], axis=0
+    )
+    flux = face_flux(
+        [
+            jnp.concatenate([west[i : i + faces, :total], east[i : i + faces, :total]], axis=0)
+            for i in range(2 * HALO)
+        ],
+        jnp.concatenate([number] * tracers, axis=1),
+    )
+    change = flux[1:] - flux[:-1]
     lanes = jnp.concatenate(
         [
-            *east_cells,
-            east_flux,
-            jnp.zeros((width - 2 * HALO - 1, total), jnp.float32),
-            from_west[0:HALO, :total],
+            sides[0:HALO, :total] - change[0:HALO],
+            jnp.zeros((width - 2 * HALO, total), jnp.float32),
+            sides[3 * HALO : 4 * HALO, :total] - change[faces : faces + HALO],
         ],
         axis=0,
     ).T
@@ -247,28 +278,14 @@
     column = lax.broadcasted_iota(jnp.int32, (span, width), 1)
     row = lax.broadcasted_iota(jnp.int32, (levels, rows, width), 1)
 
-    weights = mass[...].reshape(levels, rows, width)
     for tracer in range(tracers):
         part = pl.ds(tracer * span, span)
         cells = field[part, :]
-        halo = lanes[tracer * span : (tracer + 1) * span]
-        along = []
-        for shift in (3, 2, 1, 0, -1, -2):
-            if shift > 0:
-                along.append(
-                    pltpu.roll(jnp.where(column >= width - shift, halo, cells), shift, 1)
-                )
-            elif shift < 0:
-                along.append(
-                    pltpu.roll(jnp.where(column < -shift, halo, cells), width + shift, 1)
-                )
-            else:
-                along.append(cells)
-        flux = face_flux(along, zonal[...])
-        next_flux = pltpu.roll(
-            jnp.where(column == 0, halo[:, HALO : HALO + 1], flux), width - 1, 1
+        result = jnp.where(
+            (column < HALO) | (column >= width - HALO),
+            lanes[tracer * span : (tracer + 1) * span],
+            moved[part, :],
         )
-        result = cells - (next_flux - flux)
         cells3 = cells.reshape(levels, rows, width)
         halo3 = edge_rows[part, :].reshape(levels, rows, width)
         along = []
@@ -284,43 +301,53 @@
         next_flux = pltpu.roll(jnp.where(row == 0, edge3, flux), rows - 1, 1)
         result = result.reshape(levels, rows, width) - (next_flux - flux)
         flat = result.reshape(span, width)
-        remaining = result * kept[...][None]
-        advected[part, :] = remaining.reshape(span, width)
-
-        high, low = two_parts(flat)
-        across = dot(high, weight_high[...]) + (
-            dot(high, weight_low[...]) + dot(low, weight_high[...])
-        )
-        payload = jnp.sum(across.reshape(levels, rows, -1) * row_weight[...][None], axis=1)
+        advected[part, :] = flat
+    high, low = two_parts(advected[...])
+    across = dot_parts((high, low), weight_high[...]) + dot(high, weight_low[...])
+    payloads = jnp.sum(across.reshape(fields, rows, -1) * row_weight[...][None], axis=1)
+    for tracer in range(tracers):
+        payload = payloads[tracer * levels : (tracer + 1) * levels]
         base, lane = sizes.spot(tracer)
+        half = sizes.margin_rows // 2
+        outgoing = (first_half, second_half)[base // half]
         for block in range(blocks):
             at = block * capacity
-            outgoing[
-                pl.ds(block * sizes.margin_rows + base, levels), lane : lane + capacity
-            ] = payload[:, at : at + capacity]
-        partial[tracer : tracer + 1, :] = jnp.sum(
-            weights * remaining, axis=(0, 1)
+            outgoing[pl.ds(block * half + base % half, levels), lane : lane + capacity] = payload[
+                :, at : at + capacity
+            ]
+
+
+def sums_kernel(sizes, field, mass, advected, kept, remaining, partial):
+    tracers, levels, rows, width, *_ = sizes
+    span = levels * rows
+    weights = mass[...].reshape(levels, rows, width)
+    for tracer in range(tracers):
+        part = pl.ds(tracer * span, span)
+        held = advected[part, :].reshape(levels, rows, width) * kept[...][None]
+        remaining[part, :] = held.reshape(span, width)
+        before = field[part, :].reshape(levels, rows, width)
+        partial[tracer : tracer + 1, :] = jnp.sum(weights * held, axis=(0, 1))[None]
+        partial[tracers + tracer : tracers + tracer + 1, :] = jnp.sum(
+            weights * before, axis=(0, 1)
         )[None]
-        partial[tracers + tracer : tracers + tracer + 1, :] = jnp.sum(
-            weights * cells3, axis=(0, 1)
-        )[None]
-
-
-def blocks_kernel(sizes, own, given, partial, masses, all_blocks):
+
+
+def blocks_kernel(sizes, own, given_first, given_second, partial, masses, all_blocks):
     tracers, levels, _, width, blocks, capacity, places = sizes
-    size = sizes.margin_rows
-    half = size // 2
+    half = sizes.margin_rows // 2
     mine = lax.axis_index("panel")
-    weighed = jnp.zeros((size, width), jnp.float32)
+    weighed = [jnp.zeros((half, width), jnp.float32) for _ in range(2)]
     for block in range(blocks):
-        margin = given[pl.ds(block * size, size), :]
+        part = pl.ds(block * half, half)
         mass = masses[pl.ds(block * levels, levels), :]
-        weighed = weighed + margin * jnp.concatenate([mass] * (size // levels), axis=0)
-        made = own[pl.ds(block * size, half), :]
-        for panel, piece in ((mine, margin[half:]), (1 - mine, made)):
+        mass = jnp.concatenate([mass] * (half // levels), axis=0)
+        margins = (given_first[part, :], given_second[part, :])
+        weighed = [total + margin * mass for total, margin in zip(weighed, margins, strict=True)]
+        for panel, piece in ((mine, margins[1]), (1 - mine, own[part, :])):
             for place in range(places):
                 start = ((panel * blocks + block) * places + place) * (half + 1)
                 all_blocks[pl.ds(start, half), :] = piece
+    weighed = jnp.concatenate(weighed, axis=0)
     column = lax.broadcasted_iota(jnp.int32, (1, width), 1)
     added = []
     for tracer in range(tracers):
@@ -358,11 +385,11 @@
     line = jnp.sum(
         incoming[pl.ds(half, 2 * blocks * places, stride=half + 1), :], axis=0, keepdims=True
     )
+    spread = (arrived[:, None, :] * row_hit[...][None]).reshape(sizes.fields * rows, -1)
+    filled = dot_parts(two_parts(spread), column_hot[...], True)
     copies = []
     for tracer in range(tracers):
-        values = arrived[tracer * levels : (tracer + 1) * levels]
-        spread = (values[:, None, :] * row_hit[...][None]).reshape(levels * rows, -1)
-        placed = sum(dot(part, column_hot[...], True) for part in two_parts(spread))
+        placed = filled[tracer * levels * rows : (tracer + 1) * levels * rows]
         old = advected[pl.ds(tracer * levels * rows, levels * rows), :]
         scale = line[:, tracers + tracer : tracers + tracer + 1] / line[:, tracer : tracer + 1]
         stage[tracer] = ((old + placed) * scale).reshape(levels, rows, width)
@@ -401,10 +428,11 @@
         return (pltpu.with_memory_space_constraint(value, pltpu.VMEM) for value in values)
 
     slots = blocks * capacity
-    columns, lat_even, lat_odd, masses, *index_copies = pl.pallas_call(
+    columns, sides, lat_even, lat_odd, masses, *index_copies = pl.pallas_call(
         functools.partial(pack_kernel, sizes),
         out_shape=(
             shape(COLUMN_ROWS, (fields + levels) * rows),
+            shape(4 * HALO, (fields + levels) * rows),
             shape(sizes.halo_rows + (2 * levels if two_hops(sizes) else 0), width),
             shape(sizes.halo_rows, width),
             shape(blocks * levels, width),
@@ -455,12 +483,17 @@
         ),
         name="index_tables",
     )(*near(*index_copies))
-    advected, outgoing, partial = pl.pallas_call(
+    moved = pl.pallas_call(
+        functools.partial(zonal_kernel, sizes),
+        out_shape=shape(fields * rows, width),
+        name="own_zonal",
+    )(*near(field, zonal))
+    advected, first_half, second_half = pl.pallas_call(
         functools.partial(main_kernel, sizes),
         out_shape=(
             shape(fields * rows, width),
-            shape(blocks * sizes.margin_rows, width),
-            shape(2 * sizes.tracers, width),
+            shape(blocks * sizes.margin_rows // 2, width),
+            shape(blocks * sizes.margin_rows // 2, width),
         ),
         scratch_shapes=[
             pltpu.VMEM((fields * rows, width), jnp.float32),
@@ -469,17 +502,23 @@
         name="advect_and_interpolate",
     )(
         *near(
-            field, zonal, meridional, mass, columns, odd_pairs, even_pairs, lat_odd, lat_even,
-            kept, *weights,
+            field, moved, meridional, sides, odd_pairs, even_pairs, lat_odd, lat_even,
+            *weights,
         )
     )
-    given = lax.ppermute(outgoing, "panel", [(0, 1), (1, 0)])
+    given_first = lax.ppermute(first_half, "panel", [(0, 1), (1, 0)])
+    given_second = lax.ppermute(second_half, "panel", [(0, 1), (1, 0)])
+    remaining, partial = pl.pallas_call(
+        functools.partial(sums_kernel, sizes),
+        out_shape=(shape(fields * rows, width), shape(2 * sizes.tracers, width)),
+        name="kept_and_sums",
+    )(*near(field, mass, advected, kept))
     block_rows, devices = sizes.margin_rows // 2 + 1, 2 * blocks * places
     all_blocks = pl.pallas_call(
         functools.partial(blocks_kernel, sizes),
         out_shape=shape(devices * block_rows, width),
         name="margin_blocks",
-    )(*near(outgoing, given, partial, masses))
+    )(*near(first_half, given_first, given_second, partial, masses))
     incoming = lax.all_to_all(
         all_blocks.reshape(devices, 1, block_rows * width), ("panel", "lat", "lon"), 0, 0, tiled=True
     ).reshape(devices * block_rows, width)
@@ -492,7 +531,7 @@
             pltpu.SemaphoreType.DMA((sizes.tracers,)),
         ],
         name="fill_and_scale",
-    )(*near(advected, incoming, row_hit, column_hot))
+    )(*near(remaining, incoming, row_hit, column_hot))
 
 
 def solution(mesh):

time: 28.3 us -> 28.1 us (level)
  starting transfers between devices: 10.7 us -> 11.2 us
  waiting for transfers between devices: 1.29 us -> 0.87 us
  blocking collectives: 12.3 us -> 11.9 us
    ppermute x1, waiting for transfers between devices: 0.61 us -> 0.01 us  [body(): lax.ppermute(forwarded, 'lat', [(i, i ^ 2) for i in range(blocks)])]
    ppermute x1 -> x2, starting transfers between devices: 0.01 us -> 0.53 us  [the longest x1 0.5 us: body(): given_first = lax.ppermute(first_half, 'panel', [(0, 1), (1, 0)])]
    pallas_call x0 -> x2, Pallas kernels: none -> 0.5 us  [the longest x1 0.46 us: body(): pl.pallas_call(functools.partial(zonal_kernel, sizes), out_shape=shape(fi...]
    all_to_all x1, blocking collectives: 12.3 us -> 11.9 us  [body(): lax.all_to_all(all_blocks.reshape(devices, 1, block_rows * width), ('pane...]
    pallas_call x1, Pallas kernels: 1 us -> 0.6 us  [body(): pl.pallas_call(functools.partial(main_kernel, sizes), out_shape=(shape(fi...]
    ppermute x1 -> x2, waiting for transfers between devices: 0.58 us -> 0.76 us  [the longest x1 0.59 us: body(): given_second = lax.ppermute(second_half, 'panel', [(0, 1), (1, 0)])]
  transfers between devices with their start and end apart: 6 -> 7, of which waited for: 3 -> 3; matrix products, arithmetic and copies ran while one was open for 0% -> 0% of each run, Pallas kernels for 5% -> 5%
where the time goes in v9:
time: 28.1 us; the launch traced here: 27.9 us
  blocking collectives  11.9 us (42%)
  starting transfers between devices  11.2 us (40%)
  Pallas kernels  3.86 us (14%)
  waiting for transfers between devices  0.87 us (3%)
    all_to_all x1, blocking collectives, body(): lax.all_to_all(all_blocks.reshape(devices, 1, block_rows * width), ('pane...  11.9 us
    ppermute x3, starting transfers between devices, exchanged(): return lax.ppermute(value, axis, pairs)  5.23 us
    ppermute x1, starting transfers between devices, body(): lax.ppermute(forwarded, 'lat', [(i, i ^ 2) for i in range(blocks)])  3.37 us
    ppermute x1, starting transfers between devices, body(): lax.ppermute(relayed, 'lon', [(i, i ^ 2) for i in range(places)])  2.05 us
    pallas_call x1, Pallas kernels, body(): pl.pallas_call(functools.partial(pack_kernel, sizes), out_shape=(shape(CO...  1.39 us
    pallas_call x1, Pallas kernels, body(): pl.pallas_call(functools.partial(fill_kernel, sizes), out_shape=jax.Shape...  0.97 us
    pallas_call x1, Pallas kernels, body(): pl.pallas_call(functools.partial(main_kernel, sizes), out_shape=(shape(fi...  0.6 us
    ppermute x1, waiting for transfers between devices, body(): given_second = lax.ppermute(second_half, 'panel', [(0, 1), (1, 0)])  0.59 us
  transfers between devices with their start and end apart: 7, of which 3 were waited for; matrix products, arithmetic and copies ran while one was open for 0% of the time, Pallas kernels for 5%

profile of v9, /device:TPU:0, one launch (start us, length us, event | category | flops | bytes accessed | tf_op | source)
XLA Modules:
  0.0 27.9 jit_solution(14235740597955346210)
XLA Ops:
  0.0 1.4 %pack_edges.1 = (f32[44,320]{1,0:T(8,128)S(1)}, f32[12,320]{1,0:T(8,128)S(1)}, f32[120,128]{1,0:T(8,128)S(1)}, f32[104,128]{1,0:T(8,128)S(1)}, f32[32,128]{1,0:T...) custom-call(f32[256,128]{1,0:T(8,128)} %bitcast.10, ...), custom_call_target="tpu_custom_call" | custom-call | tf_op jit(solution)/shard_map/pack_edges/pallas_call | solution.py:431
  1.4 0.0 copy-start
  1.4 3.0 %collective-permute-start = (f32[44,320]{1,0:T(8,128)S(1)}, f32[44,320]{1,0:T(8,128)S(1)}, u32[]{:S(2)}, u32[]{:S(2)}) collective-permute-start(f32[44,320]{1,0:T(8,128)S(1)} %get-tuple-element.26), channel_id=1, source_target_pairs={{0,1},{1,0},{2,3},{3,2},{4,5},{5,4},{6,7},{7,6},{8,9},{9,8},{10,11... | collective-permute-start | bytes 168968 | tf_op jit(solution)/shard_map/ppermute | solution.py:406
  4.4 1.6 %collective-permute-start.3 = (f32[120,128]{1,0:T(8,128)S(1)}, f32[120,128]{1,0:T(8,128)S(1)}, u32[]{:S(2)}, u32[]{:S(2)}) collective-permute-start(f32[120,128]{1,0:T(8,128)S(1)} %get-tuple-element.28), channel_id=1, source_target_pairs={{0,4},{4,0},{8,12},{12,8},{1,5},{5,1},{9,13},{13,9},{2,6},{6,2},{1... | collective-permute-start | bytes 184328 | tf_op jit(solution)/shard_map/ppermute | solution.py:406
  6.0 0.7 %collective-permute-start.2 = (f32[104,128]{1,0:T(8,128)S(1)}, f32[104,128]{1,0:T(8,128)S(1)}, u32[]{:S(2)}, u32[]{:S(2)}) collective-permute-start(f32[104,128]{1,0:T(8,128)S(1)} %get-tuple-element.27), channel_id=1, source_target_pairs={{4,8},{8,4},{5,9},{9,5},{6,10},{10,6},{7,11},{11,7},{20,24},{24,20... | collective-permute-start | bytes 159752 | tf_op jit(solution)/shard_map/ppermute | solution.py:406
  6.7 0.1 collective-permute-done.columns.even_pairs
  6.8 2.0 %collective-permute-start.1 = (f32[8,320]{1,0:T(8,128)S(1)}, f32[8,320]{1,0:T(8,128)S(1)}, u32[]{:S(2)}, u32[]{:S(2)}) collective-permute-start(f32[8,320]{1,0:T(8,128)S(1)} %relay_columns.1), channel_id=1, source_target_pairs={{0,2},{1,3},{2,0},{3,1},{4,6},{5,7},{6,4},{7,5},{8,10},{9,11},{10,... | collective-permute-start | bytes 30728 | tf_op jit(solution)/shard_map/ppermute | solution.py:455
  8.8 0.0 collective-permute-done.3.lat_even
  8.8 0.0 copy-start.1
  8.8 3.4 %collective-permute-start.6 = (f32[36,128]{1,0:T(8,128)S(1)}, f32[36,128]{1,0:T(8,128)S(1)}, u32[]{:S(2)}, u32[]{:S(2)}) collective-permute-start(f32[36,128]{1,0:T(8,128)S(1)} %forward_masses.1), channel_id=1, source_target_pairs={{0,8},{4,12},{8,0},{12,4},{1,9},{5,13},{9,1},{13,5},{2,10},{6,14},... | collective-permute-start | bytes 55304 | tf_op jit(solution)/shard_map/ppermute | solution.py:464
  12.2 0.0 copy-done
  12.2 0.0 copy-done.1
  12.2 0.0 copy-start.2
  12.2 0.5 %own_zonal.1.moved = f32[256,128]{1,0:T(8,128)S(1)} custom-call(f32[256,128]{1,0:T(8,128)S(1)} %bitcast.11, f32[64,128]{1,0:T(8,128)S(1)} %bitcast.17), custom_call_target="tpu_custom_call" | custom-call | tf_op jit(solution)/shard_map/own_zonal/pallas_call | solution.py:486
  12.7 0.3 index_tables.1
  12.9 0.0 collective-permute-done.2.lat_odd
  12.9 0.0 collective-permute-done.1.odd_pairs
  12.9 0.0 copy-done.2
  12.9 0.0 copy-start.3
  12.9 0.6 %advect_and_interpolate.1 = (f32[256,128]{1,0:T(8,128)S(1)}, f32[32,128]{1,0:T(8,128)S(1)}, f32[32,128]{1,0:T(8,128)S(1)}) custom-call(f32[256,128]{1,0:T(8,128)S(1)} %bitcast.12, f32[256,128]{1,0:T(8,128)S(1)} %own_zonal.1.moved, f32[64,128]{1,0:T(8,128)S(1)} %bitcast.19, f32[12,320]{1,0:T(8,128)S(1)} %get-tuple-element.25.sides, ...), custom_call_target="tpu_custom_call" | custom-call | tf_op jit(solution)/shard_map/advect_and_interpolate/pallas_call | solution.py:491
  13.6 0.0 collective-permute-start.5
  13.6 0.5 %collective-permute-start.4 = (f32[32,128]{1,0:T(8,128)S(1)}, f32[32,128]{1,0:T(8,128)S(1)}, u32[]{:S(2)}, u32[]{:S(2)}) collective-permute-start(f32[32,128]{1,0:T(8,128)S(1)} %get-tuple-element.39.own), channel_id=1, source_target_pairs={{0,16},{16,0},{1,17},{17,1},{2,18},{18,2},{3,19},{19,3},{4,20},{20... | collective-permute-start | bytes 49160 | tf_op jit(solution)/shard_map/ppermute | solution.py:509
  14.1 0.0 copy-done.3
  14.1 0.0 collective-permute-done.6.forwarded
  14.2 0.6 %collective-permute-done.5.given_second = f32[32,128]{1,0:T(8,128)S(1)} collective-permute-done((f32[32,128]{1,0:T(8,128)S(1)}, f32[32,128]{1,0:T(8,128)S(1)}, u32[]{:S(2)}, u32[]{:S(2)}) %collective-permute-start.5) | collective-permute-done | bytes 16416 | tf_op jit(solution)/shard_map/ppermute | solution.py:510
  14.8 0.2 collective-permute-done.4.given_first
  14.9 0.1 margin_blocks.1
  15.0 11.9 %all_to_all.5 = f32[32,1,1152]{2,1,0:T(1,128)S(1)} all-to-all(f32[32,1,1152]{2,1,0:T(1,128)S(1)} %bitcast.14), channel_id=1, replica_groups=mesh['panel'=2,'lat'=4,'lon'=4] {'panel','lat','lon'}, dimensions={0} | all-to-all | bytes 294912 | tf_op jit(solution)/shard_map/all_to_all | solution.py:522
  26.9 1.0 %fill_and_scale.1 = f32[1,4,8,8,128]{4,3,2,1,0:T(8,128)} custom-call(f32[256,128]{1,0:T(8,128)S(1)} %get-tuple-element.38.advected, f32[288,128]{1,0:T(8,128)S(1)} %bitcast.15, f32[8,256]{1,0:T(8,128)S(1)} %get-tuple-element.43.row_hit, bf16[128,256]{1,0:T(8,128)(2,1)S(1)} %get-tuple-element.44.column_hot), custom_call_target="tpu_custom_call" | custom-call | tf_op jit(solution)/shard_map/fill_and_scale/pallas_call | solution.py:525
  (4 shorter events, 0.1 us)
Async XLA Ops:
  1.4 10.8 %copy-start = (f32[1,4,8,8,128]{4,3,2,1,0:T(8,128)S(1)}, f32[1,4,8,8,128]{4,3,2,1,0:T(8,128)}, u32[]{:S(2)}) copy-start(f32[1,4,8,8,128]{4,3,2,1,0:T(8,128)} %param.8) | copy-start | bytes 393220
  1.4 5.3 %collective-permute-start = (f32[44,320]{1,0:T(8,128)S(1)}, f32[44,320]{1,0:T(8,128)S(1)}, u32[]{:S(2)}, u32[]{:S(2)}) collective-permute-start(f32[44,320]{1,0:T(8,128)S(1)} %get-tuple-element.26), channel_id=1, source_target_pairs={{0,1},{1,0},{2,3},{3,2},{4,5},{5,4},{6,7},{7,6},{8,9},{9,8},{10,11... | collective-permute-start | bytes 168968 | tf_op jit(solution)/shard_map/ppermute | solution.py:406
  4.4 4.4 %collective-permute-start.3 = (f32[120,128]{1,0:T(8,128)S(1)}, f32[120,128]{1,0:T(8,128)S(1)}, u32[]{:S(2)}, u32[]{:S(2)}) collective-permute-start(f32[120,128]{1,0:T(8,128)S(1)} %get-tuple-element.28), channel_id=1, source_target_pairs={{0,4},{4,0},{8,12},{12,8},{1,5},{5,1},{9,13},{13,9},{2,6},{6,2},{1... | collective-permute-start | bytes 184328 | tf_op jit(solution)/shard_map/ppermute | solution.py:406
  6.0 6.9 %collective-permute-start.2 = (f32[104,128]{1,0:T(8,128)S(1)}, f32[104,128]{1,0:T(8,128)S(1)}, u32[]{:S(2)}, u32[]{:S(2)}) collective-permute-start(f32[104,128]{1,0:T(8,128)S(1)} %get-tuple-element.27), channel_id=1, source_target_pairs={{4,8},{8,4},{5,9},{9,5},{6,10},{10,6},{7,11},{11,7},{20,24},{24,20... | collective-permute-start | bytes 159752 | tf_op jit(solution)/shard_map/ppermute | solution.py:406
  6.8 6.2 %collective-permute-start.1 = (f32[8,320]{1,0:T(8,128)S(1)}, f32[8,320]{1,0:T(8,128)S(1)}, u32[]{:S(2)}, u32[]{:S(2)}) collective-permute-start(f32[8,320]{1,0:T(8,128)S(1)} %relay_columns.1), channel_id=1, source_target_pairs={{0,2},{1,3},{2,0},{3,1},{4,6},{5,7},{6,4},{7,5},{8,10},{9,11},{10,... | collective-permute-start | bytes 30728 | tf_op jit(solution)/shard_map/ppermute | solution.py:455
  8.8 3.4 %copy-start.1 = (f32[1,8,8,128]{3,2,1,0:T(8,128)S(1)}, f32[1,8,8,128]{3,2,1,0:T(8,128)}, u32[]{:S(2)}) copy-start(f32[1,8,8,128]{3,2,1,0:T(8,128)} %param.9) | copy-start | bytes 98308
  8.8 5.3 %collective-permute-start.6 = (f32[36,128]{1,0:T(8,128)S(1)}, f32[36,128]{1,0:T(8,128)S(1)}, u32[]{:S(2)}, u32[]{:S(2)}) collective-permute-start(f32[36,128]{1,0:T(8,128)S(1)} %forward_masses.1), channel_id=1, source_target_pairs={{0,8},{4,12},{8,0},{12,4},{1,9},{5,13},{9,1},{13,5},{2,10},{6,14},... | collective-permute-start | bytes 55304 | tf_op jit(solution)/shard_map/ppermute | solution.py:464
  12.2 0.8 %copy-start.2 = (f32[1,8,8,128]{3,2,1,0:T(8,128)S(1)}, f32[1,8,8,128]{3,2,1,0:T(8,128)}, u32[]{:S(2)}) copy-start(f32[1,8,8,128]{3,2,1,0:T(8,128)} %param.10) | copy-start | bytes 98308
  12.9 1.1 %copy-start.3 = (f32[1,8,8,128]{3,2,1,0:T(8,128)S(1)}, f32[1,8,8,128]{3,2,1,0:T(8,128)}, u32[]{:S(2)}) copy-start(f32[1,8,8,128]{3,2,1,0:T(8,128)} %param.11) | copy-start | bytes 98308
  13.6 1.2 %collective-permute-start.5 = (f32[32,128]{1,0:T(8,128)S(1)}, f32[32,128]{1,0:T(8,128)S(1)}, u32[]{:S(2)}, u32[]{:S(2)}) collective-permute-start(f32[32,128]{1,0:T(8,128)S(1)} %get-tuple-element.40), channel_id=1, source_target_pairs={{0,16},{16,0},{1,17},{17,1},{2,18},{18,2},{3,19},{19,3},{4,20},{20... | collective-permute-start | bytes 49160 | tf_op jit(solution)/shard_map/ppermute | solution.py:510
  13.6 1.3 %collective-permute-start.4 = (f32[32,128]{1,0:T(8,128)S(1)}, f32[32,128]{1,0:T(8,128)S(1)}, u32[]{:S(2)}, u32[]{:S(2)}) collective-permute-start(f32[32,128]{1,0:T(8,128)S(1)} %get-tuple-element.39.own), channel_id=1, source_target_pairs={{0,16},{16,0},{1,17},{17,1},{2,18},{18,2},{3,19},{19,3},{4,20},{20... | collective-permute-start | bytes 49160 | tf_op jit(solution)/shard_map/ppermute | solution.py:509

commit v10 on v9

--- a/solution.py
+++ b/solution.py
@@ -9,7 +9,7 @@
 from jax.sharding import PartitionSpec as P
 
 HALO = 3
-COLUMN_ROWS = 44
+COLUMN_ROWS = 104
 FORWARD_ROWS = 36
 
 
@@ -37,6 +37,10 @@
     @property
     def halo_rows(self):
         return HALO * self.fields + self.levels
+
+    @property
+    def chunks(self):
+        return -(-(self.fields + self.levels) * self.rows // self.width)
 
     def spot(self, tracer):
         start = tracer * self.levels
@@ -155,11 +159,16 @@
         [
             turned[width - HALO : width],
             turned[0:HALO],
-            jnp.zeros((columns.shape[0] - 2 * HALO, columns.shape[1]), jnp.float32),
+            jnp.zeros((8 - 2 * HALO, turned.shape[1]), jnp.float32),
         ],
         axis=0,
     )
-    columns[...] = edges
+    spare = jnp.zeros((8, sizes.chunks * width - edges.shape[1]), jnp.float32)
+    edges = jnp.concatenate([edges, spare], axis=1)
+    for i in range(sizes.chunks):
+        columns[pl.ds(8 * i, 8), :] = edges[:, i * width : (i + 1) * width]
+    start = 8 * sizes.chunks
+    columns[start:, :] = jnp.zeros((columns.shape[0] - start, width), jnp.float32)
     sides[0 : 2 * HALO] = turned[0 : 2 * HALO]
     sides[2 * HALO : 4 * HALO] = turned[width - 2 * HALO : width]
 
@@ -211,6 +220,11 @@
     )
 
 
+def unfold(sizes, rows):
+    chunks = [rows[pl.ds(8 * i, 8), :] for i in range(sizes.chunks)]
+    return jnp.concatenate(chunks, axis=1)[:, : (sizes.fields + sizes.levels) * sizes.rows]
+
+
 def zonal_kernel(sizes, field, zonal, moved):
     tracers, levels, rows, width, *_ = sizes
     span = levels * rows
@@ -235,9 +249,10 @@
     place = lax.axis_index("lon")
     even = lax.rem(place, 2) == 0
     inner = (place > 0) & (place < sizes.places - 1)
-    second = jnp.where(inner, odd_pairs[...], 0.0)
-    from_west = jnp.where(even, second[0:HALO], even_pairs[0:HALO])
-    from_east = jnp.where(even, even_pairs[HALO : 2 * HALO], second[HALO : 2 * HALO])
+    first, second = unfold(sizes, even_pairs), unfold(sizes, odd_pairs)
+    second = jnp.where(inner, second, 0.0)
+    from_west = jnp.where(even, second[0:HALO], first[0:HALO])
+    from_east = jnp.where(even, first[HALO : 2 * HALO], second[HALO : 2 * HALO])
     west = jnp.concatenate([from_west, sides[0 : 2 * HALO]], axis=0)
     east = jnp.concatenate([sides[2 * HALO : 4 * HALO], from_east], axis=0)
     faces = HALO + 1
@@ -431,7 +446,7 @@
     columns, sides, lat_even, lat_odd, masses, *index_copies = pl.pallas_call(
         functools.partial(pack_kernel, sizes),
         out_shape=(
-            shape(COLUMN_ROWS, (fields + levels) * rows),
+            shape(max(COLUMN_ROWS, 8 * sizes.chunks), width),
             shape(4 * HALO, (fields + levels) * rows),
             shape(sizes.halo_rows + (2 * levels if two_hops(sizes) else 0), width),
             shape(sizes.halo_rows, width),
@@ -449,7 +464,7 @@
     if places == 4:
         relayed = pl.pallas_call(
             relay_kernel,
-            out_shape=shape(8, even_pairs.shape[1]),
+            out_shape=shape(8 * sizes.chunks, width),
             name="relay_columns",
         )(*near(even_pairs))
         odd_pairs = lax.ppermute(relayed, "lon", [(i, i ^ 2) for i in range(places)])

time: 28.1 us -> 27.9 us (level)
  blocking collectives: 11.9 us -> 11.6 us
where the time goes in v10:
time: 27.9 us; the launch traced here: 27.6 us
  blocking collectives  11.6 us (42%)
  starting transfers between devices  11.2 us (40%)
  Pallas kernels  3.84 us (14%)
  waiting for transfers between devices  0.83 us (3%)
    all_to_all x1, blocking collectives, body(): lax.all_to_all(all_blocks.reshape(devices, 1, block_rows * width), ('pane...  11.6 us
    ppermute x3, starting transfers between devices, exchanged(): return lax.ppermute(value, axis, pairs)  5.23 us
    ppermute x1, starting transfers between devices, body(): lax.ppermute(forwarded, 'lat', [(i, i ^ 2) for i in range(blocks)])  3.54 us
    ppermute x1, starting transfers between devices, body(): lax.ppermute(relayed, 'lon', [(i, i ^ 2) for i in range(places)])  1.91 us
    pallas_call x1, Pallas kernels, body(): pl.pallas_call(functools.partial(pack_kernel, sizes), out_shape=(shape(ma...  1.38 us
    pallas_call x1, Pallas kernels, body(): pl.pallas_call(functools.partial(fill_kernel, sizes), out_shape=jax.Shape...  0.97 us
    pallas_call x1, Pallas kernels, body(): pl.pallas_call(functools.partial(main_kernel, sizes), out_shape=(shape(fi...  0.6 us
    ppermute x1, waiting for transfers between devices, body(): given_second = lax.ppermute(second_half, 'panel', [(0, 1), (1, 0)])  0.6 us
  transfers between devices with their start and end apart: 7, of which 3 were waited for; matrix products, arithmetic and copies ran while one was open for 0% of the time, Pallas kernels for 5%

profile of v10, /device:TPU:0, one launch (start us, length us, event | category | flops | bytes accessed | tf_op | source)
XLA Modules:
  0.0 27.6 jit_solution(8527174141715202004)
XLA Ops:
  0.0 1.4 %pack_edges.1 = (f32[104,128]{1,0:T(8,128)S(1)}, f32[12,320]{1,0:T(8,128)S(1)}, f32[120,128]{1,0:T(8,128)S(1)}, f32[104,128]{1,0:T(8,128)S(1)}, f32[32,128]{1,0:...) custom-call(f32[256,128]{1,0:T(8,128)} %bitcast.10, ...), custom_call_target="tpu_custom_call" | custom-call | tf_op jit(solution)/shard_map/pack_edges/pallas_call | solution.py:446
  1.4 0.0 copy-start
  1.4 3.0 %collective-permute-start = (f32[104,128]{1,0:T(8,128)S(1)}, f32[104,128]{1,0:T(8,128)S(1)}, u32[]{:S(2)}, u32[]{:S(2)}) collective-permute-start(f32[104,128]{1,0:T(8,128)S(1)} %get-tuple-element.26), channel_id=1, source_target_pairs={{0,1},{1,0},{2,3},{3,2},{4,5},{5,4},{6,7},{7,6},{8,9},{9,8},{10,11... | collective-permute-start | bytes 159752 | tf_op jit(solution)/shard_map/ppermute | solution.py:421
  4.4 1.6 %collective-permute-start.3 = (f32[120,128]{1,0:T(8,128)S(1)}, f32[120,128]{1,0:T(8,128)S(1)}, u32[]{:S(2)}, u32[]{:S(2)}) collective-permute-start(f32[120,128]{1,0:T(8,128)S(1)} %get-tuple-element.28), channel_id=1, source_target_pairs={{0,4},{4,0},{8,12},{12,8},{1,5},{5,1},{9,13},{13,9},{2,6},{6,2},{1... | collective-permute-start | bytes 184328 | tf_op jit(solution)/shard_map/ppermute | solution.py:421
  6.0 0.7 %collective-permute-start.2 = (f32[104,128]{1,0:T(8,128)S(1)}, f32[104,128]{1,0:T(8,128)S(1)}, u32[]{:S(2)}, u32[]{:S(2)}) collective-permute-start(f32[104,128]{1,0:T(8,128)S(1)} %get-tuple-element.27), channel_id=1, source_target_pairs={{4,8},{8,4},{5,9},{9,5},{6,10},{10,6},{7,11},{11,7},{20,24},{24,20... | collective-permute-start | bytes 159752 | tf_op jit(solution)/shard_map/ppermute | solution.py:421
  6.6 0.0 collective-permute-done.columns.even_pairs
  6.7 1.9 %collective-permute-start.1 = (f32[24,128]{1,0:T(8,128)S(1)}, f32[24,128]{1,0:T(8,128)S(1)}, u32[]{:S(2)}, u32[]{:S(2)}) collective-permute-start(f32[24,128]{1,0:T(8,128)S(1)} %relay_columns.1), channel_id=1, source_target_pairs={{0,2},{1,3},{2,0},{3,1},{4,6},{5,7},{6,4},{7,5},{8,10},{9,11},{10,... | collective-permute-start | bytes 36872 | tf_op jit(solution)/shard_map/ppermute | solution.py:470
  8.6 0.1 collective-permute-done.3.lat_even
  8.6 0.0 copy-start.1
  8.6 3.5 %collective-permute-start.6 = (f32[36,128]{1,0:T(8,128)S(1)}, f32[36,128]{1,0:T(8,128)S(1)}, u32[]{:S(2)}, u32[]{:S(2)}) collective-permute-start(f32[36,128]{1,0:T(8,128)S(1)} %forward_masses.1), channel_id=1, source_target_pairs={{0,8},{4,12},{8,0},{12,4},{1,9},{5,13},{9,1},{13,5},{2,10},{6,14},... | collective-permute-start | bytes 55304 | tf_op jit(solution)/shard_map/ppermute | solution.py:479
  12.2 0.0 copy-done
  12.2 0.0 copy-done.1
  12.2 0.0 copy-start.2
  12.2 0.5 %own_zonal.1.moved = f32[256,128]{1,0:T(8,128)S(1)} custom-call(f32[256,128]{1,0:T(8,128)S(1)} %bitcast.11, f32[64,128]{1,0:T(8,128)S(1)} %bitcast.17), custom_call_target="tpu_custom_call" | custom-call | tf_op jit(solution)/shard_map/own_zonal/pallas_call | solution.py:501
  12.6 0.3 index_tables.1
  12.9 0.0 collective-permute-done.2.lat_odd
  12.9 0.0 collective-permute-done.1.odd_pairs
  12.9 0.0 copy-done.2
  12.9 0.0 copy-start.3
  12.9 0.6 %advect_and_interpolate.1 = (f32[256,128]{1,0:T(8,128)S(1)}, f32[32,128]{1,0:T(8,128)S(1)}, f32[32,128]{1,0:T(8,128)S(1)}) custom-call(f32[256,128]{1,0:T(8,128)S(1)} %bitcast.12, f32[256,128]{1,0:T(8,128)S(1)} %own_zonal.1.moved, f32[64,128]{1,0:T(8,128)S(1)} %bitcast.19, f32[12,320]{1,0:T(8,128)S(1)} %get-tuple-element.25.sides, ...), custom_call_target="tpu_custom_call" | custom-call | tf_op jit(solution)/shard_map/advect_and_interpolate/pallas_call | solution.py:506
  13.5 0.0 collective-permute-start.5
  13.6 0.5 %collective-permute-start.4 = (f32[32,128]{1,0:T(8,128)S(1)}, f32[32,128]{1,0:T(8,128)S(1)}, u32[]{:S(2)}, u32[]{:S(2)}) collective-permute-start(f32[32,128]{1,0:T(8,128)S(1)} %get-tuple-element.39.own), channel_id=1, source_target_pairs={{0,16},{16,0},{1,17},{17,1},{2,18},{18,2},{3,19},{19,3},{4,20},{20... | collective-permute-start | bytes 49160 | tf_op jit(solution)/shard_map/ppermute | solution.py:524
  14.1 0.0 copy-done.3
  14.1 0.0 collective-permute-done.6.forwarded
  14.2 0.6 %collective-permute-done.5.given_second = f32[32,128]{1,0:T(8,128)S(1)} collective-permute-done((f32[32,128]{1,0:T(8,128)S(1)}, f32[32,128]{1,0:T(8,128)S(1)}, u32[]{:S(2)}, u32[]{:S(2)}) %collective-permute-start.5) | collective-permute-done | bytes 16416 | tf_op jit(solution)/shard_map/ppermute | solution.py:525
  14.8 0.2 collective-permute-done.4.given_first
  14.9 0.1 margin_blocks.1
  15.0 11.6 %all_to_all.5 = f32[32,1,1152]{2,1,0:T(1,128)S(1)} all-to-all(f32[32,1,1152]{2,1,0:T(1,128)S(1)} %bitcast.14), channel_id=1, replica_groups=mesh['panel'=2,'lat'=4,'lon'=4] {'panel','lat','lon'}, dimensions={0} | all-to-all | bytes 294912 | tf_op jit(solution)/shard_map/all_to_all | solution.py:537
  26.7 1.0 %fill_and_scale.1 = f32[1,4,8,8,128]{4,3,2,1,0:T(8,128)} custom-call(f32[256,128]{1,0:T(8,128)S(1)} %get-tuple-element.38.advected, f32[288,128]{1,0:T(8,128)S(1)} %bitcast.15, f32[8,256]{1,0:T(8,128)S(1)} %get-tuple-element.43.row_hit, bf16[128,256]{1,0:T(8,128)(2,1)S(1)} %get-tuple-element.44.column_hot), custom_call_target="tpu_custom_call" | custom-call | tf_op jit(solution)/shard_map/fill_and_scale/pallas_call | solution.py:540
  (4 shorter events, 0.1 us)
Async XLA Ops:
  1.4 10.8 %copy-start = (f32[1,4,8,8,128]{4,3,2,1,0:T(8,128)S(1)}, f32[1,4,8,8,128]{4,3,2,1,0:T(8,128)}, u32[]{:S(2)}) copy-start(f32[1,4,8,8,128]{4,3,2,1,0:T(8,128)} %param.8) | copy-start | bytes 393220
  1.4 5.2 %collective-permute-start = (f32[104,128]{1,0:T(8,128)S(1)}, f32[104,128]{1,0:T(8,128)S(1)}, u32[]{:S(2)}, u32[]{:S(2)}) collective-permute-start(f32[104,128]{1,0:T(8,128)S(1)} %get-tuple-element.26), channel_id=1, source_target_pairs={{0,1},{1,0},{2,3},{3,2},{4,5},{5,4},{6,7},{7,6},{8,9},{9,8},{10,11... | collective-permute-start | bytes 159752 | tf_op jit(solution)/shard_map/ppermute | solution.py:421
  4.4 4.2 %collective-permute-start.3 = (f32[120,128]{1,0:T(8,128)S(1)}, f32[120,128]{1,0:T(8,128)S(1)}, u32[]{:S(2)}, u32[]{:S(2)}) collective-permute-start(f32[120,128]{1,0:T(8,128)S(1)} %get-tuple-element.28), channel_id=1, source_target_pairs={{0,4},{4,0},{8,12},{12,8},{1,5},{5,1},{9,13},{13,9},{2,6},{6,2},{1... | collective-permute-start | bytes 184328 | tf_op jit(solution)/shard_map/ppermute | solution.py:421
  6.0 6.9 %collective-permute-start.2 = (f32[104,128]{1,0:T(8,128)S(1)}, f32[104,128]{1,0:T(8,128)S(1)}, u32[]{:S(2)}, u32[]{:S(2)}) collective-permute-start(f32[104,128]{1,0:T(8,128)S(1)} %get-tuple-element.27), channel_id=1, source_target_pairs={{4,8},{8,4},{5,9},{9,5},{6,10},{10,6},{7,11},{11,7},{20,24},{24,20... | collective-permute-start | bytes 159752 | tf_op jit(solution)/shard_map/ppermute | solution.py:421
  6.7 6.2 %collective-permute-start.1 = (f32[24,128]{1,0:T(8,128)S(1)}, f32[24,128]{1,0:T(8,128)S(1)}, u32[]{:S(2)}, u32[]{:S(2)}) collective-permute-start(f32[24,128]{1,0:T(8,128)S(1)} %relay_columns.1), channel_id=1, source_target_pairs={{0,2},{1,3},{2,0},{3,1},{4,6},{5,7},{6,4},{7,5},{8,10},{9,11},{10,... | collective-permute-start | bytes 36872 | tf_op jit(solution)/shard_map/ppermute | solution.py:470
  8.6 3.5 %copy-start.1 = (f32[1,8,8,128]{3,2,1,0:T(8,128)S(1)}, f32[1,8,8,128]{3,2,1,0:T(8,128)}, u32[]{:S(2)}) copy-start(f32[1,8,8,128]{3,2,1,0:T(8,128)} %param.9) | copy-start | bytes 98308
  8.6 5.5 %collective-permute-start.6 = (f32[36,128]{1,0:T(8,128)S(1)}, f32[36,128]{1,0:T(8,128)S(1)}, u32[]{:S(2)}, u32[]{:S(2)}) collective-permute-start(f32[36,128]{1,0:T(8,128)S(1)} %forward_masses.1), channel_id=1, source_target_pairs={{0,8},{4,12},{8,0},{12,4},{1,9},{5,13},{9,1},{13,5},{2,10},{6,14},... | collective-permute-start | bytes 55304 | tf_op jit(solution)/shard_map/ppermute | solution.py:479
  12.2 0.8 %copy-start.2 = (f32[1,8,8,128]{3,2,1,0:T(8,128)S(1)}, f32[1,8,8,128]{3,2,1,0:T(8,128)}, u32[]{:S(2)}) copy-start(f32[1,8,8,128]{3,2,1,0:T(8,128)} %param.10) | copy-start | bytes 98308
  12.9 1.1 %copy-start.3 = (f32[1,8,8,128]{3,2,1,0:T(8,128)S(1)}, f32[1,8,8,128]{3,2,1,0:T(8,128)}, u32[]{:S(2)}) copy-start(f32[1,8,8,128]{3,2,1,0:T(8,128)} %param.11) | copy-start | bytes 98308
  13.5 1.2 %collective-permute-start.5 = (f32[32,128]{1,0:T(8,128)S(1)}, f32[32,128]{1,0:T(8,128)S(1)}, u32[]{:S(2)}, u32[]{:S(2)}) collective-permute-start(f32[32,128]{1,0:T(8,128)S(1)} %get-tuple-element.40), channel_id=1, source_target_pairs={{0,16},{16,0},{1,17},{17,1},{2,18},{18,2},{3,19},{19,3},{4,20},{20... | collective-permute-start | bytes 49160 | tf_op jit(solution)/shard_map/ppermute | solution.py:525
  13.6 1.3 %collective-permute-start.4 = (f32[32,128]{1,0:T(8,128)S(1)}, f32[32,128]{1,0:T(8,128)S(1)}, u32[]{:S(2)}, u32[]{:S(2)}) collective-permute-start(f32[32,128]{1,0:T(8,128)S(1)} %get-tuple-element.39.own), channel_id=1, source_target_pairs={{0,16},{16,0},{1,17},{17,1},{2,18},{18,2},{3,19},{19,3},{4,20},{20... | collective-permute-start | bytes 49160 | tf_op jit(solution)/shard_map/ppermute | solution.py:524

commit v11 on v10

--- a/solution.py
+++ b/solution.py
@@ -9,8 +9,8 @@
 from jax.sharding import PartitionSpec as P
 
 HALO = 3
-COLUMN_ROWS = 104
-FORWARD_ROWS = 36
+COLUMN_ROWS = 24
+FORWARD_ROWS = 16
 
 
 class Sizes(NamedTuple):
@@ -168,7 +168,9 @@
     for i in range(sizes.chunks):
         columns[pl.ds(8 * i, 8), :] = edges[:, i * width : (i + 1) * width]
     start = 8 * sizes.chunks
-    columns[start:, :] = jnp.zeros((columns.shape[0] - start, width), jnp.float32)
+    spare = columns.shape[0] - start
+    if spare:
+        columns[pl.ds(start, spare), :] = jnp.zeros((spare, width), jnp.float32)
     sides[0 : 2 * HALO] = turned[0 : 2 * HALO]
     sides[2 * HALO : 4 * HALO] = turned[width - 2 * HALO : width]
 
@@ -242,7 +244,7 @@
 def main_kernel(
     sizes, field, moved, meridional, sides, odd_pairs, even_pairs, lat_odd, lat_even,
     row_weight, weight_high, weight_low,
-    advected, first_half, second_half, edge_rows, flux_rows,
+    advected, outgoing, edge_rows, flux_rows,
 ):
     tracers, levels, rows, width, blocks, capacity, _ = sizes
     fields, span, total = sizes.fields, levels * rows, sizes.fields * rows
@@ -323,13 +325,11 @@
     for tracer in range(tracers):
         payload = payloads[tracer * levels : (tracer + 1) * levels]
         base, lane = sizes.spot(tracer)
-        half = sizes.margin_rows // 2
-        outgoing = (first_half, second_half)[base // half]
         for block in range(blocks):
             at = block * capacity
-            outgoing[pl.ds(block * half + base % half, levels), lane : lane + capacity] = payload[
-                :, at : at + capacity
-            ]
+            outgoing[
+                pl.ds(block * sizes.margin_rows + base, levels), lane : lane + capacity
+            ] = payload[:, at : at + capacity]
 
 
 def sums_kernel(sizes, field, mass, advected, kept, remaining, partial):
@@ -347,22 +347,21 @@
         )[None]
 
 
-def blocks_kernel(sizes, own, given_first, given_second, partial, masses, all_blocks):
+def blocks_kernel(sizes, own, given, partial, masses, all_blocks):
     tracers, levels, _, width, blocks, capacity, places = sizes
-    half = sizes.margin_rows // 2
+    size = sizes.margin_rows
+    half = size // 2
     mine = lax.axis_index("panel")
-    weighed = [jnp.zeros((half, width), jnp.float32) for _ in range(2)]
+    weighed = jnp.zeros((size, width), jnp.float32)
     for block in range(blocks):
-        part = pl.ds(block * half, half)
+        margin = given[pl.ds(block * size, size), :]
         mass = masses[pl.ds(block * levels, levels), :]
-        mass = jnp.concatenate([mass] * (half // levels), axis=0)
-        margins = (given_first[part, :], given_second[part, :])
-        weighed = [total + margin * mass for total, margin in zip(weighed, margins, strict=True)]
-        for panel, piece in ((mine, margins[1]), (1 - mine, own[part, :])):
+        weighed = weighed + margin * jnp.concatenate([mass] * (size // levels), axis=0)
+        made = own[pl.ds(block * size, half), :]
+        for panel, piece in ((mine, margin[half:]), (1 - mine, made)):
             for place in range(places):
                 start = ((panel * blocks + block) * places + place) * (half + 1)
                 all_blocks[pl.ds(start, half), :] = piece
-    weighed = jnp.concatenate(weighed, axis=0)
     column = lax.broadcasted_iota(jnp.int32, (1, width), 1)
     added = []
     for tracer in range(tracers):
@@ -465,6 +464,7 @@
         relayed = pl.pallas_call(
             relay_kernel,
             out_shape=shape(8 * sizes.chunks, width),
+            cost_estimate=pl.CostEstimate(flops=600000000, bytes_accessed=0, transcendentals=0),
             name="relay_columns",
         )(*near(even_pairs))
         odd_pairs = lax.ppermute(relayed, "lon", [(i, i ^ 2) for i in range(places)])
@@ -480,6 +480,7 @@
         masses = pl.pallas_call(
             functools.partial(masses_kernel, sizes),
             out_shape=shape(blocks * levels, width),
+            cost_estimate=pl.CostEstimate(flops=500000000, bytes_accessed=0, transcendentals=0),
             name="gather_masses",
         )(*near(masses, lat_even, forwarded))
     else:
@@ -503,12 +504,11 @@
         out_shape=shape(fields * rows, width),
         name="own_zonal",
     )(*near(field, zonal))
-    advected, first_half, second_half = pl.pallas_call(
+    advected, outgoing = pl.pallas_call(
         functools.partial(main_kernel, sizes),
         out_shape=(
             shape(fields * rows, width),
-            shape(blocks * sizes.margin_rows // 2, width),
-            shape(blocks * sizes.margin_rows // 2, width),
+            shape(blocks * sizes.margin_rows, width),
         ),
         scratch_shapes=[
             pltpu.VMEM((fields * rows, width), jnp.float32),
@@ -521,8 +521,7 @@
             *weights,
         )
     )
-    given_first = lax.ppermute(first_half, "panel", [(0, 1), (1, 0)])
-    given_second = lax.ppermute(second_half, "panel", [(0, 1), (1, 0)])
+    given = lax.ppermute(outgoing, "panel", [(0, 1), (1, 0)])
     remaining, partial = pl.pallas_call(
         functools.partial(sums_kernel, sizes),
         out_shape=(shape(fields * rows, width), shape(2 * sizes.tracers, width)),
@@ -533,7 +532,7 @@
         functools.partial(blocks_kernel, sizes),
         out_shape=shape(devices * block_rows, width),
         name="margin_blocks",
-    )(*near(first_half, given_first, given_second, partial, masses))
+    )(*near(outgoing, given, partial, masses))
     incoming = lax.all_to_all(
         all_blocks.reshape(devices, 1, block_rows * width), ("panel", "lat", "lon"), 0, 0, tiled=True
     ).reshape(devices * block_rows, width)

time: 27.9 us -> 27.5 us (0.986)
  starting transfers between devices: 11.2 us -> 10.4 us
  waiting for transfers between devices: 0.83 us -> 1.41 us
  blocking collectives: 11.6 us -> 11.3 us
    ppermute x2 -> x1, starting transfers between devices: 0.53 us -> 0.04 us  [body(): given = lax.ppermute(outgoing, 'panel', [(0, 1), (1, 0)])]
    all_to_all x1, blocking collectives: 11.6 us -> 11.3 us  [body(): lax.all_to_all(all_blocks.reshape(devices, 1, block_rows * width), ('pane...]
    ppermute x1, starting transfers between devices: 1.91 us -> 1.58 us  [body(): lax.ppermute(relayed, 'lon', [(i, i ^ 2) for i in range(places)])]
    ppermute x3, waiting for transfers between devices: 0.06 us -> 0.37 us  [exchanged(): return lax.ppermute(value, axis, pairs)]
    ppermute x2 -> x1, waiting for transfers between devices: 0.76 us -> 0.97 us  [body(): given = lax.ppermute(outgoing, 'panel', [(0, 1), (1, 0)])]
  transfers between devices with their start and end apart: 7 -> 6, of which waited for: 3 -> 3; matrix products, arithmetic and copies ran while one was open for 0% -> 0% of each run, Pallas kernels for 5% -> 5%
where the time goes in v11:
time: 27.5 us; the launch traced here: 27.2 us
  blocking collectives  11.3 us (41%)
  starting transfers between devices  10.4 us (38%)
  Pallas kernels  3.83 us (14%)
  waiting for transfers between devices  1.41 us (5%)
    all_to_all x1, blocking collectives, body(): lax.all_to_all(all_blocks.reshape(devices, 1, block_rows * width), ('pane...  11.3 us
    ppermute x3, starting transfers between devices, exchanged(): return lax.ppermute(value, axis, pairs)  5.23 us
    ppermute x1, starting transfers between devices, body(): lax.ppermute(forwarded, 'lat', [(i, i ^ 2) for i in range(blocks)])  3.55 us
    ppermute x1, starting transfers between devices, body(): lax.ppermute(relayed, 'lon', [(i, i ^ 2) for i in range(places)])  1.58 us
    pallas_call x1, Pallas kernels, body(): pl.pallas_call(functools.partial(pack_kernel, sizes), out_shape=(shape(ma...  1.38 us
    ppermute x1, waiting for transfers between devices, body(): given = lax.ppermute(outgoing, 'panel', [(0, 1), (1, 0)])  0.97 us
    pallas_call x1, Pallas kernels, body(): pl.pallas_call(functools.partial(fill_kernel, sizes), out_shape=jax.Shape...  0.97 us
    pallas_call x1, Pallas kernels, body(): pl.pallas_call(functools.partial(main_kernel, sizes), out_shape=(shape(fi...  0.6 us
  transfers between devices with their start and end apart: 6, of which 3 were waited for; matrix products, arithmetic and copies ran while one was open for 0% of the time, Pallas kernels for 5%

profile of v11, /device:TPU:0, one launch (start us, length us, event | category | flops | bytes accessed | tf_op | source)
XLA Modules:
  0.0 27.2 jit_solution(9636867918455713980)
XLA Ops:
  0.0 1.4 %pack_edges.1 = (f32[24,128]{1,0:T(8,128)S(1)}, f32[12,320]{1,0:T(8,128)S(1)}, f32[120,128]{1,0:T(8,128)S(1)}, f32[104,128]{1,0:T(8,128)S(1)}, f32[32,128]{1,0:T...) custom-call(f32[256,128]{1,0:T(8,128)} %bitcast.10, ...), custom_call_target="tpu_custom_call" | custom-call | tf_op jit(solution)/shard_map/pack_edges/pallas_call | solution.py:445
  1.4 3.0 %collective-permute-start = (f32[24,128]{1,0:T(8,128)S(1)}, f32[24,128]{1,0:T(8,128)S(1)}, u32[]{:S(2)}, u32[]{:S(2)}) collective-permute-start(f32[24,128]{1,0:T(8,128)S(1)} %get-tuple-element.25), channel_id=1, source_target_pairs={{0,1},{1,0},{2,3},{3,2},{4,5},{5,4},{6,7},{7,6},{8,9},{9,8},{10,11... | collective-permute-start | bytes 36872 | tf_op jit(solution)/shard_map/ppermute | solution.py:420
  4.4 1.6 %collective-permute-start.3 = (f32[120,128]{1,0:T(8,128)S(1)}, f32[120,128]{1,0:T(8,128)S(1)}, u32[]{:S(2)}, u32[]{:S(2)}) collective-permute-start(f32[120,128]{1,0:T(8,128)S(1)} %get-tuple-element.27), channel_id=1, source_target_pairs={{0,4},{4,0},{8,12},{12,8},{1,5},{5,1},{9,13},{13,9},{2,6},{6,2},{1... | collective-permute-start | bytes 184328 | tf_op jit(solution)/shard_map/ppermute | solution.py:420
  6.0 0.7 %collective-permute-start.2 = (f32[104,128]{1,0:T(8,128)S(1)}, f32[104,128]{1,0:T(8,128)S(1)}, u32[]{:S(2)}, u32[]{:S(2)}) collective-permute-start(f32[104,128]{1,0:T(8,128)S(1)} %get-tuple-element.26), channel_id=1, source_target_pairs={{4,8},{8,4},{5,9},{9,5},{6,10},{10,6},{7,11},{11,7},{20,24},{24,20... | collective-permute-start | bytes 159752 | tf_op jit(solution)/shard_map/ppermute | solution.py:420
  6.6 0.0 collective-permute-done.columns.even_pairs
  6.6 0.0 copy-start
  6.7 1.6 %collective-permute-start.1 = (f32[24,128]{1,0:T(8,128)S(1)}, f32[24,128]{1,0:T(8,128)S(1)}, u32[]{:S(2)}, u32[]{:S(2)}) collective-permute-start(f32[24,128]{1,0:T(8,128)S(1)} %relay_columns.1), channel_id=1, source_target_pairs={{0,2},{1,3},{2,0},{3,1},{4,6},{5,7},{6,4},{7,5},{8,10},{9,11},{10,... | collective-permute-start | bytes 36872 | tf_op jit(solution)/shard_map/ppermute | solution.py:470
  8.2 0.4 %collective-permute-done.3.lat_even = f32[120,128]{1,0:T(8,128)S(1)} collective-permute-done((f32[120,128]{1,0:T(8,128)S(1)}, f32[120,128]{1,0:T(8,128)S(1)}, u32[]{:S(2)}, u32[]{:S(2)}) %collective-permute-start.3) | collective-permute-done | bytes 61472 | tf_op jit(solution)/shard_map/ppermute | solution.py:420
  8.6 0.0 copy-start.1
  8.6 3.5 %collective-permute-start.5 = (f32[16,128]{1,0:T(8,128)S(1)}, f32[16,128]{1,0:T(8,128)S(1)}, u32[]{:S(2)}, u32[]{:S(2)}) collective-permute-start(f32[16,128]{1,0:T(8,128)S(1)} %forward_masses.1), channel_id=1, source_target_pairs={{0,8},{4,12},{8,0},{12,4},{1,9},{5,13},{9,1},{13,5},{2,10},{6,14},... | collective-permute-start | bytes 24584 | tf_op jit(solution)/shard_map/ppermute | solution.py:479
  12.2 0.0 copy-done
  12.2 0.0 copy-done.1
  12.2 0.0 copy-start.2
  12.2 0.5 %own_zonal.1.moved = f32[256,128]{1,0:T(8,128)S(1)} custom-call(f32[256,128]{1,0:T(8,128)S(1)} %bitcast.11, f32[64,128]{1,0:T(8,128)S(1)} %bitcast.17), custom_call_target="tpu_custom_call" | custom-call | tf_op jit(solution)/shard_map/own_zonal/pallas_call | solution.py:502
  12.6 0.3 index_tables.1
  12.9 0.0 collective-permute-done.1.odd_pairs
  12.9 0.0 collective-permute-done.2.lat_odd
  12.9 0.0 copy-done.2
  12.9 0.0 copy-start.3
  12.9 0.6 %advect_and_interpolate.1 = (f32[256,128]{1,0:T(8,128)S(1)}, f32[64,128]{1,0:T(8,128)S(1)}) custom-call(f32[256,128]{1,0:T(8,128)S(1)} %bitcast.12, f32[256,128]{1,0:T(8,128)S(1)} %own_zonal.1.moved, f32[64,128]{1,0:T(8,128)S(1)} %bitcast.19, f32[12,320]{1,0:T(8,128)S(1)} %get-tuple-element.24.sides, f32[24,128]{1,0:T(8,128)S(1)} %collective-permute-done.1.odd_pairs, ...), custom_call_target="tpu_custom_call" | custom-call | tf_op jit(solution)/shard_map/advect_and_interpolate/pallas_call | solution.py:507
  13.5 0.0 collective-permute-start.4
  13.6 0.1 copy-done.3
  13.7 0.1 collective-permute-done.5.forwarded
  13.8 1.0 %collective-permute-done.4.given = f32[64,128]{1,0:T(8,128)S(1)} collective-permute-done((f32[64,128]{1,0:T(8,128)S(1)}, f32[64,128]{1,0:T(8,128)S(1)}, u32[]{:S(2)}, u32[]{:S(2)}) %collective-permute-start.4) | collective-permute-done | bytes 32800 | tf_op jit(solution)/shard_map/ppermute | solution.py:524
  14.8 0.1 margin_blocks.1
  14.9 11.3 %all_to_all.5 = f32[32,1,1152]{2,1,0:T(1,128)S(1)} all-to-all(f32[32,1,1152]{2,1,0:T(1,128)S(1)} %bitcast.14), channel_id=1, replica_groups=mesh['panel'=2,'lat'=4,'lon'=4] {'panel','lat','lon'}, dimensions={0} | all-to-all | bytes 294912 | tf_op jit(solution)/shard_map/all_to_all | solution.py:536
  26.2 1.0 %fill_and_scale.1 = f32[1,4,8,8,128]{4,3,2,1,0:T(8,128)} custom-call(f32[256,128]{1,0:T(8,128)S(1)} %get-tuple-element.37.advected, f32[288,128]{1,0:T(8,128)S(1)} %bitcast.15, f32[8,256]{1,0:T(8,128)S(1)} %get-tuple-element.41.row_hit, bf16[128,256]{1,0:T(8,128)(2,1)S(1)} %get-tuple-element.42.column_hot), custom_call_target="tpu_custom_call" | custom-call | tf_op jit(solution)/shard_map/fill_and_scale/pallas_call | solution.py:539
  (4 shorter events, 0.1 us)
Async XLA Ops:
  1.4 5.2 %collective-permute-start = (f32[24,128]{1,0:T(8,128)S(1)}, f32[24,128]{1,0:T(8,128)S(1)}, u32[]{:S(2)}, u32[]{:S(2)}) collective-permute-start(f32[24,128]{1,0:T(8,128)S(1)} %get-tuple-element.25), channel_id=1, source_target_pairs={{0,1},{1,0},{2,3},{3,2},{4,5},{5,4},{6,7},{7,6},{8,9},{9,8},{10,11... | collective-permute-start | bytes 36872 | tf_op jit(solution)/shard_map/ppermute | solution.py:420
  4.4 4.2 %collective-permute-start.3 = (f32[120,128]{1,0:T(8,128)S(1)}, f32[120,128]{1,0:T(8,128)S(1)}, u32[]{:S(2)}, u32[]{:S(2)}) collective-permute-start(f32[120,128]{1,0:T(8,128)S(1)} %get-tuple-element.27), channel_id=1, source_target_pairs={{0,4},{4,0},{8,12},{12,8},{1,5},{5,1},{9,13},{13,9},{2,6},{6,2},{1... | collective-permute-start | bytes 184328 | tf_op jit(solution)/shard_map/ppermute | solution.py:420
  6.0 6.9 %collective-permute-start.2 = (f32[104,128]{1,0:T(8,128)S(1)}, f32[104,128]{1,0:T(8,128)S(1)}, u32[]{:S(2)}, u32[]{:S(2)}) collective-permute-start(f32[104,128]{1,0:T(8,128)S(1)} %get-tuple-element.26), channel_id=1, source_target_pairs={{4,8},{8,4},{5,9},{9,5},{6,10},{10,6},{7,11},{11,7},{20,24},{24,20... | collective-permute-start | bytes 159752 | tf_op jit(solution)/shard_map/ppermute | solution.py:420
  6.6 5.5 %copy-start = (f32[1,4,8,8,128]{4,3,2,1,0:T(8,128)S(1)}, f32[1,4,8,8,128]{4,3,2,1,0:T(8,128)}, u32[]{:S(2)}) copy-start(f32[1,4,8,8,128]{4,3,2,1,0:T(8,128)} %param.8) | copy-start | bytes 393220
  6.7 6.2 %collective-permute-start.1 = (f32[24,128]{1,0:T(8,128)S(1)}, f32[24,128]{1,0:T(8,128)S(1)}, u32[]{:S(2)}, u32[]{:S(2)}) collective-permute-start(f32[24,128]{1,0:T(8,128)S(1)} %relay_columns.1), channel_id=1, source_target_pairs={{0,2},{1,3},{2,0},{3,1},{4,6},{5,7},{6,4},{7,5},{8,10},{9,11},{10,... | collective-permute-start | bytes 36872 | tf_op jit(solution)/shard_map/ppermute | solution.py:470
  8.6 3.6 %copy-start.1 = (f32[1,8,8,128]{3,2,1,0:T(8,128)S(1)}, f32[1,8,8,128]{3,2,1,0:T(8,128)}, u32[]{:S(2)}) copy-start(f32[1,8,8,128]{3,2,1,0:T(8,128)} %param.9) | copy-start | bytes 98308
  8.6 5.2 %collective-permute-start.5 = (f32[16,128]{1,0:T(8,128)S(1)}, f32[16,128]{1,0:T(8,128)S(1)}, u32[]{:S(2)}, u32[]{:S(2)}) collective-permute-start(f32[16,128]{1,0:T(8,128)S(1)} %forward_masses.1), channel_id=1, source_target_pairs={{0,8},{4,12},{8,0},{12,4},{1,9},{5,13},{9,1},{13,5},{2,10},{6,14},... | collective-permute-start | bytes 24584 | tf_op jit(solution)/shard_map/ppermute | solution.py:479
  12.2 0.8 %copy-start.2 = (f32[1,8,8,128]{3,2,1,0:T(8,128)S(1)}, f32[1,8,8,128]{3,2,1,0:T(8,128)}, u32[]{:S(2)}) copy-start(f32[1,8,8,128]{3,2,1,0:T(8,128)} %param.10) | copy-start | bytes 98308
  12.9 0.8 %copy-start.3 = (f32[1,8,8,128]{3,2,1,0:T(8,128)S(1)}, f32[1,8,8,128]{3,2,1,0:T(8,128)}, u32[]{:S(2)}) copy-start(f32[1,8,8,128]{3,2,1,0:T(8,128)} %param.11) | copy-start | bytes 98308
  13.5 1.2 %collective-permute-start.4 = (f32[64,128]{1,0:T(8,128)S(1)}, f32[64,128]{1,0:T(8,128)S(1)}, u32[]{:S(2)}, u32[]{:S(2)}) collective-permute-start(f32[64,128]{1,0:T(8,128)S(1)} %get-tuple-element.38.own), channel_id=1, source_target_pairs={{0,16},{16,0},{1,17},{17,1},{2,18},{18,2},{3,19},{19,3},{4,20},{20... | collective-permute-start | bytes 98312 | tf_op jit(solution)/shard_map/ppermute | solution.py:524

commit v12 on v11

--- a/solution.py
+++ b/solution.py
@@ -141,7 +141,7 @@
     spots = row_of(target[...])
     row_hot = one_hot(spots // width, rows)
     column_hot = one_hot(lax.rem(spots, width), width).astype(jnp.bfloat16)
-    picked = dot_parts(three_parts(mass[...]), column_hot)
+    picked = dot_parts(two_parts(mass[...]), column_hot)
     picked = jnp.sum(
         picked.reshape(levels, rows, spots.shape[1]) * row_hot[None], axis=1
     ) * live_row(live[...], capacity)
@@ -239,6 +239,11 @@
         ]
         flux = face_flux(along, zonal[...])
         moved[part, :] = cells - (pltpu.roll(flux, width - 1, 1) - flux)
+
+
+def prepare_kernel(sizes, field, zonal, donor, fraction, target, live, moved, *tables):
+    zonal_kernel(sizes, field, zonal, moved)
+    tables_kernel(sizes, donor, fraction, target, live, *tables)
 
 
 def main_kernel(
@@ -360,7 +365,7 @@
         made = own[pl.ds(block * size, half), :]
         for panel, piece in ((mine, margin[half:]), (1 - mine, made)):
             for place in range(places):
-                start = ((panel * blocks + block) * places + place) * (half + 1)
+                start = ((panel * places + place) * blocks + block) * (half + 1)
                 all_blocks[pl.ds(start, half), :] = piece
     column = lax.broadcasted_iota(jnp.int32, (1, width), 1)
     added = []
@@ -387,7 +392,7 @@
     for block in range(blocks):
         halves = []
         for panel in (1 - mine, mine):
-            start = ((panel * blocks + block) * places + place) * (half + 1)
+            start = ((panel * places + place) * blocks + block) * (half + 1)
             halves.append(incoming[pl.ds(start, half), :])
         piece = jnp.concatenate(halves, axis=0)
         arrived.append(
@@ -487,9 +492,10 @@
         masses = lax.all_to_all(
             masses.reshape(blocks, levels, width), "lat", 0, 0, tiled=True
         ).reshape(blocks * levels, width)
-    kept, row_hit, column_hot, *weights = pl.pallas_call(
-        functools.partial(tables_kernel, sizes),
+    moved, kept, row_hit, column_hot, *weights = pl.pallas_call(
+        functools.partial(prepare_kernel, sizes),
         out_shape=(
+            shape(fields * rows, width),
             shape(rows, width),
             shape(rows, slots),
             pltpu.VMEM((width, slots), jnp.bfloat16),
@@ -497,13 +503,8 @@
             pltpu.VMEM((width, slots), jnp.bfloat16),
             pltpu.VMEM((width, slots), jnp.bfloat16),
         ),
-        name="index_tables",
-    )(*near(*index_copies))
-    moved = pl.pallas_call(
-        functools.partial(zonal_kernel, sizes),
-        out_shape=shape(fields * rows, width),
-        name="own_zonal",
-    )(*near(field, zonal))
+        name="zonal_and_tables",
+    )(*near(field, zonal, *index_copies))
     advected, outgoing = pl.pallas_call(
         functools.partial(main_kernel, sizes),
         out_shape=(
@@ -534,7 +535,7 @@
         name="margin_blocks",
     )(*near(outgoing, given, partial, masses))
     incoming = lax.all_to_all(
-        all_blocks.reshape(devices, 1, block_rows * width), ("panel", "lat", "lon"), 0, 0, tiled=True
+        all_blocks.reshape(devices, 1, block_rows * width), ("panel", "lon", "lat"), 0, 0, tiled=True
     ).reshape(devices * block_rows, width)
     return pl.pallas_call(
         functools.partial(fill_kernel, sizes),

time: 27.5 us -> 27.3 us (level)
    pallas_call x2 -> x1, Pallas kernels: 0.72 us -> 0.5 us  [body(): pl.pallas_call(functools.partial(prepare_kernel, sizes), out_shape=(shape...]
  transfers between devices with their start and end apart: 6 -> 6, of which waited for: 3 -> 3; matrix products, arithmetic and copies ran while one was open for 0% -> 0% of each run, Pallas kernels for 5% -> 4%
where the time goes in v12:
time: 27.3 us; the launch traced here: 27 us
  blocking collectives  11.2 us (41%)
  starting transfers between devices  10.4 us (38%)
  Pallas kernels  3.59 us (13%)
  waiting for transfers between devices  1.41 us (5%)
  local copies, waits for them, and re-layouts  0.36 us (1%)
    all_to_all x1, blocking collectives, body(): lax.all_to_all(all_blocks.reshape(devices, 1, block_rows * width), ('pane...  11.2 us
    ppermute x3, starting transfers between devices, exchanged(): return lax.ppermute(value, axis, pairs)  5.23 us
    ppermute x1, starting transfers between devices, body(): lax.ppermute(forwarded, 'lat', [(i, i ^ 2) for i in range(blocks)])  3.55 us
    ppermute x1, starting transfers between devices, body(): lax.ppermute(relayed, 'lon', [(i, i ^ 2) for i in range(places)])  1.58 us
    pallas_call x1, Pallas kernels, body(): pl.pallas_call(functools.partial(pack_kernel, sizes), out_shape=(shape(ma...  1.36 us
    pallas_call x1, Pallas kernels, body(): pl.pallas_call(functools.partial(fill_kernel, sizes), out_shape=jax.Shape...  0.97 us
    ppermute x1, waiting for transfers between devices, body(): given = lax.ppermute(outgoing, 'panel', [(0, 1), (1, 0)])  0.97 us
    pallas_call x1, Pallas kernels, body(): pl.pallas_call(functools.partial(main_kernel, sizes), out_shape=(shape(fi...  0.6 us
  transfers between devices with their start and end apart: 6, of which 3 were waited for; matrix products, arithmetic and copies ran while one was open for 0% of the time, Pallas kernels for 4%

profile of v12, /device:TPU:0, one launch (start us, length us, event | category | flops | bytes accessed | tf_op | source)
XLA Modules:
  0.0 27.0 jit_solution(4979951429616913238)
XLA Ops:
  0.0 1.4 %pack_edges.1 = (f32[24,128]{1,0:T(8,128)S(1)}, f32[12,320]{1,0:T(8,128)S(1)}, f32[120,128]{1,0:T(8,128)S(1)}, f32[104,128]{1,0:T(8,128)S(1)}, f32[32,128]{1,0:T...) custom-call(f32[256,128]{1,0:T(8,128)} %bitcast.10, ...), custom_call_target="tpu_custom_call" | custom-call | tf_op jit(solution)/shard_map/pack_edges/pallas_call | solution.py:450
  1.4 3.0 %collective-permute-start = (f32[24,128]{1,0:T(8,128)S(1)}, f32[24,128]{1,0:T(8,128)S(1)}, u32[]{:S(2)}, u32[]{:S(2)}) collective-permute-start(f32[24,128]{1,0:T(8,128)S(1)} %get-tuple-element.31), channel_id=1, source_target_pairs={{0,1},{1,0},{2,3},{3,2},{4,5},{5,4},{6,7},{7,6},{8,9},{9,8},{10,11... | collective-permute-start | bytes 36872 | tf_op jit(solution)/shard_map/ppermute | solution.py:425
  4.4 1.6 %collective-permute-start.3 = (f32[120,128]{1,0:T(8,128)S(1)}, f32[120,128]{1,0:T(8,128)S(1)}, u32[]{:S(2)}, u32[]{:S(2)}) collective-permute-start(f32[120,128]{1,0:T(8,128)S(1)} %get-tuple-element.33), channel_id=1, source_target_pairs={{0,4},{4,0},{8,12},{12,8},{1,5},{5,1},{9,13},{13,9},{2,6},{6,2},{1... | collective-permute-start | bytes 184328 | tf_op jit(solution)/shard_map/ppermute | solution.py:425
  6.0 0.7 %collective-permute-start.2 = (f32[104,128]{1,0:T(8,128)S(1)}, f32[104,128]{1,0:T(8,128)S(1)}, u32[]{:S(2)}, u32[]{:S(2)}) collective-permute-start(f32[104,128]{1,0:T(8,128)S(1)} %get-tuple-element.32), channel_id=1, source_target_pairs={{4,8},{8,4},{5,9},{9,5},{6,10},{10,6},{7,11},{11,7},{20,24},{24,20... | collective-permute-start | bytes 159752 | tf_op jit(solution)/shard_map/ppermute | solution.py:425
  6.6 0.0 collective-permute-done.columns.even_pairs
  6.6 0.0 copy-start
  6.6 1.6 %collective-permute-start.1 = (f32[24,128]{1,0:T(8,128)S(1)}, f32[24,128]{1,0:T(8,128)S(1)}, u32[]{:S(2)}, u32[]{:S(2)}) collective-permute-start(f32[24,128]{1,0:T(8,128)S(1)} %relay_columns.1), channel_id=1, source_target_pairs={{0,2},{1,3},{2,0},{3,1},{4,6},{5,7},{6,4},{7,5},{8,10},{9,11},{10,... | collective-permute-start | bytes 36872 | tf_op jit(solution)/shard_map/ppermute | solution.py:475
  8.2 0.4 %collective-permute-done.3.lat_even = f32[120,128]{1,0:T(8,128)S(1)} collective-permute-done((f32[120,128]{1,0:T(8,128)S(1)}, f32[120,128]{1,0:T(8,128)S(1)}, u32[]{:S(2)}, u32[]{:S(2)}) %collective-permute-start.3) | collective-permute-done | bytes 61472 | tf_op jit(solution)/shard_map/ppermute | solution.py:425
  8.6 0.0 copy-start.3
  8.6 3.6 %collective-permute-start.5 = (f32[16,128]{1,0:T(8,128)S(1)}, f32[16,128]{1,0:T(8,128)S(1)}, u32[]{:S(2)}, u32[]{:S(2)}) collective-permute-start(f32[16,128]{1,0:T(8,128)S(1)} %forward_masses.1), channel_id=1, source_target_pairs={{0,8},{4,12},{8,0},{12,4},{1,9},{5,13},{9,1},{13,5},{2,10},{6,14},... | collective-permute-start | bytes 24584 | tf_op jit(solution)/shard_map/ppermute | solution.py:484
  12.2 0.0 copy-done
  12.2 0.0 copy-done.3
  12.2 0.0 copy-start.1
  12.2 0.5 %zonal_and_tables.1 = (f32[256,128]{1,0:T(8,128)S(1)}, f32[8,128]{1,0:T(8,128)S(1)}, f32[8,256]{1,0:T(8,128)S(1)}, bf16[128,256]{1,0:T(8,128)(2,1)S(1)}, f32[8,2...) custom-call(f32[256,128]{1,0:T(8,128)S(1)} %bitcast.11, f32[64,128]{1,0:T(8,128)S(1)} %bitcast.21, ...), custom_call_target="tpu_custom_call" | custom-call | tf_op jit(solution)/shard_map/zonal_and_tables/pallas_call | solution.py:495
  12.7 0.0 collective-permute-done.1.odd_pairs
  12.7 0.0 collective-permute-done.2.lat_odd
  12.7 0.2 copy-done.1
  12.9 0.0 copy-start.2
  12.9 0.6 %advect_and_interpolate.1 = (f32[256,128]{1,0:T(8,128)S(1)}, f32[64,128]{1,0:T(8,128)S(1)}) custom-call(f32[256,128]{1,0:T(8,128)S(1)} %bitcast.12, f32[256,128]{1,0:T(8,128)S(1)} %get-tuple-element.29.moved, f32[64,128]{1,0:T(8,128)S(1)} %bitcast.17, f32[12,320]{1,0:T(8,128)S(1)} %get-tuple-element.30.sides, ...), custom_call_target="tpu_custom_call" | custom-call | tf_op jit(solution)/shard_map/advect_and_interpolate/pallas_call | solution.py:508
  13.5 0.0 collective-permute-start.4
  13.6 0.1 copy-done.2
  13.7 0.1 collective-permute-done.5.forwarded
  13.8 1.0 %collective-permute-done.4.given = f32[64,128]{1,0:T(8,128)S(1)} collective-permute-done((f32[64,128]{1,0:T(8,128)S(1)}, f32[64,128]{1,0:T(8,128)S(1)}, u32[]{:S(2)}, u32[]{:S(2)}) %collective-permute-start.4) | collective-permute-done | bytes 32800 | tf_op jit(solution)/shard_map/ppermute | solution.py:525
  14.8 0.1 margin_blocks.1
  14.9 11.2 %all_to_all.5 = f32[32,1,1152]{2,1,0:T(1,128)S(1)} all-to-all(f32[32,1,1152]{2,1,0:T(1,128)S(1)} %bitcast.14), channel_id=1, replica_groups=mesh['panel'=2,'lat'=4,'lon'=4] {'panel','lon','lat'}, dimensions={0} | all-to-all | bytes 294912 | tf_op jit(solution)/shard_map/all_to_all | solution.py:537
  26.0 1.0 %fill_and_scale.1 = f32[1,4,8,8,128]{4,3,2,1,0:T(8,128)} custom-call(f32[256,128]{1,0:T(8,128)S(1)} %get-tuple-element.39.advected, f32[288,128]{1,0:T(8,128)S(1)} %bitcast.15, f32[8,256]{1,0:T(8,128)S(1)} %get-tuple-element.43.row_hit, bf16[128,256]{1,0:T(8,128)(2,1)S(1)} %get-tuple-element.44.column_hot), custom_call_target="tpu_custom_call" | custom-call | tf_op jit(solution)/shard_map/fill_and_scale/pallas_call | solution.py:540
  (4 shorter events, 0.1 us)
Async XLA Ops:
  1.4 5.2 %collective-permute-start = (f32[24,128]{1,0:T(8,128)S(1)}, f32[24,128]{1,0:T(8,128)S(1)}, u32[]{:S(2)}, u32[]{:S(2)}) collective-permute-start(f32[24,128]{1,0:T(8,128)S(1)} %get-tuple-element.31), channel_id=1, source_target_pairs={{0,1},{1,0},{2,3},{3,2},{4,5},{5,4},{6,7},{7,6},{8,9},{9,8},{10,11... | collective-permute-start | bytes 36872 | tf_op jit(solution)/shard_map/ppermute | solution.py:425
  4.4 4.2 %collective-permute-start.3 = (f32[120,128]{1,0:T(8,128)S(1)}, f32[120,128]{1,0:T(8,128)S(1)}, u32[]{:S(2)}, u32[]{:S(2)}) collective-permute-start(f32[120,128]{1,0:T(8,128)S(1)} %get-tuple-element.33), channel_id=1, source_target_pairs={{0,4},{4,0},{8,12},{12,8},{1,5},{5,1},{9,13},{13,9},{2,6},{6,2},{1... | collective-permute-start | bytes 184328 | tf_op jit(solution)/shard_map/ppermute | solution.py:425
  6.0 6.7 %collective-permute-start.2 = (f32[104,128]{1,0:T(8,128)S(1)}, f32[104,128]{1,0:T(8,128)S(1)}, u32[]{:S(2)}, u32[]{:S(2)}) collective-permute-start(f32[104,128]{1,0:T(8,128)S(1)} %get-tuple-element.32), channel_id=1, source_target_pairs={{4,8},{8,4},{5,9},{9,5},{6,10},{10,6},{7,11},{11,7},{20,24},{24,20... | collective-permute-start | bytes 159752 | tf_op jit(solution)/shard_map/ppermute | solution.py:425
  6.6 5.5 %copy-start = (f32[1,4,8,8,128]{4,3,2,1,0:T(8,128)S(1)}, f32[1,4,8,8,128]{4,3,2,1,0:T(8,128)}, u32[]{:S(2)}) copy-start(f32[1,4,8,8,128]{4,3,2,1,0:T(8,128)} %param.8) | copy-start | bytes 393220
  6.6 6.0 %collective-permute-start.1 = (f32[24,128]{1,0:T(8,128)S(1)}, f32[24,128]{1,0:T(8,128)S(1)}, u32[]{:S(2)}, u32[]{:S(2)}) collective-permute-start(f32[24,128]{1,0:T(8,128)S(1)} %relay_columns.1), channel_id=1, source_target_pairs={{0,2},{1,3},{2,0},{3,1},{4,6},{5,7},{6,4},{7,5},{8,10},{9,11},{10,... | collective-permute-start | bytes 36872 | tf_op jit(solution)/shard_map/ppermute | solution.py:475
  8.6 3.6 %copy-start.3 = (f32[1,8,8,128]{3,2,1,0:T(8,128)S(1)}, f32[1,8,8,128]{3,2,1,0:T(8,128)}, u32[]{:S(2)}) copy-start(f32[1,8,8,128]{3,2,1,0:T(8,128)} %param.9) | copy-start | bytes 98308
  8.6 5.2 %collective-permute-start.5 = (f32[16,128]{1,0:T(8,128)S(1)}, f32[16,128]{1,0:T(8,128)S(1)}, u32[]{:S(2)}, u32[]{:S(2)}) collective-permute-start(f32[16,128]{1,0:T(8,128)S(1)} %forward_masses.1), channel_id=1, source_target_pairs={{0,8},{4,12},{8,0},{12,4},{1,9},{5,13},{9,1},{13,5},{2,10},{6,14},... | collective-permute-start | bytes 24584 | tf_op jit(solution)/shard_map/ppermute | solution.py:484
  12.2 0.8 %copy-start.1 = (f32[1,8,8,128]{3,2,1,0:T(8,128)S(1)}, f32[1,8,8,128]{3,2,1,0:T(8,128)}, u32[]{:S(2)}) copy-start(f32[1,8,8,128]{3,2,1,0:T(8,128)} %param.10) | copy-start | bytes 98308
  12.9 0.8 %copy-start.2 = (f32[1,8,8,128]{3,2,1,0:T(8,128)S(1)}, f32[1,8,8,128]{3,2,1,0:T(8,128)}, u32[]{:S(2)}) copy-start(f32[1,8,8,128]{3,2,1,0:T(8,128)} %param.11) | copy-start | bytes 98308
  13.5 1.2 %collective-permute-start.4 = (f32[64,128]{1,0:T(8,128)S(1)}, f32[64,128]{1,0:T(8,128)S(1)}, u32[]{:S(2)}, u32[]{:S(2)}) collective-permute-start(f32[64,128]{1,0:T(8,128)S(1)} %get-tuple-element.40.own), channel_id=1, source_target_pairs={{0,16},{16,0},{1,17},{17,1},{2,18},{18,2},{3,19},{19,3},{4,20},{20... | collective-permute-start | bytes 98312 | tf_op jit(solution)/shard_map/ppermute | solution.py:525

commit v13 on v12

--- a/solution.py
+++ b/solution.py
@@ -175,6 +175,10 @@
     sides[2 * HALO : 4 * HALO] = turned[width - 2 * HALO : width]
 
 
+def passed_on(sizes):
+    return sizes.places == 4
+
+
 def relay_kernel(columns, relayed):
     relayed[...] = columns[0 : relayed.shape[0], :]
 
@@ -255,9 +259,9 @@
     fields, span, total = sizes.fields, levels * rows, sizes.fields * rows
     place = lax.axis_index("lon")
     even = lax.rem(place, 2) == 0
-    inner = (place > 0) & (place < sizes.places - 1)
     first, second = unfold(sizes, even_pairs), unfold(sizes, odd_pairs)
-    second = jnp.where(inner, second, 0.0)
+    if passed_on(sizes):
+        second = jnp.where((place > 0) & (place < sizes.places - 1), second, 0.0)
     from_west = jnp.where(even, second[0:HALO], first[0:HALO])
     from_east = jnp.where(even, first[HALO : 2 * HALO], second[HALO : 2 * HALO])
     west = jnp.concatenate([from_west, sides[0 : 2 * HALO]], axis=0)
@@ -465,7 +469,7 @@
     lat_even = exchanged(lat_even, "lat", 0)
     lat_odd = exchanged(lat_odd, "lat", 1)
     even_pairs = exchanged(columns, "lon", 0)
-    if places == 4:
+    if passed_on(sizes):
         relayed = pl.pallas_call(
             relay_kernel,
             out_shape=shape(8 * sizes.chunks, width),

time: 27.3 us -> 27.3 us (level)
  no operation moved by 1% of the time
where the time goes in v13:
time: 27.3 us; the launch traced here: 27 us
  blocking collectives  11.2 us (41%)
  starting transfers between devices  10.4 us (38%)
  Pallas kernels  3.59 us (13%)
  waiting for transfers between devices  1.41 us (5%)
  local copies, waits for them, and re-layouts  0.36 us (1%)
    all_to_all x1, blocking collectives, body(): lax.all_to_all(all_blocks.reshape(devices, 1, block_rows * width), ('pane...  11.2 us
    ppermute x3, starting transfers between devices, exchanged(): return lax.ppermute(value, axis, pairs)  5.23 us
    ppermute x1, starting transfers between devices, body(): lax.ppermute(forwarded, 'lat', [(i, i ^ 2) for i in range(blocks)])  3.55 us
    ppermute x1, starting transfers between devices, body(): lax.ppermute(relayed, 'lon', [(i, i ^ 2) for i in range(places)])  1.58 us
    pallas_call x1, Pallas kernels, body(): pl.pallas_call(functools.partial(pack_kernel, sizes), out_shape=(shape(ma...  1.36 us
    pallas_call x1, Pallas kernels, body(): pl.pallas_call(functools.partial(fill_kernel, sizes), out_shape=jax.Shape...  0.97 us
    ppermute x1, waiting for transfers between devices, body(): given = lax.ppermute(outgoing, 'panel', [(0, 1), (1, 0)])  0.97 us
    pallas_call x1, Pallas kernels, body(): pl.pallas_call(functools.partial(main_kernel, sizes), out_shape=(shape(fi...  0.6 us
  transfers between devices with their start and end apart: 6, of which 3 were waited for; matrix products, arithmetic and copies ran while one was open for 0% of the time, Pallas kernels for 4%

profile of v13, /device:TPU:0, one launch (start us, length us, event | category | flops | bytes accessed | tf_op | source)
XLA Modules:
  0.0 27.0 jit_solution(4979951429616913238)
XLA Ops:
  0.0 1.4 %pack_edges.1 = (f32[24,128]{1,0:T(8,128)S(1)}, f32[12,320]{1,0:T(8,128)S(1)}, f32[120,128]{1,0:T(8,128)S(1)}, f32[104,128]{1,0:T(8,128)S(1)}, f32[32,128]{1,0:T...) custom-call(f32[256,128]{1,0:T(8,128)} %bitcast.10, ...), custom_call_target="tpu_custom_call" | custom-call | tf_op jit(solution)/shard_map/pack_edges/pallas_call | solution.py:454
  1.4 3.0 %collective-permute-start = (f32[24,128]{1,0:T(8,128)S(1)}, f32[24,128]{1,0:T(8,128)S(1)}, u32[]{:S(2)}, u32[]{:S(2)}) collective-permute-start(f32[24,128]{1,0:T(8,128)S(1)} %get-tuple-element.31), channel_id=1, source_target_pairs={{0,1},{1,0},{2,3},{3,2},{4,5},{5,4},{6,7},{7,6},{8,9},{9,8},{10,11... | collective-permute-start | bytes 36872 | tf_op jit(solution)/shard_map/ppermute | solution.py:429
  4.4 1.6 %collective-permute-start.3 = (f32[120,128]{1,0:T(8,128)S(1)}, f32[120,128]{1,0:T(8,128)S(1)}, u32[]{:S(2)}, u32[]{:S(2)}) collective-permute-start(f32[120,128]{1,0:T(8,128)S(1)} %get-tuple-element.33), channel_id=1, source_target_pairs={{0,4},{4,0},{8,12},{12,8},{1,5},{5,1},{9,13},{13,9},{2,6},{6,2},{1... | collective-permute-start | bytes 184328 | tf_op jit(solution)/shard_map/ppermute | solution.py:429
  6.0 0.7 %collective-permute-start.2 = (f32[104,128]{1,0:T(8,128)S(1)}, f32[104,128]{1,0:T(8,128)S(1)}, u32[]{:S(2)}, u32[]{:S(2)}) collective-permute-start(f32[104,128]{1,0:T(8,128)S(1)} %get-tuple-element.32), channel_id=1, source_target_pairs={{4,8},{8,4},{5,9},{9,5},{6,10},{10,6},{7,11},{11,7},{20,24},{24,20... | collective-permute-start | bytes 159752 | tf_op jit(solution)/shard_map/ppermute | solution.py:429
  6.6 0.0 collective-permute-done.columns.even_pairs
  6.6 0.0 copy-start
  6.6 1.6 %collective-permute-start.1 = (f32[24,128]{1,0:T(8,128)S(1)}, f32[24,128]{1,0:T(8,128)S(1)}, u32[]{:S(2)}, u32[]{:S(2)}) collective-permute-start(f32[24,128]{1,0:T(8,128)S(1)} %relay_columns.1), channel_id=1, source_target_pairs={{0,2},{1,3},{2,0},{3,1},{4,6},{5,7},{6,4},{7,5},{8,10},{9,11},{10,... | collective-permute-start | bytes 36872 | tf_op jit(solution)/shard_map/ppermute | solution.py:479
  8.2 0.4 %collective-permute-done.3.lat_even = f32[120,128]{1,0:T(8,128)S(1)} collective-permute-done((f32[120,128]{1,0:T(8,128)S(1)}, f32[120,128]{1,0:T(8,128)S(1)}, u32[]{:S(2)}, u32[]{:S(2)}) %collective-permute-start.3) | collective-permute-done | bytes 61472 | tf_op jit(solution)/shard_map/ppermute | solution.py:429
  8.6 0.0 copy-start.3
  8.6 3.6 %collective-permute-start.5 = (f32[16,128]{1,0:T(8,128)S(1)}, f32[16,128]{1,0:T(8,128)S(1)}, u32[]{:S(2)}, u32[]{:S(2)}) collective-permute-start(f32[16,128]{1,0:T(8,128)S(1)} %forward_masses.1), channel_id=1, source_target_pairs={{0,8},{4,12},{8,0},{12,4},{1,9},{5,13},{9,1},{13,5},{2,10},{6,14},... | collective-permute-start | bytes 24584 | tf_op jit(solution)/shard_map/ppermute | solution.py:488
  12.2 0.0 copy-done
  12.2 0.0 copy-done.3
  12.2 0.0 copy-start.1
  12.2 0.5 %zonal_and_tables.1 = (f32[256,128]{1,0:T(8,128)S(1)}, f32[8,128]{1,0:T(8,128)S(1)}, f32[8,256]{1,0:T(8,128)S(1)}, bf16[128,256]{1,0:T(8,128)(2,1)S(1)}, f32[8,2...) custom-call(f32[256,128]{1,0:T(8,128)S(1)} %bitcast.11, f32[64,128]{1,0:T(8,128)S(1)} %bitcast.21, ...), custom_call_target="tpu_custom_call" | custom-call | tf_op jit(solution)/shard_map/zonal_and_tables/pallas_call | solution.py:499
  12.7 0.0 collective-permute-done.1.odd_pairs
  12.7 0.0 collective-permute-done.2.lat_odd
  12.7 0.2 copy-done.1
  12.9 0.0 copy-start.2
  12.9 0.6 %advect_and_interpolate.1 = (f32[256,128]{1,0:T(8,128)S(1)}, f32[64,128]{1,0:T(8,128)S(1)}) custom-call(f32[256,128]{1,0:T(8,128)S(1)} %bitcast.12, f32[256,128]{1,0:T(8,128)S(1)} %get-tuple-element.29.moved, f32[64,128]{1,0:T(8,128)S(1)} %bitcast.17, f32[12,320]{1,0:T(8,128)S(1)} %get-tuple-element.30.sides, ...), custom_call_target="tpu_custom_call" | custom-call | tf_op jit(solution)/shard_map/advect_and_interpolate/pallas_call | solution.py:512
  13.5 0.0 collective-permute-start.4
  13.6 0.1 copy-done.2
  13.7 0.1 collective-permute-done.5.forwarded
  13.8 1.0 %collective-permute-done.4.given = f32[64,128]{1,0:T(8,128)S(1)} collective-permute-done((f32[64,128]{1,0:T(8,128)S(1)}, f32[64,128]{1,0:T(8,128)S(1)}, u32[]{:S(2)}, u32[]{:S(2)}) %collective-permute-start.4) | collective-permute-done | bytes 32800 | tf_op jit(solution)/shard_map/ppermute | solution.py:529
  14.8 0.1 margin_blocks.1
  14.9 11.2 %all_to_all.5 = f32[32,1,1152]{2,1,0:T(1,128)S(1)} all-to-all(f32[32,1,1152]{2,1,0:T(1,128)S(1)} %bitcast.14), channel_id=1, replica_groups=mesh['panel'=2,'lat'=4,'lon'=4] {'panel','lon','lat'}, dimensions={0} | all-to-all | bytes 294912 | tf_op jit(solution)/shard_map/all_to_all | solution.py:541
  26.0 1.0 %fill_and_scale.1 = f32[1,4,8,8,128]{4,3,2,1,0:T(8,128)} custom-call(f32[256,128]{1,0:T(8,128)S(1)} %get-tuple-element.39.advected, f32[288,128]{1,0:T(8,128)S(1)} %bitcast.15, f32[8,256]{1,0:T(8,128)S(1)} %get-tuple-element.43.row_hit, bf16[128,256]{1,0:T(8,128)(2,1)S(1)} %get-tuple-element.44.column_hot), custom_call_target="tpu_custom_call" | custom-call | tf_op jit(solution)/shard_map/fill_and_scale/pallas_call | solution.py:544
  (4 shorter events, 0.1 us)
Async XLA Ops:
  1.4 5.2 %collective-permute-start = (f32[24,128]{1,0:T(8,128)S(1)}, f32[24,128]{1,0:T(8,128)S(1)}, u32[]{:S(2)}, u32[]{:S(2)}) collective-permute-start(f32[24,128]{1,0:T(8,128)S(1)} %get-tuple-element.31), channel_id=1, source_target_pairs={{0,1},{1,0},{2,3},{3,2},{4,5},{5,4},{6,7},{7,6},{8,9},{9,8},{10,11... | collective-permute-start | bytes 36872 | tf_op jit(solution)/shard_map/ppermute | solution.py:429
  4.4 4.2 %collective-permute-start.3 = (f32[120,128]{1,0:T(8,128)S(1)}, f32[120,128]{1,0:T(8,128)S(1)}, u32[]{:S(2)}, u32[]{:S(2)}) collective-permute-start(f32[120,128]{1,0:T(8,128)S(1)} %get-tuple-element.33), channel_id=1, source_target_pairs={{0,4},{4,0},{8,12},{12,8},{1,5},{5,1},{9,13},{13,9},{2,6},{6,2},{1... | collective-permute-start | bytes 184328 | tf_op jit(solution)/shard_map/ppermute | solution.py:429
  6.0 6.7 %collective-permute-start.2 = (f32[104,128]{1,0:T(8,128)S(1)}, f32[104,128]{1,0:T(8,128)S(1)}, u32[]{:S(2)}, u32[]{:S(2)}) collective-permute-start(f32[104,128]{1,0:T(8,128)S(1)} %get-tuple-element.32), channel_id=1, source_target_pairs={{4,8},{8,4},{5,9},{9,5},{6,10},{10,6},{7,11},{11,7},{20,24},{24,20... | collective-permute-start | bytes 159752 | tf_op jit(solution)/shard_map/ppermute | solution.py:429
  6.6 5.5 %copy-start = (f32[1,4,8,8,128]{4,3,2,1,0:T(8,128)S(1)}, f32[1,4,8,8,128]{4,3,2,1,0:T(8,128)}, u32[]{:S(2)}) copy-start(f32[1,4,8,8,128]{4,3,2,1,0:T(8,128)} %param.8) | copy-start | bytes 393220
  6.6 6.0 %collective-permute-start.1 = (f32[24,128]{1,0:T(8,128)S(1)}, f32[24,128]{1,0:T(8,128)S(1)}, u32[]{:S(2)}, u32[]{:S(2)}) collective-permute-start(f32[24,128]{1,0:T(8,128)S(1)} %relay_columns.1), channel_id=1, source_target_pairs={{0,2},{1,3},{2,0},{3,1},{4,6},{5,7},{6,4},{7,5},{8,10},{9,11},{10,... | collective-permute-start | bytes 36872 | tf_op jit(solution)/shard_map/ppermute | solution.py:479
  8.6 3.6 %copy-start.3 = (f32[1,8,8,128]{3,2,1,0:T(8,128)S(1)}, f32[1,8,8,128]{3,2,1,0:T(8,128)}, u32[]{:S(2)}) copy-start(f32[1,8,8,128]{3,2,1,0:T(8,128)} %param.9) | copy-start | bytes 98308
  8.6 5.2 %collective-permute-start.5 = (f32[16,128]{1,0:T(8,128)S(1)}, f32[16,128]{1,0:T(8,128)S(1)}, u32[]{:S(2)}, u32[]{:S(2)}) collective-permute-start(f32[16,128]{1,0:T(8,128)S(1)} %forward_masses.1), channel_id=1, source_target_pairs={{0,8},{4,12},{8,0},{12,4},{1,9},{5,13},{9,1},{13,5},{2,10},{6,14},... | collective-permute-start | bytes 24584 | tf_op jit(solution)/shard_map/ppermute | solution.py:488
  12.2 0.8 %copy-start.1 = (f32[1,8,8,128]{3,2,1,0:T(8,128)S(1)}, f32[1,8,8,128]{3,2,1,0:T(8,128)}, u32[]{:S(2)}) copy-start(f32[1,8,8,128]{3,2,1,0:T(8,128)} %param.10) | copy-start | bytes 98308
  12.9 0.8 %copy-start.2 = (f32[1,8,8,128]{3,2,1,0:T(8,128)S(1)}, f32[1,8,8,128]{3,2,1,0:T(8,128)}, u32[]{:S(2)}) copy-start(f32[1,8,8,128]{3,2,1,0:T(8,128)} %param.11) | copy-start | bytes 98308
  13.5 1.2 %collective-permute-start.4 = (f32[64,128]{1,0:T(8,128)S(1)}, f32[64,128]{1,0:T(8,128)S(1)}, u32[]{:S(2)}, u32[]{:S(2)}) collective-permute-start(f32[64,128]{1,0:T(8,128)S(1)} %get-tuple-element.40.own), channel_id=1, source_target_pairs={{0,16},{16,0},{1,17},{17,1},{2,18},{18,2},{3,19},{19,3},{4,20},{20... | collective-permute-start | bytes 98312 | tf_op jit(solution)/shard_map/ppermute | solution.py:529

commit v14 on v13

--- a/solution.py
+++ b/solution.py
@@ -121,12 +121,13 @@
 
 def pack_kernel(
     sizes, field, zonal, meridional, mass, target, live, donor, fraction,
-    columns, sides, lat_even, lat_odd, masses, *index_copies,
+    columns, sides, lat_even, lat_odd, masses, *near_copies,
 ):
     _, levels, rows, width, blocks, capacity, _ = sizes
     fields = sizes.fields
     here = lax.axis_index("lat")
-    for copy, source in zip(index_copies, (donor, fraction, target, live), strict=True):
+    sources = (donor, fraction, target, live, field, zonal, meridional, mass)
+    for copy, source in zip(near_copies, sources, strict=True):
         copy[...] = source[...]
     even = lax.rem(here, 2) == 0
     for i in range(HALO):
@@ -451,7 +452,7 @@
         return (pltpu.with_memory_space_constraint(value, pltpu.VMEM) for value in values)
 
     slots = blocks * capacity
-    columns, sides, lat_even, lat_odd, masses, *index_copies = pl.pallas_call(
+    columns, sides, lat_even, lat_odd, masses, *near_copies = pl.pallas_call(
         functools.partial(pack_kernel, sizes),
         out_shape=(
             shape(max(COLUMN_ROWS, 8 * sizes.chunks), width),
@@ -463,9 +464,14 @@
             pltpu.VMEM(fraction.shape, fraction.dtype),
             pltpu.VMEM(target.shape, target.dtype),
             pltpu.VMEM(live.shape, live.dtype),
+            shape(*field.shape),
+            shape(*zonal.shape),
+            shape(*meridional.shape),
+            shape(*mass.shape),
         ),
         name="pack_edges",
     )(field, zonal, meridional, mass, target, live, donor, fraction)
+    *index_copies, field, zonal, meridional, mass = near_copies
     lat_even = exchanged(lat_even, "lat", 0)
     lat_odd = exchanged(lat_odd, "lat", 1)
     even_pairs = exchanged(columns, "lon", 0)

time: 27.3 us -> 27.1 us (level)
  local copies, waits for them, and re-layouts: 0.36 us -> 0 us
  blocking collectives: 11.2 us -> 11.5 us
    unnamed x8 -> x0, local copies, waits for them, and re-layouts: 0.36 us -> none
    ppermute x1, waiting for transfers between devices: 0.06 us -> 0.4 us  [body(): lax.ppermute(forwarded, 'lat', [(i, i ^ 2) for i in range(blocks)])]
    all_to_all x1, blocking collectives: 11.2 us -> 11.5 us  [body(): lax.all_to_all(all_blocks.reshape(devices, 1, block_rows * width), ('pane...]
where the time goes in v14:
time: 27.1 us; the launch traced here: 27 us
  blocking collectives  11.5 us (42%)
  starting transfers between devices  10.3 us (38%)
  Pallas kernels  3.57 us (13%)
  waiting for transfers between devices  1.53 us (6%)
    all_to_all x1, blocking collectives, body(): lax.all_to_all(all_blocks.reshape(devices, 1, block_rows * width), ('pane...  11.5 us
    ppermute x3, starting transfers between devices, exchanged(): return lax.ppermute(value, axis, pairs)  5.23 us
    ppermute x1, starting transfers between devices, body(): lax.ppermute(forwarded, 'lat', [(i, i ^ 2) for i in range(blocks)])  3.47 us
    ppermute x1, starting transfers between devices, body(): lax.ppermute(relayed, 'lon', [(i, i ^ 2) for i in range(places)])  1.58 us
    pallas_call x1, Pallas kernels, body(): pl.pallas_call(functools.partial(pack_kernel, sizes), out_shape=(shape(ma...  1.34 us
    pallas_call x1, Pallas kernels, body(): pl.pallas_call(functools.partial(fill_kernel, sizes), out_shape=jax.Shape...  0.97 us
    ppermute x1, waiting for transfers between devices, body(): given = lax.ppermute(outgoing, 'panel', [(0, 1), (1, 0)])  0.74 us
    pallas_call x1, Pallas kernels, body(): pl.pallas_call(functools.partial(main_kernel, sizes), out_shape=(shape(fi...  0.61 us
  transfers between devices with their start and end apart: 6, of which 3 were waited for; matrix products, arithmetic and copies ran while one was open for 0% of the time, Pallas kernels for 4%

profile of v14, /device:TPU:0, one launch (start us, length us, event | category | flops | bytes accessed | tf_op | source)
XLA Modules:
  0.0 27.0 jit_solution(11997185265310938406)
XLA Ops:
  0.0 1.3 %pack_edges.1 = (f32[24,128]{1,0:T(8,128)S(1)}, f32[12,320]{1,0:T(8,128)S(1)}, f32[120,128]{1,0:T(8,128)S(1)}, f32[104,128]{1,0:T(8,128)S(1)}, f32[32,128]{1,0:T...) custom-call(f32[256,128]{1,0:T(8,128)} %bitcast.12, ...), custom_call_target="tpu_custom_call" | custom-call | tf_op jit(solution)/shard_map/pack_edges/pallas_call | solution.py:455
  1.3 3.0 %collective-permute-start = (f32[24,128]{1,0:T(8,128)S(1)}, f32[24,128]{1,0:T(8,128)S(1)}, u32[]{:S(2)}, u32[]{:S(2)}) collective-permute-start(f32[24,128]{1,0:T(8,128)S(1)} %get-tuple-element.39), channel_id=1, source_target_pairs={{0,1},{1,0},{2,3},{3,2},{4,5},{5,4},{6,7},{7,6},{8,9},{9,8},{10,11... | collective-permute-start | bytes 36872 | tf_op jit(solution)/shard_map/ppermute | solution.py:430
  4.3 1.6 %collective-permute-start.3 = (f32[120,128]{1,0:T(8,128)S(1)}, f32[120,128]{1,0:T(8,128)S(1)}, u32[]{:S(2)}, u32[]{:S(2)}) collective-permute-start(f32[120,128]{1,0:T(8,128)S(1)} %get-tuple-element.41), channel_id=1, source_target_pairs={{0,4},{4,0},{8,12},{12,8},{1,5},{5,1},{9,13},{13,9},{2,6},{6,2},{1... | collective-permute-start | bytes 184328 | tf_op jit(solution)/shard_map/ppermute | solution.py:430
  5.9 0.7 %collective-permute-start.2 = (f32[104,128]{1,0:T(8,128)S(1)}, f32[104,128]{1,0:T(8,128)S(1)}, u32[]{:S(2)}, u32[]{:S(2)}) collective-permute-start(f32[104,128]{1,0:T(8,128)S(1)} %get-tuple-element.40), channel_id=1, source_target_pairs={{4,8},{8,4},{5,9},{9,5},{6,10},{10,6},{7,11},{11,7},{20,24},{24,20... | collective-permute-start | bytes 159752 | tf_op jit(solution)/shard_map/ppermute | solution.py:430
  6.6 0.0 collective-permute-done.columns.even_pairs
  6.6 1.6 %collective-permute-start.1 = (f32[24,128]{1,0:T(8,128)S(1)}, f32[24,128]{1,0:T(8,128)S(1)}, u32[]{:S(2)}, u32[]{:S(2)}) collective-permute-start(f32[24,128]{1,0:T(8,128)S(1)} %relay_columns.1), channel_id=1, source_target_pairs={{0,2},{1,3},{2,0},{3,1},{4,6},{5,7},{6,4},{7,5},{8,10},{9,11},{10,... | collective-permute-start | bytes 36872 | tf_op jit(solution)/shard_map/ppermute | solution.py:485
  8.2 0.4 %collective-permute-done.3.lat_even = f32[120,128]{1,0:T(8,128)S(1)} collective-permute-done((f32[120,128]{1,0:T(8,128)S(1)}, f32[120,128]{1,0:T(8,128)S(1)}, u32[]{:S(2)}, u32[]{:S(2)}) %collective-permute-start.3) | collective-permute-done | bytes 61472 | tf_op jit(solution)/shard_map/ppermute | solution.py:430
  8.6 3.5 %collective-permute-start.5 = (f32[16,128]{1,0:T(8,128)S(1)}, f32[16,128]{1,0:T(8,128)S(1)}, u32[]{:S(2)}, u32[]{:S(2)}) collective-permute-start(f32[16,128]{1,0:T(8,128)S(1)} %forward_masses.1), channel_id=1, source_target_pairs={{0,8},{4,12},{8,0},{12,4},{1,9},{5,13},{9,1},{13,5},{2,10},{6,14},... | collective-permute-start | bytes 24584 | tf_op jit(solution)/shard_map/ppermute | solution.py:494
  12.0 0.5 %zonal_and_tables.1 = (f32[256,128]{1,0:T(8,128)S(1)}, f32[8,128]{1,0:T(8,128)S(1)}, f32[8,256]{1,0:T(8,128)S(1)}, bf16[128,256]{1,0:T(8,128)(2,1)S(1)}, f32[8,2...) custom-call(f32[256,128]{1,0:T(8,128)S(1)} %get-tuple-element.29.field, ...), custom_call_target="tpu_custom_call" | custom-call | tf_op jit(solution)/shard_map/zonal_and_tables/pallas_call | solution.py:505
  12.5 0.0 collective-permute-done.1.odd_pairs
  12.6 0.0 collective-permute-done.2.lat_odd
  12.6 0.6 %advect_and_interpolate.1 = (f32[256,128]{1,0:T(8,128)S(1)}, f32[64,128]{1,0:T(8,128)S(1)}) custom-call(f32[256,128]{1,0:T(8,128)S(1)} %get-tuple-element.29.field, f32[256,128]{1,0:T(8,128)S(1)} %get-tuple-element.36.moved, f32[64,128]{1,0:T(8,128)S(1)} %get-tuple-element.37.meridional, f32[12,320]{1,0:T(8,128)S(1)} %get-tuple-element.38.sides, ...), custom_call_target="tpu_custom_call" | custom-call | tf_op jit(solution)/shard_map/advect_and_interpolate/pallas_call | solution.py:518
  13.2 0.0 collective-permute-start.4
  13.3 0.4 %collective-permute-done.5.forwarded = f32[16,128]{1,0:T(8,128)S(1)} collective-permute-done((f32[16,128]{1,0:T(8,128)S(1)}, f32[16,128]{1,0:T(8,128)S(1)}, u32[]{:S(2)}, u32[]{:S(2)}) %collective-permute-start.5) | collective-permute-done | bytes 8224 | tf_op jit(solution)/shard_map/ppermute | solution.py:494
  13.7 0.7 %collective-permute-done.4.given = f32[64,128]{1,0:T(8,128)S(1)} collective-permute-done((f32[64,128]{1,0:T(8,128)S(1)}, f32[64,128]{1,0:T(8,128)S(1)}, u32[]{:S(2)}, u32[]{:S(2)}) %collective-permute-start.4) | collective-permute-done | bytes 32800 | tf_op jit(solution)/shard_map/ppermute | solution.py:535
  14.4 0.1 margin_blocks.1
  14.5 11.5 %all_to_all.5 = f32[32,1,1152]{2,1,0:T(1,128)S(1)} all-to-all(f32[32,1,1152]{2,1,0:T(1,128)S(1)} %bitcast.10), channel_id=1, replica_groups=mesh['panel'=2,'lat'=4,'lon'=4] {'panel','lon','lat'}, dimensions={0} | all-to-all | bytes 294912 | tf_op jit(solution)/shard_map/all_to_all | solution.py:547
  26.0 1.0 %fill_and_scale.1 = f32[1,4,8,8,128]{4,3,2,1,0:T(8,128)} custom-call(f32[256,128]{1,0:T(8,128)S(1)} %get-tuple-element.47.advected, f32[288,128]{1,0:T(8,128)S(1)} %bitcast.11, f32[8,256]{1,0:T(8,128)S(1)} %get-tuple-element.51.row_hit, bf16[128,256]{1,0:T(8,128)(2,1)S(1)} %get-tuple-element.52.column_hot), custom_call_target="tpu_custom_call" | custom-call | tf_op jit(solution)/shard_map/fill_and_scale/pallas_call | solution.py:550
  (4 shorter events, 0.1 us)
Async XLA Ops:
  1.3 5.2 %collective-permute-start = (f32[24,128]{1,0:T(8,128)S(1)}, f32[24,128]{1,0:T(8,128)S(1)}, u32[]{:S(2)}, u32[]{:S(2)}) collective-permute-start(f32[24,128]{1,0:T(8,128)S(1)} %get-tuple-element.39), channel_id=1, source_target_pairs={{0,1},{1,0},{2,3},{3,2},{4,5},{5,4},{6,7},{7,6},{8,9},{9,8},{10,11... | collective-permute-start | bytes 36872 | tf_op jit(solution)/shard_map/ppermute | solution.py:430
  4.3 4.2 %collective-permute-start.3 = (f32[120,128]{1,0:T(8,128)S(1)}, f32[120,128]{1,0:T(8,128)S(1)}, u32[]{:S(2)}, u32[]{:S(2)}) collective-permute-start(f32[120,128]{1,0:T(8,128)S(1)} %get-tuple-element.41), channel_id=1, source_target_pairs={{0,4},{4,0},{8,12},{12,8},{1,5},{5,1},{9,13},{13,9},{2,6},{6,2},{1... | collective-permute-start | bytes 184328 | tf_op jit(solution)/shard_map/ppermute | solution.py:430
  5.9 6.6 %collective-permute-start.2 = (f32[104,128]{1,0:T(8,128)S(1)}, f32[104,128]{1,0:T(8,128)S(1)}, u32[]{:S(2)}, u32[]{:S(2)}) collective-permute-start(f32[104,128]{1,0:T(8,128)S(1)} %get-tuple-element.40), channel_id=1, source_target_pairs={{4,8},{8,4},{5,9},{9,5},{6,10},{10,6},{7,11},{11,7},{20,24},{24,20... | collective-permute-start | bytes 159752 | tf_op jit(solution)/shard_map/ppermute | solution.py:430
  6.6 5.9 %collective-permute-start.1 = (f32[24,128]{1,0:T(8,128)S(1)}, f32[24,128]{1,0:T(8,128)S(1)}, u32[]{:S(2)}, u32[]{:S(2)}) collective-permute-start(f32[24,128]{1,0:T(8,128)S(1)} %relay_columns.1), channel_id=1, source_target_pairs={{0,2},{1,3},{2,0},{3,1},{4,6},{5,7},{6,4},{7,5},{8,10},{9,11},{10,... | collective-permute-start | bytes 36872 | tf_op jit(solution)/shard_map/ppermute | solution.py:485
  8.6 5.1 %collective-permute-start.5 = (f32[16,128]{1,0:T(8,128)S(1)}, f32[16,128]{1,0:T(8,128)S(1)}, u32[]{:S(2)}, u32[]{:S(2)}) collective-permute-start(f32[16,128]{1,0:T(8,128)S(1)} %forward_masses.1), channel_id=1, source_target_pairs={{0,8},{4,12},{8,0},{12,4},{1,9},{5,13},{9,1},{13,5},{2,10},{6,14},... | collective-permute-start | bytes 24584 | tf_op jit(solution)/shard_map/ppermute | solution.py:494
  13.2 1.2 %collective-permute-start.4 = (f32[64,128]{1,0:T(8,128)S(1)}, f32[64,128]{1,0:T(8,128)S(1)}, u32[]{:S(2)}, u32[]{:S(2)}) collective-permute-start(f32[64,128]{1,0:T(8,128)S(1)} %get-tuple-element.48.own), channel_id=1, source_target_pairs={{0,16},{16,0},{1,17},{17,1},{2,18},{18,2},{3,19},{19,3},{4,20},{20... | collective-permute-start | bytes 98312 | tf_op jit(solution)/shard_map/ppermute | solution.py:535
